TPU v7x, 128 devices: a whole 4x4x4 slice. The times are simulated.
128 devices in a mesh: rep: 16 (over y_lo, x, core), dp: 8 (over y_hi, z).
Axes of the slice: x: 4, y: 4 (y_hi: 2, y_lo: 2; y = y_hi * 2 + y_lo), z: 4, core: 2. Of those that a mesh axis runs over, the one named last changes fastest.
Arguments:
- queries: bfloat16 [2048, 64, 576], P(('rep', 'dp')), parts along dimension 0, may hold values from -50 to 50
- latent_cache: bfloat16 [2048, 512, 576], P(('rep', 'dp')), parts along dimension 0, may hold values from -8 to 8
- new_latent: bfloat16 [2048, 576], P(('rep', 'dp')), parts along dimension 0, may hold values from -6 to 6
- lengths: int32 [2048], P('rep'), parts along dimension 0, may hold values from 2 to 512, as said below
- value_up: bfloat16 [64, 512, 128], P('dp'), may hold values from -0.75 to 0.75
- output_proj: bfloat16 [8192, 7168], P('dp'), may hold values from -0.0625 to 0.0625
- residual: bfloat16 [2048, 7168], P(('rep', 'dp')), parts along dimension 0, may hold values from -3 to 3
- norm_gain: bfloat16 [7168], replicated, may hold values from 0.5 to 1.5
Outputs:
- hidden_next: bfloat16 [2048, 7168], P(('rep', 'dp')), parts along dimension 0
- normed: bfloat16 [2048, 7168], P(('rep', 'dp')), parts along dimension 0
There are 16 independent parts, one for each index of `rep`. A program takes and returns all parts, laid end to end along the dimension named above; an argument that names none is the same for every part. Nothing has to cross between parts.
Inputs may be any that keep to these rules, and one draw needn't show every extreme that they name: The rows of one device share a ceiling of 128, 256 or 512 on their lengths; one device of each part has the ceiling 512 and a row of exactly 512.
All inputs are finite; a program needn't handle non-finite values.
Results may differ from a plain program's by a relative error of at most 0.017.
Values may be sent and summed in bfloat16 or wider, within the bound.
No kernel may reach another device: no remote copies, remote signals or barrier semaphores. Data moves between devices by JAX's collectives and lax.ppermute only.
A program may use at most 128 MiB of HBM per device.

v0:
```python
import jax
import jax.numpy as jnp
from jax import lax
from jax.experimental import pallas as pl
from jax.experimental.pallas import tpu as pltpu
from jax.sharding import PartitionSpec as P

LAT = 512
GROUP_PAIRS = 2
PROJ_STEP = 1024
LEFT_COLUMNS = 3072
score_scale = 192.0 ** (-0.5)
norm_eps = 1e-06
MIB = 1024 * 1024


def attend_kernel(
    lengths_hbm, queries_hbm, latent_hbm, cache_ref, proj_hbm, out_ref, proj_ref,
    held, queries_ref, latent_ref, latent_wide, lengths_ref, order, arrived, arrived_small,
):
    row_count, width, span = held.shape
    owners, _, _ = out_ref.shape
    heads = queries_ref.shape[1]
    owned = heads // owners
    first_row = lax.axis_index("dp") * row_count
    pair_count = row_count // 2
    group_count = pair_count // GROUP_PAIRS
    short = span // 2

    lengths_copy = pltpu.make_async_copy(lengths_hbm, lengths_ref, arrived_small.at[0])
    latent_copy = pltpu.make_async_copy(latent_hbm, latent_ref, arrived_small.at[1])
    proj_copy = pltpu.make_async_copy(proj_hbm, proj_ref, arrived_small.at[2])

    def fetch_queries(pair):
        rows = pl.ds(2 * pair, 2)
        return pltpu.make_async_copy(queries_hbm.at[rows], queries_ref.at[rows], arrived.at[0, pair])

    def fetch_half(pair, half):
        rows, keys = pl.ds(2 * pair, 2), pl.ds(half * short, short)
        return pltpu.make_async_copy(
            cache_ref.at[rows, :, keys], held.at[rows, :, keys], arrived.at[1 + half, pair]
        )

    lengths_copy.start()
    latent_copy.start()
    for pair in range(pair_count):
        fetch_queries(pair).start()
        fetch_half(pair, 0).start()

    lengths_copy.wait()
    longest = [
        jnp.maximum(lengths_ref[first_row + 2 * pair], lengths_ref[first_row + 2 * pair + 1])
        for pair in range(pair_count)
    ]
    is_long = [(length > short).astype(jnp.int32) for length in longest]
    long_slot, short_slot = pair_count - sum(is_long), 0
    short_groups = long_slot // GROUP_PAIRS
    for pair in range(pair_count):
        order[jnp.where(is_long[pair] == 1, long_slot, short_slot)] = pair
        long_slot = long_slot + is_long[pair]
        short_slot = short_slot + 1 - is_long[pair]

    def start_second(slot, carry):
        fetch_half(order[slot], 1).start()
        return carry

    lax.fori_loop(short_groups * GROUP_PAIRS, pair_count, start_second, 0)
    proj_copy.start()
    latent_copy.wait()
    latent_wide[...] = latent_ref[...].astype(jnp.float32)

    def score(row, keys):
        queries = queries_ref[row]
        fresh = latent_wide[pl.ds(row, 1), :]
        scores = (
            jnp.dot(queries, held[row, :, :keys], preferred_element_type=jnp.float32)
            * score_scale
        )
        self_score = (
            jnp.sum(queries.astype(jnp.float32) * fresh, axis=1, keepdims=True) * score_scale
        )
        return scores, self_score

    def weigh(row, scores, self_score):
        position = lax.broadcasted_iota(jnp.int32, scores.shape, 1)
        scores = jnp.where(position < lengths_ref[first_row + row], scores, -jnp.inf)
        row_max = jnp.maximum(jnp.max(scores, axis=1, keepdims=True), self_score)
        raised = jnp.exp(scores - row_max)
        self_raised = jnp.exp(self_score - row_max)
        row_total = jnp.sum(raised, axis=1, keepdims=True) + self_raised
        self_weight = self_raised.astype(jnp.bfloat16).astype(jnp.float32)
        return raised.astype(jnp.bfloat16), self_weight, row_total

    def gather(row, keys, weights, self_weight, row_total):
        gathered = lax.dot_general(
            weights,
            held[row, :LAT, :keys],
            (((1,), (1,)), ((), ())),
            preferred_element_type=jnp.float32,
        )
        gathered = gathered + self_weight * latent_wide[pl.ds(row, 1), :LAT]
        return (gathered / row_total).reshape(owners, owned, LAT)

    def attend_group(keys):
        def body(group, carry):
            pairs = [order[group * GROUP_PAIRS + i] for i in range(GROUP_PAIRS)]
            for pair in pairs:
                fetch_queries(pair).wait()
                for half in range(keys // short):
                    fetch_half(pair, half).wait()
            rows = [2 * pair + i for pair in pairs for i in range(2)]
            scored = [score(row, keys) for row in rows]
            weighed = [weigh(row, *both) for row, both in zip(rows, scored)]
            done = [gather(row, keys, *parts) for row, parts in zip(rows, weighed)]
            for i, pair in enumerate(pairs):
                block = jnp.concatenate(done[2 * i : 2 * i + 2], axis=1).astype(jnp.bfloat16)
                size = 2 * owned
                out_ref[:, pl.ds(pl.multiple_of(pair * size, size), size), :] = block
            return carry

        return body

    lax.fori_loop(0, short_groups, attend_group(short), 0)
    lax.fori_loop(short_groups, group_count, attend_group(span), 0)
    proj_copy.wait()


def attend(queries, latent_cache, new_latent, lengths, output_proj, owners):
    row_count, span, width = latent_cache.shape
    heads = queries.shape[1]
    owned = heads // owners
    vmem = pl.BlockSpec(memory_space=pltpu.VMEM)
    hbm = pl.BlockSpec(memory_space=pltpu.HBM)
    return pl.pallas_call(
        attend_kernel,
        out_shape=(
            jax.ShapeDtypeStruct((owners, row_count * owned, LAT), jnp.bfloat16),
            pltpu.VMEM(output_proj.shape, jnp.bfloat16),
        ),
        in_specs=[
            hbm,
            hbm,
            hbm,
            hbm,
            hbm,
        ],
        out_specs=(vmem, vmem),
        scratch_shapes=[
            pltpu.VMEM((row_count, width, span), jnp.bfloat16),
            pltpu.VMEM(queries.shape, jnp.bfloat16),
            pltpu.VMEM(new_latent.shape, jnp.bfloat16),
            pltpu.VMEM((row_count, width), jnp.float32),
            pltpu.SMEM(lengths.shape, jnp.int32),
            pltpu.SMEM((row_count // 2,), jnp.int32),
            pltpu.SemaphoreType.DMA((3, row_count // 2)),
            pltpu.SemaphoreType.DMA((3,)),
        ],
        cost_estimate=pl.CostEstimate(
            flops=4 * row_count * heads * span * width,
            bytes_accessed=2 * row_count * span * width,
            transcendentals=row_count * heads * span,
        ),
        compiler_params=pltpu.CompilerParams(vmem_limit_bytes=24 * MIB),
        name="attend",
    )(
        *(
            pltpu.with_memory_space_constraint(x, pltpu.HBM)
            for x in (lengths, queries, new_latent, jnp.swapaxes(latent_cache, 1, 2), output_proj)
        ),
    )


def values_kernel(latent_ref, value_up_ref, proj_ref, values_ref, own_ref, send_ref, wide):
    owned, lat, value_size = value_up_ref.shape
    owners, rows_here, columns = 2 * own_ref.shape[0], own_ref.shape[1], own_ref.shape[2]
    rows = owners * rows_here
    z_size = owners // 2
    here = lax.axis_index("dp")

    for c in range(lat // 128):
        wide[c] = latent_ref[:, c * 128 : (c + 1) * 128].astype(jnp.float32)
    for h in range(owned):
        mine = jnp.concatenate(
            [wide[c, pl.ds(h, rows, stride=owned), :] for c in range(lat // 128)], axis=1
        ).astype(jnp.bfloat16)
        made = jnp.dot(mine, value_up_ref[h], preferred_element_type=jnp.float32).astype(
            jnp.bfloat16
        )
        for owner in range(owners):
            far = (owner // z_size + here // z_size) % 2
            step = (owner % z_size - here % z_size + z_size) % z_size
            place = pl.multiple_of((far * z_size + step) * rows_here, rows_here)
            values_ref[pl.ds(place, rows_here), h * value_size : (h + 1) * value_size] = made[
                owner * rows_here : (owner + 1) * rows_here
            ]
    flattened = values_ref[...]
    width = proj_ref.shape[1]
    for start in range(0, columns, PROJ_STEP):
        stop = min(start + PROJ_STEP, columns)
        done = jnp.dot(
            flattened,
            proj_ref[:, width - columns + start : width - columns + stop],
            preferred_element_type=jnp.float32,
        ).astype(jnp.bfloat16)
        done = done.reshape(2, z_size, rows_here, stop - start)
        own_ref[:, :, start:stop] = done[0]
        send_ref[:, :, start:stop] = done[1]


def make_values(owned_latent, value_up, output_proj, owners, rows_here, columns):
    owned, lat, value_size = value_up.shape
    depth, width = output_proj.shape
    rows = owners * rows_here
    vmem = pl.BlockSpec(memory_space=pltpu.VMEM)
    half = jax.ShapeDtypeStruct((owners // 2, rows_here, columns), jnp.bfloat16)
    return pl.pallas_call(
        values_kernel,
        out_shape=(jax.ShapeDtypeStruct((rows, owned * value_size), jnp.bfloat16), half, half),
        in_specs=[vmem, vmem, vmem],
        out_specs=(vmem, vmem, vmem),
        scratch_shapes=[pltpu.VMEM((lat // 128, rows * owned, 128), jnp.float32)],
        cost_estimate=pl.CostEstimate(
            flops=2 * rows * depth * columns, bytes_accessed=2 * depth * columns, transcendentals=0
        ),
        compiler_params=pltpu.CompilerParams(vmem_limit_bytes=20 * MIB),
        name="values",
    )(owned_latent, value_up, pltpu.with_memory_space_constraint(output_proj, pltpu.VMEM))


def project_kernel(values_ref, proj_ref, *out_refs):
    rows_here, columns = out_refs[0].shape[1:]
    z_size = len(out_refs)
    flattened = values_ref[...]
    for start in range(0, columns, PROJ_STEP):
        stop = min(start + PROJ_STEP, columns)
        done = jnp.dot(
            flattened, proj_ref[:, start:stop], preferred_element_type=jnp.float32
        ).astype(jnp.bfloat16)
        done = done.reshape(2, z_size, rows_here, stop - start)
        for step in range(z_size):
            out_refs[step][:, :, start:stop] = done[:, step]


def project(values, output_proj, owners, rows_here, columns):
    rows, depth = values.shape
    z_size = owners // 2
    vmem = pl.BlockSpec(memory_space=pltpu.VMEM)
    part = jax.ShapeDtypeStruct((2, rows_here, columns), jnp.bfloat16)
    return pl.pallas_call(
        project_kernel,
        out_shape=[part] * z_size,
        in_specs=[vmem, vmem],
        out_specs=[vmem] * z_size,
        cost_estimate=pl.CostEstimate(
            flops=2 * rows * depth * columns, bytes_accessed=2 * depth * columns, transcendentals=0
        ),
        compiler_params=pltpu.CompilerParams(vmem_limit_bytes=20 * MIB),
        name="project",
    )(values, pltpu.with_memory_space_constraint(output_proj, pltpu.VMEM))


def add_far_kernel(own_ref, came_ref, *out_refs):
    for step, out_ref in enumerate(out_refs, 1):
        both = own_ref[step].astype(jnp.float32) + came_ref[step].astype(jnp.float32)
        out_ref[...] = both.astype(jnp.bfloat16)


def add_far(own, came):
    vmem = pl.BlockSpec(memory_space=pltpu.VMEM)
    return pl.pallas_call(
        add_far_kernel,
        out_shape=[jax.ShapeDtypeStruct(own.shape[1:], jnp.bfloat16)] * (own.shape[0] - 1),
        in_specs=[vmem, vmem],
        out_specs=[vmem] * (own.shape[0] - 1),
        cost_estimate=pl.CostEstimate(flops=own.size, bytes_accessed=own.size * 6, transcendentals=0),
        compiler_params=pltpu.CompilerParams(vmem_limit_bytes=16 * MIB),
        name="add_far",
    )(own, came)


def add_near_kernel(*refs):
    *part_refs, out_ref = refs
    total = part_refs[0][1].astype(jnp.float32)
    for part_ref in part_refs[1:]:
        total = total + part_ref[1].astype(jnp.float32)
    out_ref[...] = total.astype(jnp.bfloat16)


def add_near(parts):
    vmem = pl.BlockSpec(memory_space=pltpu.VMEM)
    return pl.pallas_call(
        add_near_kernel,
        out_shape=jax.ShapeDtypeStruct(parts[0].shape[1:], jnp.bfloat16),
        in_specs=[vmem] * len(parts),
        out_specs=vmem,
        cost_estimate=pl.CostEstimate(
            flops=parts[0].size * 2, bytes_accessed=parts[0].size * 8, transcendentals=0
        ),
        compiler_params=pltpu.CompilerParams(vmem_limit_bytes=16 * MIB),
        name="add_near",
    )(*parts)


def finish_kernel(near_refs, far_ref, own_ref, came_ref, step_refs, residual_ref, gain_ref,
                  hidden_ref, normed_ref):
    rows, first = far_ref.shape
    width = residual_ref.shape[1]
    left = residual_ref[:, :first].astype(jnp.float32) + far_ref[...].astype(jnp.float32)
    for near_ref in near_refs:
        left = left + near_ref[0].astype(jnp.float32)
    right = residual_ref[:, first:].astype(jnp.float32) + (
        own_ref[0].astype(jnp.float32) + came_ref[0].astype(jnp.float32)
    )
    for step_ref in step_refs:
        right = right + step_ref[...].astype(jnp.float32)
    total = jnp.sum(left * left, axis=1, keepdims=True) + jnp.sum(
        right * right, axis=1, keepdims=True
    )
    inverse_rms = lax.rsqrt(total * (1.0 / width) + norm_eps)
    for part, here in ((left, slice(0, first)), (right, slice(first, width))):
        hidden_ref[:, here] = part.astype(jnp.bfloat16)
        normed = part * inverse_rms * gain_ref[:, here].astype(jnp.float32)
        normed_ref[:, here] = normed.astype(jnp.bfloat16)


def finish(nears, far, own, came, steps, residual, norm_gain):
    vmem = pl.BlockSpec(memory_space=pltpu.VMEM)
    shape = jax.ShapeDtypeStruct(residual.shape, jnp.bfloat16)
    return pl.pallas_call(
        finish_kernel,
        out_shape=(shape, shape),
        in_specs=[[vmem] * len(nears), vmem, vmem, vmem, [vmem] * len(steps), vmem, vmem],
        out_specs=(vmem, vmem),
        compiler_params=pltpu.CompilerParams(vmem_limit_bytes=32 * MIB),
        name="finish",
    )(nears, far, own, came, steps, residual, norm_gain.reshape(1, -1))


def exchange(blocks, mesh_shape):
    replicas, owners = mesh_shape
    half_rep, half_dp = replicas // 2, owners // 2
    groups = []
    for side in range(2):
        for rest in range(half_rep):
            groups.append(
                [
                    (((side + owner // half_dp) % 2) * half_rep + rest) * owners + owner
                    for owner in range(owners)
                ]
            )
    return lax.all_to_all(
        blocks,
        ("rep", "dp"),
        split_axis=0,
        concat_axis=0,
        axis_index_groups=groups,
        tiled=True,
    )


def step_along(array, step, owners):
    z_size = owners // 2
    pairs = [
        (owner, owner // z_size * z_size + (owner + step) % z_size) for owner in range(owners)
    ]
    return lax.ppermute(array, "dp", pairs)


def step_across(array, mesh_shape):
    replicas, owners = mesh_shape
    pairs = [
        (
            replica * owners + owner,
            (replica + replicas // 2) % replicas * owners + (owner + owners // 2) % owners,
        )
        for replica in range(replicas)
        for owner in range(owners)
    ]
    return lax.ppermute(array, ("rep", "dp"), pairs)


def per_device(
    queries, latent_cache, new_latent, lengths, value_up, output_proj, residual, norm_gain
):
    owners = lax.axis_size("dp")
    mesh_shape = (lax.axis_size("rep"), owners)
    rows_here = latent_cache.shape[0]
    owned = value_up.shape[0]
    width = output_proj.shape[1]
    first = LEFT_COLUMNS
    latent_out, proj_near = attend(
        queries, latent_cache, new_latent, lengths, output_proj, owners
    )
    owned_latent = exchange(latent_out, mesh_shape).reshape(owners * rows_here * owned, LAT)
    values, own, send = make_values(
        owned_latent, value_up, proj_near, owners, rows_here, width - first
    )
    came = step_across(send, mesh_shape)
    parts = project(values, proj_near, owners, rows_here, first)
    nears = [parts[0]] + [step_along(parts[k], k, owners) for k in range(1, len(parts))]
    pairs = add_far(own, came)
    steps = [step_along(pair, k, owners) for k, pair in enumerate(pairs, 1)]
    far = step_across(add_near(nears), mesh_shape)
    return finish(nears, far, own, came, steps, residual, norm_gain)


def solution(mesh):
    return jax.shard_map(
        per_device,
        mesh=mesh,
        in_specs=(
            P(("rep", "dp"), None, None),
            P(("rep", "dp"), None, None),
            P(("rep", "dp"), None),
            P("rep"),
            P("dp", None, None),
            P("dp", None),
            P(("rep", "dp"), None),
            P(),
        ),
        out_specs=(P(("rep", "dp"), None), P(("rep", "dp"), None)),
        check_vma=False,
    )
```

profile of v0, /device:TPU:4, one launch (start us, length us, event | category | flops | bytes accessed | tf_op | source)
XLA Modules:
  0.0 61.0 jit_solution(16715953082853831699)
XLA Ops:
  0.6 0.0 copy-start
  0.6 7.6 %attend.1 = (bf16[8,128,512]{2,1,0:T(8,128)(2,1)S(1)}, bf16[1024,7168]{1,0:T(8,128)(2,1)S(1)}) custom-call(s32[128]{0:T(128)} %lengths_hbm.1, bf16[16,64,576]{2,1,0:T(8,128)(2,1)} %queries_hbm.1, bf16[16,576]{1,0:T(8,128)(2,1)} %latent_hbm.1, bf16[16,576,512]{2,1,0:T(8,128)(2,1)} %bitcast.3, bf16[1024,7168]{1,0:T(8,128)(2,1)} %proj_hbm.1), custom_call_target="tpu_custom_call" | custom-call | flops 1207959552 | bytes 9437184 | tf_op jit(solution)/shard_map/attend/pallas_call | solution.py:134
  8.2 25.0 %all_to_all.5 = bf16[8,128,512]{2,1,0:T(8,128)(2,1)S(1)} all-to-all(bf16[8,128,512]{2,1,0:T(8,128)(2,1)S(1)} %get-tuple-element.14), channel_id=1, replica_groups={{0,1,2,3,68,69,70,71},{8,9,10,11,76,77,78,79},{16,17,18,19,84,85,86,87}..., dimensions={0} | all-to-all | bytes 2097152 | tf_op jit(solution)/shard_map/all_to_all | solution.py:351
  33.2 0.0 copy-done
  33.2 0.0 copy-start.2
  33.2 0.0 copy-start.1
  33.2 2.0 %values.1 = (bf16[128,1024]{1,0:T(8,128)(2,1)S(1)}, bf16[4,16,4096]{2,1,0:T(8,128)(2,1)S(1)}, bf16[4,16,4096]{2,1,0:T(8,128)(2,1)S(1)}) custom-call(bf16[1024,512]{1,0:T(8,128)(2,1)S(1)} %bitcast.2, bf16[8,512,128]{2,1,0:T(8,128)(2,1)S(1)} %copy-done, bf16[1024,7168]{1,0:T(8,128)(2,1)S(1)} %get-tuple-element.15.proj_ref), custom_call_target="tpu_custom_call" | custom-call | flops 1073741824 | bytes 8388608 | tf_op jit(solution)/shard_map/values/pallas_call | solution.py:216
  35.2 1.0 %collective-permute-start.4 = (bf16[4,16,4096]{2,1,0:T(8,128)(2,1)S(1)}, bf16[4,16,4096]{2,1,0:T(8,128)(2,1)S(1)}, u32[]{:S(2)}, u32[]{:S(2)}) collective-permute-start(bf16[4,16,4096]{2,1,0:T(8,128)(2,1)S(1)} %get-tuple-element.22), channel_id=1, source_target_pairs={{0,68},{1,69},{2,70},{3,71},{4,64},{5,65},{6,66},{7,67},{8,76},{9,... | collective-permute-start | bytes 1572872 | tf_op jit(solution)/shard_map/ppermute | solution.py:379
  36.2 1.0 %project.1 = (bf16[2,16,3072]{2,1,0:T(8,128)(2,1)S(1)}, bf16[2,16,3072]{2,1,0:T(8,128)(2,1)S(1)}, bf16[2,16,3072]{2,1,0:T(8,128)(2,1)S(1)}, bf16[2,16,3072]{2,1,0:T(8,128)(2,1)S(1)}) custom-call(bf16[128,1024]{1,0:T(8,128)(2,1)S(1)} %get-tuple-element.16.values_ref, bf16[1024,7168]{1,0:T(8,128)(2,1)S(1)} %get-tuple-element.15.proj_ref), custom_call_target="tpu_custom_call" | custom-call | flops 805306368 | bytes 6291456 | tf_op jit(solution)/shard_map/project/pallas_call | solution.py:249
  37.2 0.9 %collective-permute-start = (bf16[2,16,3072]{2,1,0:T(8,128)(2,1)S(1)}, bf16[2,16,3072]{2,1,0:T(8,128)(2,1)S(1)}, u32[]{:S(2)}, u32[]{:S(2)}) collective-permute-start(bf16[2,16,3072]{2,1,0:T(8,128)(2,1)S(1)} %get-tuple-element.18), channel_id=1, source_target_pairs={{0,1},{1,2},{2,3},{3,0},{4,5},{5,6},{6,7},{7,4},{8,9},{9,10},{10,1... | collective-permute-start | bytes 589832 | tf_op jit(solution)/shard_map/ppermute | solution.py:366
  38.1 2.1 %collective-permute-start.1 = (bf16[2,16,3072]{2,1,0:T(8,128)(2,1)S(1)}, bf16[2,16,3072]{2,1,0:T(8,128)(2,1)S(1)}, u32[]{:S(2)}, u32[]{:S(2)}) collective-permute-start(bf16[2,16,3072]{2,1,0:T(8,128)(2,1)S(1)} %get-tuple-element.19), channel_id=1, source_target_pairs={{0,2},{1,3},{2,0},{3,1},{4,6},{5,7},{6,4},{7,5},{8,10},{9,11},{10,... | collective-permute-start | bytes 589832 | tf_op jit(solution)/shard_map/ppermute | solution.py:366
  40.2 0.7 %collective-permute-start.2 = (bf16[2,16,3072]{2,1,0:T(8,128)(2,1)S(1)}, bf16[2,16,3072]{2,1,0:T(8,128)(2,1)S(1)}, u32[]{:S(2)}, u32[]{:S(2)}) collective-permute-start(bf16[2,16,3072]{2,1,0:T(8,128)(2,1)S(1)} %get-tuple-element.20), channel_id=1, source_target_pairs={{0,3},{1,0},{2,1},{3,2},{4,7},{5,4},{6,5},{7,6},{8,11},{9,8},{10,9... | collective-permute-start | bytes 589832 | tf_op jit(solution)/shard_map/ppermute | solution.py:366
  40.9 8.7 %collective-permute-done.4.came_ref = bf16[4,16,4096]{2,1,0:T(8,128)(2,1)S(1)} collective-permute-done((bf16[4,16,4096]{2,1,0:T(8,128)(2,1)S(1)}, bf16[4,16,4096]{2,1,0:T(8,128)(2,1)S(1)}, u32[]{:S(2)}, u32[]{:S(2)}) %collective-permute-start.4) | collective-permute-done | bytes 524320 | tf_op jit(solution)/shard_map/ppermute | solution.py:379
  49.6 0.1 add_far.1
  49.7 0.1 collective-permute-start.5
  49.8 2.7 %collective-permute-start.6 = (bf16[16,4096]{1,0:T(8,128)(2,1)S(1)}, bf16[16,4096]{1,0:T(8,128)(2,1)S(1)}, u32[]{:S(2)}, u32[]{:S(2)}) collective-permute-start(bf16[16,4096]{1,0:T(8,128)(2,1)S(1)} %get-tuple-element.24), channel_id=1, source_target_pairs={{0,2},{1,3},{2,0},{3,1},{4,6},{5,7},{6,4},{7,5},{8,10},{9,11},{10,... | collective-permute-start | bytes 393224 | tf_op jit(solution)/shard_map/ppermute | solution.py:366
  52.5 0.0 collective-permute-done.refs_1_.near_refs_1_
  52.5 1.5 %collective-permute-start.7 = (bf16[16,4096]{1,0:T(8,128)(2,1)S(1)}, bf16[16,4096]{1,0:T(8,128)(2,1)S(1)}, u32[]{:S(2)}, u32[]{:S(2)}) collective-permute-start(bf16[16,4096]{1,0:T(8,128)(2,1)S(1)} %get-tuple-element.25), channel_id=1, source_target_pairs={{0,3},{1,0},{2,1},{3,2},{4,7},{5,4},{6,5},{7,6},{8,11},{9,8},{10,9... | collective-permute-start | bytes 393224 | tf_op jit(solution)/shard_map/ppermute | solution.py:366
  54.0 0.0 collective-permute-done.1.refs_2_.near_refs_2_
  54.0 0.0 collective-permute-done.2.refs_3_.near_refs_3_
  54.0 0.1 add_near.1
  54.0 1.2 %collective-permute-start.3 = (bf16[16,3072]{1,0:T(8,128)(2,1)S(1)}, bf16[16,3072]{1,0:T(8,128)(2,1)S(1)}, u32[]{:S(2)}, u32[]{:S(2)}) collective-permute-start(bf16[16,3072]{1,0:T(8,128)(2,1)S(1)} %add_near.1), channel_id=1, source_target_pairs={{0,68},{1,69},{2,70},{3,71},{4,64},{5,65},{6,66},{7,67},{8,76},{9,... | collective-permute-start | bytes 294920 | tf_op jit(solution)/shard_map/ppermute | solution.py:379
  55.2 0.0 copy-done.2
  55.3 4.7 %collective-permute-done.3.far_ref = bf16[16,3072]{1,0:T(8,128)(2,1)S(1)} collective-permute-done((bf16[16,3072]{1,0:T(8,128)(2,1)S(1)}, bf16[16,3072]{1,0:T(8,128)(2,1)S(1)}, u32[]{:S(2)}, u32[]{:S(2)}) %collective-permute-start.3) | collective-permute-done | bytes 98336 | tf_op jit(solution)/shard_map/ppermute | solution.py:379
  60.0 0.0 collective-permute-done.5.step_refs_0_
  60.0 0.0 collective-permute-done.6.step_refs_1_
  60.0 0.0 collective-permute-done.7.step_refs_2_
  60.0 0.0 copy-done.1
  60.0 1.0 %finish.1 = (bf16[16,7168]{1,0:T(8,128)(2,1)}, bf16[16,7168]{1,0:T(8,128)(2,1)}) custom-call(bf16[2,16,3072]{2,1,0:T(8,128)(2,1)S(1)} %get-tuple-element.17.refs_0_.near_refs_0_, bf16[2,16,3072]{2,1,0:T(8,128)(2,1)S(1)} %collective-permute-done.refs_1_.near_refs_1_, bf16[2,16,3072]{2,1,0:T(8,128)(2,1)S(1)} %collective-permute-done.1.refs_2_.near_refs_2_, ...), custom_call_target="tpu_custom_call" | custom-call | tf_op jit(solution)/shard_map/finish/pallas_call | solution.py:329
  (1 shorter events, 0.0 us)
Async XLA Ops:
  0.6 32.6 %copy-start = (bf16[8,512,128]{2,1,0:T(8,128)(2,1)S(1)}, bf16[8,512,128]{2,1,0:T(8,128)(2,1)}, u32[]{:S(2)}) copy-start(bf16[8,512,128]{2,1,0:T(8,128)(2,1)} %value_up_ref.1) | copy-start | bytes 3145732
  33.2 22.0 %copy-start.2 = (bf16[7168]{0:T(1024)(128)(2,1)S(1)}, bf16[7168]{0:T(1024)(128)(2,1)}, u32[]{:S(2)}) copy-start(bf16[7168]{0:T(1024)(128)(2,1)} %param.15) | copy-start | bytes 43012
  33.2 26.8 %copy-start.1 = (bf16[16,7168]{1,0:T(8,128)(2,1)S(1)}, bf16[16,7168]{1,0:T(8,128)(2,1)}, u32[]{:S(2)}) copy-start(bf16[16,7168]{1,0:T(8,128)(2,1)} %residual_ref.1) | copy-start | bytes 688132
  35.2 14.4 %collective-permute-start.4 = (bf16[4,16,4096]{2,1,0:T(8,128)(2,1)S(1)}, bf16[4,16,4096]{2,1,0:T(8,128)(2,1)S(1)}, u32[]{:S(2)}, u32[]{:S(2)}) collective-permute-start(bf16[4,16,4096]{2,1,0:T(8,128)(2,1)S(1)} %get-tuple-element.22), channel_id=1, source_target_pairs={{0,68},{1,69},{2,70},{3,71},{4,64},{5,65},{6,66},{7,67},{8,76},{9,... | collective-permute-start | bytes 1572872 | tf_op jit(solution)/shard_map/ppermute | solution.py:379
  37.2 15.3 %collective-permute-start = (bf16[2,16,3072]{2,1,0:T(8,128)(2,1)S(1)}, bf16[2,16,3072]{2,1,0:T(8,128)(2,1)S(1)}, u32[]{:S(2)}, u32[]{:S(2)}) collective-permute-start(bf16[2,16,3072]{2,1,0:T(8,128)(2,1)S(1)} %get-tuple-element.18), channel_id=1, source_target_pairs={{0,1},{1,2},{2,3},{3,0},{4,5},{5,6},{6,7},{7,4},{8,9},{9,10},{10,1... | collective-permute-start | bytes 589832 | tf_op jit(solution)/shard_map/ppermute | solution.py:366
  38.1 15.9 %collective-permute-start.1 = (bf16[2,16,3072]{2,1,0:T(8,128)(2,1)S(1)}, bf16[2,16,3072]{2,1,0:T(8,128)(2,1)S(1)}, u32[]{:S(2)}, u32[]{:S(2)}) collective-permute-start(bf16[2,16,3072]{2,1,0:T(8,128)(2,1)S(1)} %get-tuple-element.19), channel_id=1, source_target_pairs={{0,2},{1,3},{2,0},{3,1},{4,6},{5,7},{6,4},{7,5},{8,10},{9,11},{10,... | collective-permute-start | bytes 589832 | tf_op jit(solution)/shard_map/ppermute | solution.py:366
  40.2 13.8 %collective-permute-start.2 = (bf16[2,16,3072]{2,1,0:T(8,128)(2,1)S(1)}, bf16[2,16,3072]{2,1,0:T(8,128)(2,1)S(1)}, u32[]{:S(2)}, u32[]{:S(2)}) collective-permute-start(bf16[2,16,3072]{2,1,0:T(8,128)(2,1)S(1)} %get-tuple-element.20), channel_id=1, source_target_pairs={{0,3},{1,0},{2,1},{3,2},{4,7},{5,4},{6,5},{7,6},{8,11},{9,8},{10,9... | collective-permute-start | bytes 589832 | tf_op jit(solution)/shard_map/ppermute | solution.py:366
  49.7 10.2 %collective-permute-start.5 = (bf16[16,4096]{1,0:T(8,128)(2,1)S(1)}, bf16[16,4096]{1,0:T(8,128)(2,1)S(1)}, u32[]{:S(2)}, u32[]{:S(2)}) collective-permute-start(bf16[16,4096]{1,0:T(8,128)(2,1)S(1)} %get-tuple-element.23), channel_id=1, source_target_pairs={{0,1},{1,2},{2,3},{3,0},{4,5},{5,6},{6,7},{7,4},{8,9},{9,10},{10,1... | collective-permute-start | bytes 393224 | tf_op jit(solution)/shard_map/ppermute | solution.py:366
  49.8 10.1 %collective-permute-start.6 = (bf16[16,4096]{1,0:T(8,128)(2,1)S(1)}, bf16[16,4096]{1,0:T(8,128)(2,1)S(1)}, u32[]{:S(2)}, u32[]{:S(2)}) collective-permute-start(bf16[16,4096]{1,0:T(8,128)(2,1)S(1)} %get-tuple-element.24), channel_id=1, source_target_pairs={{0,2},{1,3},{2,0},{3,1},{4,6},{5,7},{6,4},{7,5},{8,10},{9,11},{10,... | collective-permute-start | bytes 393224 | tf_op jit(solution)/shard_map/ppermute | solution.py:366
  52.5 7.4 %collective-permute-start.7 = (bf16[16,4096]{1,0:T(8,128)(2,1)S(1)}, bf16[16,4096]{1,0:T(8,128)(2,1)S(1)}, u32[]{:S(2)}, u32[]{:S(2)}) collective-permute-start(bf16[16,4096]{1,0:T(8,128)(2,1)S(1)} %get-tuple-element.25), channel_id=1, source_target_pairs={{0,3},{1,0},{2,1},{3,2},{4,7},{5,4},{6,5},{7,6},{8,11},{9,8},{10,9... | collective-permute-start | bytes 393224 | tf_op jit(solution)/shard_map/ppermute | solution.py:366
  54.0 5.9 %collective-permute-start.3 = (bf16[16,3072]{1,0:T(8,128)(2,1)S(1)}, bf16[16,3072]{1,0:T(8,128)(2,1)S(1)}, u32[]{:S(2)}, u32[]{:S(2)}) collective-permute-start(bf16[16,3072]{1,0:T(8,128)(2,1)S(1)} %add_near.1), channel_id=1, source_target_pairs={{0,68},{1,69},{2,70},{3,71},{4,64},{5,65},{6,66},{7,67},{8,76},{9,... | collective-permute-start | bytes 294920 | tf_op jit(solution)/shard_map/ppermute | solution.py:379
where the time goes:
time: 61.1 us; the launch traced here: 61 us
  blocking collectives  25 us (41%)
  waiting for transfers between devices  13.4 us (22%)
  Pallas kernels  11.7 us (19%)
  starting transfers between devices  10.1 us (17%)
  between operations  0.7 us (1%)
    all_to_all x1, blocking collectives, exchange(): lax.all_to_all(blocks, ('rep', 'dp'), split_axis=0, concat_axis=0, axis_i...  25 us
    ppermute x2, waiting for transfers between devices, step_across(): return lax.ppermute(array, ('rep', 'dp'), pairs)  13.4 us
    ppermute x6, starting transfers between devices, step_along(): return lax.ppermute(array, 'dp', pairs)  7.95 us
    pallas_call x1, Pallas kernels, attend(): pl.pallas_call(attend_kernel, out_shape=(jax.ShapeDtypeStruct((owners, ro...  7.56 us
    ppermute x2, starting transfers between devices, step_across(): return lax.ppermute(array, ('rep', 'dp'), pairs)  2.2 us
    pallas_call x1, Pallas kernels, make_values(): pl.pallas_call(values_kernel, out_shape=(jax.ShapeDtypeStruct((rows, owne...  2 us
  transfers between devices with their start and end apart: 8, of which 2 were waited for; matrix products, arithmetic and copies ran while one was open for 0% of the time, Pallas kernels for 2%

commit v1 on v0

v1 whole, which is shorter than its diff:
```python
import jax
import jax.numpy as jnp
from jax import lax
from jax.experimental import pallas as pl
from jax.experimental.pallas import tpu as pltpu
from jax.sharding import PartitionSpec as P

LAT = 512
GROUP_ROWS = 4
PROJ_STEP = 1024
LEFT_COLUMNS = 3328
score_scale = 192.0 ** (-0.5)
norm_eps = 1e-06
MIB = 1024 * 1024


def attend_kernel(
    lengths_hbm, queries_hbm, latent_hbm, cache_hbm, *refs
):
    *owner_refs, out_ref = refs[:-11]
    (
        held, queries_ref, latent_ref, latent_wide, gathered_ref, softmax_ref,
        lengths_ref, order, arrived_small, arrived_first, arrived_second,
    ) = refs[-11:]
    row_count, width, span = held.shape
    owners, _, _ = out_ref.shape
    heads = queries_ref.shape[1]
    owned = heads // owners
    first_row = lax.axis_index("dp") * row_count
    pair_count = row_count // 2
    group_count = row_count // GROUP_ROWS
    group_pairs = GROUP_ROWS // 2
    short = span // 2

    lengths_copy = pltpu.make_async_copy(lengths_hbm, lengths_ref, arrived_small.at[0])
    latent_copy = pltpu.make_async_copy(latent_hbm, latent_ref, arrived_small.at[1])

    def fetch_first(group):
        rows, keys = pl.ds(group * GROUP_ROWS, GROUP_ROWS), pl.ds(0, short)
        return (
            pltpu.make_async_copy(
                queries_hbm.at[rows], queries_ref.at[rows], arrived_first.at[0, group]
            ),
            pltpu.make_async_copy(
                cache_hbm.at[rows, :, keys], held.at[rows, :, keys], arrived_first.at[1, group]
            ),
        )

    def fetch_second(slot):
        rows, keys = pl.ds(2 * order[slot], 2), pl.ds(short, short)
        return pltpu.make_async_copy(
            cache_hbm.at[rows, :, keys], held.at[rows, :, keys], arrived_second.at[slot]
        )

    def start_first(group):
        for copy in fetch_first(group):
            copy.start()

    start_first(0)
    lengths_copy.start()
    latent_copy.start()
    start_first(1)

    lengths_copy.wait()
    longest = [
        jnp.maximum(lengths_ref[first_row + 2 * pair], lengths_ref[first_row + 2 * pair + 1])
        for pair in range(pair_count)
    ]
    is_long = [(length > short).astype(jnp.int32) for length in longest]
    long_slot, short_slot = 0, sum(is_long)
    long_groups = (short_slot + group_pairs - 1) // group_pairs
    for pair in range(pair_count):
        order[jnp.where(is_long[pair] == 1, long_slot, short_slot)] = pair
        long_slot = long_slot + is_long[pair]
        short_slot = short_slot + 1 - is_long[pair]
    latent_copy.wait()
    latent_wide[...] = latent_ref[...].astype(jnp.float32)

    def score(row, start):
        scores = jnp.dot(
            queries_ref[row],
            held[row, :, start : start + short],
            preferred_element_type=jnp.float32,
        )
        position = start + lax.broadcasted_iota(jnp.int32, scores.shape, 1)
        return jnp.where(
            position < lengths_ref[first_row + row], scores * score_scale, -jnp.inf
        )

    def gather(row, start, raised):
        return lax.dot_general(
            raised.astype(jnp.bfloat16),
            held[row, :LAT, start : start + short],
            (((1,), (1,)), ((), ())),
            preferred_element_type=jnp.float32,
        )

    def weigh_first(row, scores):
        fresh = latent_wide[pl.ds(row, 1), :]
        self_score = (
            jnp.sum(queries_ref[row].astype(jnp.float32) * fresh, axis=1, keepdims=True)
            * score_scale
        )
        row_max = jnp.maximum(jnp.max(scores, axis=1, keepdims=True), self_score)
        raised = jnp.exp(scores - row_max)
        self_raised = jnp.exp(self_score - row_max)
        row_total = jnp.sum(raised, axis=1, keepdims=True) + self_raised
        self_weight = self_raised.astype(jnp.bfloat16).astype(jnp.float32)
        softmax_ref[row, :, 0:1] = row_max
        softmax_ref[row, :, 1:2] = row_total
        return raised, self_weight * fresh[:, :LAT], row_total

    def weigh_second(row, scores):
        old_max = softmax_ref[row, :, 0:1]
        row_max = jnp.maximum(jnp.max(scores, axis=1, keepdims=True), old_max)
        raised = jnp.exp(scores - row_max)
        kept = jnp.exp(old_max - row_max)
        row_total = softmax_ref[row, :, 1:2] * kept + jnp.sum(raised, axis=1, keepdims=True)
        return raised, kept, row_total

    def first_half(group, carry):
        for copy in fetch_first(group):
            copy.wait()

        @pl.when(group + 2 < group_count)
        def _():
            start_first(group + 2)

        @pl.when(group == group_count - 2)
        def _():
            def start(slot, carry):
                fetch_second(slot).start()
                return carry

            lax.fori_loop(0, long_groups * group_pairs, start, 0)

        rows = [group * GROUP_ROWS + i for i in range(GROUP_ROWS)]
        scores = [score(row, 0) for row in rows]
        weighed = [weigh_first(row, some) for row, some in zip(rows, scores)]
        done = []
        for row, (raised, fresh_part, row_total) in zip(rows, weighed):
            gathered = gather(row, 0, raised) + fresh_part
            gathered_ref[row] = gathered
            done.append((gathered / row_total).reshape(owners, owned, LAT))
        size = GROUP_ROWS * owned
        out_ref[:, pl.ds(pl.multiple_of(group * size, size), size), :] = jnp.concatenate(
            done, axis=1
        ).astype(jnp.bfloat16)
        return carry

    def second_half(group, carry):
        slots = [group * group_pairs + i for i in range(group_pairs)]
        for slot in slots:
            fetch_second(slot).wait()
        pairs = [order[slot] for slot in slots]
        rows = [2 * pair + i for pair in pairs for i in range(2)]
        scores = [score(row, short) for row in rows]
        weighed = [weigh_second(row, some) for row, some in zip(rows, scores)]
        done = []
        for row, (raised, kept, row_total) in zip(rows, weighed):
            gathered = gather(row, short, raised) + gathered_ref[row] * kept
            done.append((gathered / row_total).reshape(owners, owned, LAT))
        size = 2 * owned
        for i, pair in enumerate(pairs):
            out_ref[:, pl.ds(pl.multiple_of(pair * size, size), size), :] = jnp.concatenate(
                done[2 * i : 2 * i + 2], axis=1
            ).astype(jnp.bfloat16)
        return carry

    lax.fori_loop(0, group_count, first_half, 0)
    lax.fori_loop(0, long_groups, second_half, 0)
    here = lax.axis_index("dp")
    z_size = owners // 2
    for place, owner_ref in enumerate(owner_refs):
        far = (here // z_size + place // z_size) % 2
        owner_ref[...] = out_ref[far * z_size + (here + place) % z_size]


def attend(queries, latent_cache, new_latent, lengths, owners):
    row_count, span, width = latent_cache.shape
    heads = queries.shape[1]
    owned = heads // owners
    vmem = pl.BlockSpec(memory_space=pltpu.VMEM)
    hbm = pl.BlockSpec(memory_space=pltpu.HBM)
    arrays = (lengths, queries, new_latent, jnp.swapaxes(latent_cache, 1, 2))
    return pl.pallas_call(
        attend_kernel,
        out_shape=[jax.ShapeDtypeStruct((row_count * owned, LAT), jnp.bfloat16)] * owners,
        in_specs=[hbm] * len(arrays),
        out_specs=[vmem] * owners,
        scratch_shapes=[
            pltpu.VMEM((owners, row_count * owned, LAT), jnp.bfloat16),
            pltpu.VMEM((row_count, width, span), jnp.bfloat16),
            pltpu.VMEM(queries.shape, jnp.bfloat16),
            pltpu.VMEM(new_latent.shape, jnp.bfloat16),
            pltpu.VMEM(new_latent.shape, jnp.float32),
            pltpu.VMEM((row_count, heads, LAT), jnp.float32),
            pltpu.VMEM((row_count, heads, 128), jnp.float32),
            pltpu.SMEM(lengths.shape, jnp.int32),
            pltpu.SMEM((row_count // 2,), jnp.int32),
            pltpu.SemaphoreType.DMA((2,)),
            pltpu.SemaphoreType.DMA((2, row_count // GROUP_ROWS)),
            pltpu.SemaphoreType.DMA((row_count // 2,)),
        ],
        cost_estimate=pl.CostEstimate(
            flops=4 * row_count * heads * span * width,
            bytes_accessed=2 * row_count * span * width,
            transcendentals=row_count * heads * span,
        ),
        compiler_params=pltpu.CompilerParams(vmem_limit_bytes=24 * MIB),
        name="attend",
    )(*(pltpu.with_memory_space_constraint(x, pltpu.HBM) for x in arrays))


def bring_kernel(after_hbm, proj_hbm, proj_ref, arrived):
    del after_hbm
    copy = pltpu.make_async_copy(proj_hbm, proj_ref, arrived)
    copy.start()
    copy.wait()


def bring(output_proj, after):
    return pl.pallas_call(
        bring_kernel,
        out_shape=pltpu.VMEM(output_proj.shape, jnp.bfloat16),
        in_specs=[pl.BlockSpec(memory_space=pl.ANY), pl.BlockSpec(memory_space=pltpu.HBM)],
        out_specs=pl.BlockSpec(memory_space=pltpu.VMEM),
        scratch_shapes=[pltpu.SemaphoreType.DMA],
        cost_estimate=pl.CostEstimate(
            flops=0, bytes_accessed=2 * output_proj.size, transcendentals=0
        ),
        compiler_params=pltpu.CompilerParams(vmem_limit_bytes=16 * MIB),
        name="bring",
    )(after, pltpu.with_memory_space_constraint(output_proj, pltpu.HBM))


def values_kernel(latent_refs, value_up_ref, proj_ref, values_ref, own_ref, send_ref, wide):
    owned, lat, value_size = value_up_ref.shape
    owners, rows_here, columns = 2 * own_ref.shape[0], own_ref.shape[1], own_ref.shape[2]
    rows = owners * rows_here
    z_size = owners // 2

    size = rows_here * owned
    for place, latent_ref in enumerate(latent_refs):
        far, step = place // z_size, place % z_size
        back = (far * z_size + (z_size - step) % z_size) * size
        for c in range(lat // 128):
            wide[c, back : back + size] = latent_ref[:, c * 128 : (c + 1) * 128].astype(
                jnp.float32
            )
    for h in range(owned):
        mine = jnp.concatenate(
            [wide[c, pl.ds(h, rows, stride=owned), :] for c in range(lat // 128)], axis=1
        ).astype(jnp.bfloat16)
        values_ref[:, h * value_size : (h + 1) * value_size] = jnp.dot(
            mine, value_up_ref[h], preferred_element_type=jnp.float32
        ).astype(jnp.bfloat16)
    flattened = values_ref[...]
    for start in range(0, columns, PROJ_STEP):
        stop = min(start + PROJ_STEP, columns)
        done = jnp.dot(
            flattened,
            proj_ref[:, LEFT_COLUMNS + start : LEFT_COLUMNS + stop],
            preferred_element_type=jnp.float32,
        ).astype(jnp.bfloat16)
        done = done.reshape(2, z_size, rows_here, stop - start)
        own_ref[:, :, start:stop] = done[0]
        send_ref[:, :, start:stop] = done[1]


def make_values(owned_latents, value_up, output_proj, owners, rows_here):
    owned, lat, value_size = value_up.shape
    depth, width = output_proj.shape
    columns = width - LEFT_COLUMNS
    rows = owners * rows_here
    vmem = pl.BlockSpec(memory_space=pltpu.VMEM)
    half = jax.ShapeDtypeStruct((owners // 2, rows_here, columns), jnp.bfloat16)
    return pl.pallas_call(
        values_kernel,
        out_shape=(jax.ShapeDtypeStruct((rows, owned * value_size), jnp.bfloat16), half, half),
        in_specs=[[vmem] * owners, vmem, vmem],
        out_specs=(vmem, vmem, vmem),
        scratch_shapes=[pltpu.VMEM((lat // 128, rows * owned, 128), jnp.float32)],
        cost_estimate=pl.CostEstimate(
            flops=2 * rows * depth * columns, bytes_accessed=2 * depth * columns, transcendentals=0
        ),
        compiler_params=pltpu.CompilerParams(vmem_limit_bytes=20 * MIB),
        name="values",
    )(owned_latents, value_up, pltpu.with_memory_space_constraint(output_proj, pltpu.VMEM))


def project_kernel(values_ref, proj_ref, *out_refs):
    rows_here, columns = out_refs[0].shape[1:]
    z_size = len(out_refs)
    flattened = values_ref[...]
    for start in range(0, columns, PROJ_STEP):
        stop = min(start + PROJ_STEP, columns)
        done = jnp.dot(
            flattened, proj_ref[:, start:stop], preferred_element_type=jnp.float32
        ).astype(jnp.bfloat16)
        done = done.reshape(2, z_size, rows_here, stop - start)
        for step in range(z_size):
            out_refs[step][:, :, start:stop] = done[:, step]


def project(values, output_proj, owners, rows_here):
    rows, depth = values.shape
    columns = LEFT_COLUMNS
    z_size = owners // 2
    vmem = pl.BlockSpec(memory_space=pltpu.VMEM)
    part = jax.ShapeDtypeStruct((2, rows_here, columns), jnp.bfloat16)
    return pl.pallas_call(
        project_kernel,
        out_shape=[part] * z_size,
        in_specs=[vmem, vmem],
        out_specs=[vmem] * z_size,
        cost_estimate=pl.CostEstimate(
            flops=2 * rows * depth * columns, bytes_accessed=2 * depth * columns, transcendentals=0
        ),
        compiler_params=pltpu.CompilerParams(vmem_limit_bytes=20 * MIB),
        name="project",
    )(values, pltpu.with_memory_space_constraint(output_proj, pltpu.VMEM))


def add_far_kernel(own_ref, came_ref, *out_refs):
    for step, out_ref in enumerate(out_refs, 1):
        both = own_ref[step].astype(jnp.float32) + came_ref[step].astype(jnp.float32)
        out_ref[...] = both.astype(jnp.bfloat16)


def add_far(own, came):
    vmem = pl.BlockSpec(memory_space=pltpu.VMEM)
    return pl.pallas_call(
        add_far_kernel,
        out_shape=[jax.ShapeDtypeStruct(own.shape[1:], jnp.bfloat16)] * (own.shape[0] - 1),
        in_specs=[vmem, vmem],
        out_specs=[vmem] * (own.shape[0] - 1),
        cost_estimate=pl.CostEstimate(flops=own.size, bytes_accessed=own.size * 6, transcendentals=0),
        compiler_params=pltpu.CompilerParams(vmem_limit_bytes=16 * MIB),
        name="add_far",
    )(own, came)


def add_near_kernel(*refs):
    *part_refs, out_ref = refs
    total = part_refs[0][1].astype(jnp.float32)
    for part_ref in part_refs[1:]:
        total = total + part_ref[1].astype(jnp.float32)
    out_ref[...] = total.astype(jnp.bfloat16)


def add_near(parts):
    vmem = pl.BlockSpec(memory_space=pltpu.VMEM)
    return pl.pallas_call(
        add_near_kernel,
        out_shape=jax.ShapeDtypeStruct(parts[0].shape[1:], jnp.bfloat16),
        in_specs=[vmem] * len(parts),
        out_specs=vmem,
        cost_estimate=pl.CostEstimate(
            flops=parts[0].size * 2, bytes_accessed=parts[0].size * 8, transcendentals=0
        ),
        compiler_params=pltpu.CompilerParams(vmem_limit_bytes=16 * MIB),
        name="add_near",
    )(*parts)


def finish_kernel(near_refs, far_ref, own_ref, came_ref, step_refs, residual_ref, gain_ref,
                  hidden_ref, normed_ref):
    rows, first = far_ref.shape
    width = residual_ref.shape[1]
    left = residual_ref[:, :first].astype(jnp.float32) + far_ref[...].astype(jnp.float32)
    for near_ref in near_refs:
        left = left + near_ref[0].astype(jnp.float32)
    right = residual_ref[:, first:].astype(jnp.float32) + (
        own_ref[0].astype(jnp.float32) + came_ref[0].astype(jnp.float32)
    )
    for step_ref in step_refs:
        right = right + step_ref[...].astype(jnp.float32)
    total = jnp.sum(left * left, axis=1, keepdims=True) + jnp.sum(
        right * right, axis=1, keepdims=True
    )
    inverse_rms = lax.rsqrt(total * (1.0 / width) + norm_eps)
    for part, here in ((left, slice(0, first)), (right, slice(first, width))):
        hidden_ref[:, here] = part.astype(jnp.bfloat16)
        normed = part * inverse_rms * gain_ref[:, here].astype(jnp.float32)
        normed_ref[:, here] = normed.astype(jnp.bfloat16)


def finish(nears, far, own, came, steps, residual, norm_gain):
    vmem = pl.BlockSpec(memory_space=pltpu.VMEM)
    shape = jax.ShapeDtypeStruct(residual.shape, jnp.bfloat16)
    return pl.pallas_call(
        finish_kernel,
        out_shape=(shape, shape),
        in_specs=[[vmem] * len(nears), vmem, vmem, vmem, [vmem] * len(steps), vmem, vmem],
        out_specs=(vmem, vmem),
        compiler_params=pltpu.CompilerParams(vmem_limit_bytes=32 * MIB),
        name="finish",
    )(nears, far, own, came, steps, residual, norm_gain.reshape(1, -1))


def send(array, far, step, mesh_shape):
    replicas, owners = mesh_shape
    z_size = owners // 2
    pairs = []
    for replica in range(replicas):
        for owner in range(owners):
            to_replica = (replica + far * (replicas // 2)) % replicas
            to_half = (owner // z_size + far) % 2
            to_owner = to_half * z_size + (owner + step) % z_size
            pairs.append((replica * owners + owner, to_replica * owners + to_owner))
    return lax.ppermute(array, ("rep", "dp"), pairs)


def per_device(
    queries, latent_cache, new_latent, lengths, value_up, output_proj, residual, norm_gain
):
    owners = lax.axis_size("dp")
    mesh_shape = (lax.axis_size("rep"), owners)
    rows_here = latent_cache.shape[0]
    z_size = owners // 2
    latents = attend(queries, latent_cache, new_latent, lengths, owners)
    owned_latents = [latents[0]] + [
        send(latents[place], place // z_size, place % z_size, mesh_shape)
        for place in range(1, owners)
    ]
    proj_near = bring(output_proj, latents[0])
    values, own, across = make_values(owned_latents, value_up, proj_near, owners, rows_here)
    came = send(across, 1, 0, mesh_shape)
    parts = project(values, proj_near, owners, rows_here)
    nears = [parts[0]] + [send(parts[k], 0, k, mesh_shape) for k in range(1, z_size)]
    pairs = add_far(own, came)
    steps = [send(pair, 0, k, mesh_shape) for k, pair in enumerate(pairs, 1)]
    far = send(add_near(nears), 1, 0, mesh_shape)
    return finish(nears, far, own, came, steps, residual, norm_gain)


def solution(mesh):
    return jax.shard_map(
        per_device,
        mesh=mesh,
        in_specs=(
            P(("rep", "dp"), None, None),
            P(("rep", "dp"), None, None),
            P(("rep", "dp"), None),
            P("rep"),
            P("dp", None, None),
            P("dp", None),
            P(("rep", "dp"), None),
            P(),
        ),
        out_specs=(P(("rep", "dp"), None), P(("rep", "dp"), None)),
        check_vma=False,
    )
```

time: 61.1 us -> 57.7 us (0.944)
  the two profiles are of different devices: /device:TPU:4 before, /device:TPU:0 now
where the time goes in v1:
time: 57.7 us; the launch traced here: 56.8 us
  starting transfers between devices  29.4 us (51%)
  Pallas kernels  13.9 us (24%)
  waiting for transfers between devices  12.8 us (22%)
  between operations  0.75 us (1%)
    ppermute x15, starting transfers between devices, send(): return lax.ppermute(array, ('rep', 'dp'), pairs)  29.4 us
    ppermute x15, waiting for transfers between devices, send(): return lax.ppermute(array, ('rep', 'dp'), pairs)  12.8 us
    pallas_call x1, Pallas kernels, bring(): pl.pallas_call(bring_kernel, out_shape=pltpu.VMEM(output_proj.shape, jnp....  5.27 us
    pallas_call x1, Pallas kernels, attend(): pl.pallas_call(attend_kernel, out_shape=[jax.ShapeDtypeStruct((row_count...  4.55 us
    pallas_call x1, Pallas kernels, make_values(): pl.pallas_call(values_kernel, out_shape=(jax.ShapeDtypeStruct((rows, owne...  1.82 us
  transfers between devices with their start and end apart: 15, of which 3 were waited for; matrix products, arithmetic and copies ran while one was open for 0% of the time, Pallas kernels for 11%

profile of v1, /device:TPU:0, one launch (start us, length us, event | category | flops | bytes accessed | tf_op | source)
XLA Modules:
  0.0 56.8 jit_solution(18405217931451540758)
XLA Ops:
  0.6 4.6 %attend.1 = (bf16[128,512]{1,0:T(8,128)(2,1)S(1)}, bf16[128,512]{1,0:T(8,128)(2,1)S(1)}, bf16[128,512]{1,0:T(8,128)(2,1)S(1)}, bf16[128,512]{1,0:T(8,128)(2,1)S(...) custom-call(s32[128]{0:T(128)} %lengths_hbm.1, ...), custom_call_target="tpu_custom_call" | custom-call | flops 1207959552 | bytes 9437184 | tf_op jit(solution)/shard_map/attend/pallas_call | solution.py:186
  5.2 2.1 %collective-permute-start = (bf16[128,512]{1,0:T(8,128)(2,1)S(1)}, bf16[128,512]{1,0:T(8,128)(2,1)S(1)}, u32[]{:S(2)}, u32[]{:S(2)}) collective-permute-start(bf16[128,512]{1,0:T(8,128)(2,1)S(1)} %get-tuple-element.21), channel_id=1, source_target_pairs={{0,1},{1,2},{2,3},{3,0},{4,5},{5,6},{6,7},{7,4},{8,9},{9,10},{10,1... | collective-permute-start | bytes 393224 | tf_op jit(solution)/shard_map/ppermute | solution.py:412
  7.3 3.6 %collective-permute-start.1 = (bf16[128,512]{1,0:T(8,128)(2,1)S(1)}, bf16[128,512]{1,0:T(8,128)(2,1)S(1)}, u32[]{:S(2)}, u32[]{:S(2)}) collective-permute-start(bf16[128,512]{1,0:T(8,128)(2,1)S(1)} %get-tuple-element.22), channel_id=1, source_target_pairs={{0,2},{1,3},{2,0},{3,1},{4,6},{5,7},{6,4},{7,5},{8,10},{9,11},{10,... | collective-permute-start | bytes 393224 | tf_op jit(solution)/shard_map/ppermute | solution.py:412
  10.8 1.0 %collective-permute-start.2 = (bf16[128,512]{1,0:T(8,128)(2,1)S(1)}, bf16[128,512]{1,0:T(8,128)(2,1)S(1)}, u32[]{:S(2)}, u32[]{:S(2)}) collective-permute-start(bf16[128,512]{1,0:T(8,128)(2,1)S(1)} %get-tuple-element.23), channel_id=1, source_target_pairs={{0,3},{1,0},{2,1},{3,2},{4,7},{5,4},{6,5},{7,6},{8,11},{9,8},{10,9... | collective-permute-start | bytes 393224 | tf_op jit(solution)/shard_map/ppermute | solution.py:412
  11.9 3.0 %collective-permute-start.3 = (bf16[128,512]{1,0:T(8,128)(2,1)S(1)}, bf16[128,512]{1,0:T(8,128)(2,1)S(1)}, u32[]{:S(2)}, u32[]{:S(2)}) collective-permute-start(bf16[128,512]{1,0:T(8,128)(2,1)S(1)} %get-tuple-element.24), channel_id=1, source_target_pairs={{0,68},{1,69},{2,70},{3,71},{4,64},{5,65},{6,66},{7,67},{8,76},{9,... | collective-permute-start | bytes 393224 | tf_op jit(solution)/shard_map/ppermute | solution.py:412
  14.9 0.7 %collective-permute-start.4 = (bf16[128,512]{1,0:T(8,128)(2,1)S(1)}, bf16[128,512]{1,0:T(8,128)(2,1)S(1)}, u32[]{:S(2)}, u32[]{:S(2)}) collective-permute-start(bf16[128,512]{1,0:T(8,128)(2,1)S(1)} %get-tuple-element.25), channel_id=1, source_target_pairs={{0,69},{1,70},{2,71},{3,68},{4,65},{5,66},{6,67},{7,64},{8,77},{9,... | collective-permute-start | bytes 393224 | tf_op jit(solution)/shard_map/ppermute | solution.py:412
  15.5 0.0 collective-permute-done.latent_refs_1_
  15.6 2.9 %collective-permute-start.5 = (bf16[128,512]{1,0:T(8,128)(2,1)S(1)}, bf16[128,512]{1,0:T(8,128)(2,1)S(1)}, u32[]{:S(2)}, u32[]{:S(2)}) collective-permute-start(bf16[128,512]{1,0:T(8,128)(2,1)S(1)} %get-tuple-element.26), channel_id=1, source_target_pairs={{0,70},{1,71},{2,68},{3,69},{4,66},{5,67},{6,64},{7,65},{8,78},{9,... | collective-permute-start | bytes 393224 | tf_op jit(solution)/shard_map/ppermute | solution.py:412
  18.4 0.0 collective-permute-done.1.latent_refs_2_
  18.5 2.2 %collective-permute-start.6 = (bf16[128,512]{1,0:T(8,128)(2,1)S(1)}, bf16[128,512]{1,0:T(8,128)(2,1)S(1)}, u32[]{:S(2)}, u32[]{:S(2)}) collective-permute-start(bf16[128,512]{1,0:T(8,128)(2,1)S(1)} %get-tuple-element.27), channel_id=1, source_target_pairs={{0,71},{1,68},{2,69},{3,70},{4,67},{5,64},{6,65},{7,66},{8,79},{9,... | collective-permute-start | bytes 393224 | tf_op jit(solution)/shard_map/ppermute | solution.py:412
  20.7 0.0 copy-start
  20.7 5.3 %bring.1.proj_ref = bf16[1024,7168]{1,0:T(8,128)(2,1)S(1)} custom-call(bf16[128,512]{1,0:T(8,128)(2,1)S(1)} %get-tuple-element.20.after_hbm.latent_refs_0_, bf16[1024,7168]{1,0:T(8,128)(2,1)} %proj_hbm.1), custom_call_target="tpu_custom_call" | custom-call | bytes 14680064 | tf_op jit(solution)/shard_map/bring/pallas_call | solution.py:223
  26.0 0.0 copy-start.2
  26.0 0.0 copy-start.1
  26.0 0.0 collective-permute-done.2.latent_refs_3_
  26.0 0.0 collective-permute-done.3.latent_refs_4_
  26.0 0.0 collective-permute-done.4.latent_refs_5_
  26.0 0.0 collective-permute-done.5.latent_refs_6_
  26.0 1.4 %collective-permute-done.6.latent_refs_7_ = bf16[128,512]{1,0:T(8,128)(2,1)S(1)} collective-permute-done((bf16[128,512]{1,0:T(8,128)(2,1)S(1)}, bf16[128,512]{1,0:T(8,128)(2,1)S(1)}, u32[]{:S(2)}, u32[]{:S(2)}) %collective-permute-start.6) | collective-permute-done | bytes 131104 | tf_op jit(solution)/shard_map/ppermute | solution.py:412
  27.4 0.0 copy-done
  27.4 1.8 %values.1 = (bf16[128,1024]{1,0:T(8,128)(2,1)S(1)}, bf16[4,16,3840]{2,1,0:T(8,128)(2,1)S(1)}, bf16[4,16,3840]{2,1,0:T(8,128)(2,1)S(1)}) custom-call(bf16[128,512]{1,0:T(8,128)(2,1)S(1)} %get-tuple-element.20.after_hbm.latent_refs_0_, bf16[128,512]{1,0:T(8,128)(2,1)S(1)} %collective-permute-done.latent_refs_1_, ...), custom_call_target="tpu_custom_call" | custom-call | flops 1006632960 | bytes 7864320 | tf_op jit(solution)/shard_map/values/pallas_call | solution.py:278
  29.3 2.6 %collective-permute-start.11 = (bf16[4,16,3840]{2,1,0:T(8,128)(2,1)S(1)}, bf16[4,16,3840]{2,1,0:T(8,128)(2,1)S(1)}, u32[]{:S(2)}, u32[]{:S(2)}) collective-permute-start(bf16[4,16,3840]{2,1,0:T(8,128)(2,1)S(1)} %get-tuple-element.34), channel_id=1, source_target_pairs={{0,68},{1,69},{2,70},{3,71},{4,64},{5,65},{6,66},{7,67},{8,76},{9,... | collective-permute-start | bytes 1474568 | tf_op jit(solution)/shard_map/ppermute | solution.py:412
  31.9 1.1 %project.1 = (bf16[2,16,3328]{2,1,0:T(8,128)(2,1)S(1)}, bf16[2,16,3328]{2,1,0:T(8,128)(2,1)S(1)}, bf16[2,16,3328]{2,1,0:T(8,128)(2,1)S(1)}, bf16[2,16,3328]{2,1,0:T(8,128)(2,1)S(1)}) custom-call(bf16[128,1024]{1,0:T(8,128)(2,1)S(1)} %get-tuple-element.28.values_ref, bf16[1024,7168]{1,0:T(8,128)(2,1)S(1)} %bring.1.proj_ref), custom_call_target="tpu_custom_call" | custom-call | flops 872415232 | bytes 6815744 | tf_op jit(solution)/shard_map/project/pallas_call | solution.py:312
  33.0 0.9 %collective-permute-start.7 = (bf16[2,16,3328]{2,1,0:T(8,128)(2,1)S(1)}, bf16[2,16,3328]{2,1,0:T(8,128)(2,1)S(1)}, u32[]{:S(2)}, u32[]{:S(2)}) collective-permute-start(bf16[2,16,3328]{2,1,0:T(8,128)(2,1)S(1)} %get-tuple-element.30), channel_id=1, source_target_pairs={{0,1},{1,2},{2,3},{3,0},{4,5},{5,6},{6,7},{7,4},{8,9},{9,10},{10,1... | collective-permute-start | bytes 638984 | tf_op jit(solution)/shard_map/ppermute | solution.py:412
  33.9 3.3 %collective-permute-start.8 = (bf16[2,16,3328]{2,1,0:T(8,128)(2,1)S(1)}, bf16[2,16,3328]{2,1,0:T(8,128)(2,1)S(1)}, u32[]{:S(2)}, u32[]{:S(2)}) collective-permute-start(bf16[2,16,3328]{2,1,0:T(8,128)(2,1)S(1)} %get-tuple-element.31), channel_id=1, source_target_pairs={{0,2},{1,3},{2,0},{3,1},{4,6},{5,7},{6,4},{7,5},{8,10},{9,11},{10,... | collective-permute-start | bytes 638984 | tf_op jit(solution)/shard_map/ppermute | solution.py:412
  37.2 0.0 collective-permute-start.9
  37.2 6.1 %collective-permute-done.11.came_ref = bf16[4,16,3840]{2,1,0:T(8,128)(2,1)S(1)} collective-permute-done((bf16[4,16,3840]{2,1,0:T(8,128)(2,1)S(1)}, bf16[4,16,3840]{2,1,0:T(8,128)(2,1)S(1)}, u32[]{:S(2)}, u32[]{:S(2)}) %collective-permute-start.11) | collective-permute-done | bytes 491552 | tf_op jit(solution)/shard_map/ppermute | solution.py:412
  43.3 0.1 add_far.1
  43.4 1.2 %collective-permute-start.12 = (bf16[16,3840]{1,0:T(8,128)(2,1)S(1)}, bf16[16,3840]{1,0:T(8,128)(2,1)S(1)}, u32[]{:S(2)}, u32[]{:S(2)}) collective-permute-start(bf16[16,3840]{1,0:T(8,128)(2,1)S(1)} %get-tuple-element.35), channel_id=1, source_target_pairs={{0,1},{1,2},{2,3},{3,0},{4,5},{5,6},{6,7},{7,4},{8,9},{9,10},{10,1... | collective-permute-start | bytes 368648 | tf_op jit(solution)/shard_map/ppermute | solution.py:412
  44.6 3.4 %collective-permute-start.13 = (bf16[16,3840]{1,0:T(8,128)(2,1)S(1)}, bf16[16,3840]{1,0:T(8,128)(2,1)S(1)}, u32[]{:S(2)}, u32[]{:S(2)}) collective-permute-start(bf16[16,3840]{1,0:T(8,128)(2,1)S(1)} %get-tuple-element.36), channel_id=1, source_target_pairs={{0,2},{1,3},{2,0},{3,1},{4,6},{5,7},{6,4},{7,5},{8,10},{9,11},{10,... | collective-permute-start | bytes 368648 | tf_op jit(solution)/shard_map/ppermute | solution.py:412
  48.0 0.0 collective-permute-done.7.refs_1_.near_refs_1_
  48.0 1.6 %collective-permute-start.14 = (bf16[16,3840]{1,0:T(8,128)(2,1)S(1)}, bf16[16,3840]{1,0:T(8,128)(2,1)S(1)}, u32[]{:S(2)}, u32[]{:S(2)}) collective-permute-start(bf16[16,3840]{1,0:T(8,128)(2,1)S(1)} %get-tuple-element.37), channel_id=1, source_target_pairs={{0,3},{1,0},{2,1},{3,2},{4,7},{5,4},{6,5},{7,6},{8,11},{9,8},{10,9... | collective-permute-start | bytes 368648 | tf_op jit(solution)/shard_map/ppermute | solution.py:412
  49.7 0.0 collective-permute-done.8.refs_2_.near_refs_2_
  49.7 0.0 collective-permute-done.9.refs_3_.near_refs_3_
  49.7 0.1 add_near.1
  49.7 0.8 %collective-permute-start.10 = (bf16[16,3328]{1,0:T(8,128)(2,1)S(1)}, bf16[16,3328]{1,0:T(8,128)(2,1)S(1)}, u32[]{:S(2)}, u32[]{:S(2)}) collective-permute-start(bf16[16,3328]{1,0:T(8,128)(2,1)S(1)} %add_near.1), channel_id=1, source_target_pairs={{0,68},{1,69},{2,70},{3,71},{4,64},{5,65},{6,66},{7,67},{8,76},{9,... | collective-permute-start | bytes 319496 | tf_op jit(solution)/shard_map/ppermute | solution.py:412
  50.5 0.0 copy-done.2
  50.6 5.2 %collective-permute-done.10.far_ref = bf16[16,3328]{1,0:T(8,128)(2,1)S(1)} collective-permute-done((bf16[16,3328]{1,0:T(8,128)(2,1)S(1)}, bf16[16,3328]{1,0:T(8,128)(2,1)S(1)}, u32[]{:S(2)}, u32[]{:S(2)}) %collective-permute-start.10) | collective-permute-done | bytes 106528 | tf_op jit(solution)/shard_map/ppermute | solution.py:412
  55.7 0.0 collective-permute-done.12.step_refs_0_
  55.7 0.0 collective-permute-done.13.step_refs_1_
  55.7 0.0 collective-permute-done.14.step_refs_2_
  55.7 0.0 copy-done.1
  55.7 1.0 %finish.1 = (bf16[16,7168]{1,0:T(8,128)(2,1)}, bf16[16,7168]{1,0:T(8,128)(2,1)}) custom-call(bf16[2,16,3328]{2,1,0:T(8,128)(2,1)S(1)} %get-tuple-element.29.refs_0_.near_refs_0_, bf16[2,16,3328]{2,1,0:T(8,128)(2,1)S(1)} %collective-permute-done.7.refs_1_.near_refs_1_, bf16[2,16,3328]{2,1,0:T(8,128)(2,1)S(1)} %collective-permute-done.8.refs_2_.near_refs_2_, ...), custom_call_target="tpu_custom_call" | custom-call | tf_op jit(solution)/shard_map/finish/pallas_call | solution.py:392
  (1 shorter events, 0.0 us)
Async XLA Ops:
  5.2 10.4 %collective-permute-start = (bf16[128,512]{1,0:T(8,128)(2,1)S(1)}, bf16[128,512]{1,0:T(8,128)(2,1)S(1)}, u32[]{:S(2)}, u32[]{:S(2)}) collective-permute-start(bf16[128,512]{1,0:T(8,128)(2,1)S(1)} %get-tuple-element.21), channel_id=1, source_target_pairs={{0,1},{1,2},{2,3},{3,0},{4,5},{5,6},{6,7},{7,4},{8,9},{9,10},{10,1... | collective-permute-start | bytes 393224 | tf_op jit(solution)/shard_map/ppermute | solution.py:412
  7.3 11.2 %collective-permute-start.1 = (bf16[128,512]{1,0:T(8,128)(2,1)S(1)}, bf16[128,512]{1,0:T(8,128)(2,1)S(1)}, u32[]{:S(2)}, u32[]{:S(2)}) collective-permute-start(bf16[128,512]{1,0:T(8,128)(2,1)S(1)} %get-tuple-element.22), channel_id=1, source_target_pairs={{0,2},{1,3},{2,0},{3,1},{4,6},{5,7},{6,4},{7,5},{8,10},{9,11},{10,... | collective-permute-start | bytes 393224 | tf_op jit(solution)/shard_map/ppermute | solution.py:412
  10.8 15.1 %collective-permute-start.2 = (bf16[128,512]{1,0:T(8,128)(2,1)S(1)}, bf16[128,512]{1,0:T(8,128)(2,1)S(1)}, u32[]{:S(2)}, u32[]{:S(2)}) collective-permute-start(bf16[128,512]{1,0:T(8,128)(2,1)S(1)} %get-tuple-element.23), channel_id=1, source_target_pairs={{0,3},{1,0},{2,1},{3,2},{4,7},{5,4},{6,5},{7,6},{8,11},{9,8},{10,9... | collective-permute-start | bytes 393224 | tf_op jit(solution)/shard_map/ppermute | solution.py:412
  11.9 14.1 %collective-permute-start.3 = (bf16[128,512]{1,0:T(8,128)(2,1)S(1)}, bf16[128,512]{1,0:T(8,128)(2,1)S(1)}, u32[]{:S(2)}, u32[]{:S(2)}) collective-permute-start(bf16[128,512]{1,0:T(8,128)(2,1)S(1)} %get-tuple-element.24), channel_id=1, source_target_pairs={{0,68},{1,69},{2,70},{3,71},{4,64},{5,65},{6,66},{7,67},{8,76},{9,... | collective-permute-start | bytes 393224 | tf_op jit(solution)/shard_map/ppermute | solution.py:412
  14.9 11.1 %collective-permute-start.4 = (bf16[128,512]{1,0:T(8,128)(2,1)S(1)}, bf16[128,512]{1,0:T(8,128)(2,1)S(1)}, u32[]{:S(2)}, u32[]{:S(2)}) collective-permute-start(bf16[128,512]{1,0:T(8,128)(2,1)S(1)} %get-tuple-element.25), channel_id=1, source_target_pairs={{0,69},{1,70},{2,71},{3,68},{4,65},{5,66},{6,67},{7,64},{8,77},{9,... | collective-permute-start | bytes 393224 | tf_op jit(solution)/shard_map/ppermute | solution.py:412
  15.6 10.5 %collective-permute-start.5 = (bf16[128,512]{1,0:T(8,128)(2,1)S(1)}, bf16[128,512]{1,0:T(8,128)(2,1)S(1)}, u32[]{:S(2)}, u32[]{:S(2)}) collective-permute-start(bf16[128,512]{1,0:T(8,128)(2,1)S(1)} %get-tuple-element.26), channel_id=1, source_target_pairs={{0,70},{1,71},{2,68},{3,69},{4,66},{5,67},{6,64},{7,65},{8,78},{9,... | collective-permute-start | bytes 393224 | tf_op jit(solution)/shard_map/ppermute | solution.py:412
  18.5 9.0 %collective-permute-start.6 = (bf16[128,512]{1,0:T(8,128)(2,1)S(1)}, bf16[128,512]{1,0:T(8,128)(2,1)S(1)}, u32[]{:S(2)}, u32[]{:S(2)}) collective-permute-start(bf16[128,512]{1,0:T(8,128)(2,1)S(1)} %get-tuple-element.27), channel_id=1, source_target_pairs={{0,71},{1,68},{2,69},{3,70},{4,67},{5,64},{6,65},{7,66},{8,79},{9,... | collective-permute-start | bytes 393224 | tf_op jit(solution)/shard_map/ppermute | solution.py:412
  20.7 6.8 %copy-start = (bf16[8,512,128]{2,1,0:T(8,128)(2,1)S(1)}, bf16[8,512,128]{2,1,0:T(8,128)(2,1)}, u32[]{:S(2)}) copy-start(bf16[8,512,128]{2,1,0:T(8,128)(2,1)} %value_up_ref.1) | copy-start | bytes 3145732
  26.0 24.6 %copy-start.2 = (bf16[7168]{0:T(1024)(128)(2,1)S(1)}, bf16[7168]{0:T(1024)(128)(2,1)}, u32[]{:S(2)}) copy-start(bf16[7168]{0:T(1024)(128)(2,1)} %param.15) | copy-start | bytes 43012
  26.0 29.8 %copy-start.1 = (bf16[16,7168]{1,0:T(8,128)(2,1)S(1)}, bf16[16,7168]{1,0:T(8,128)(2,1)}, u32[]{:S(2)}) copy-start(bf16[16,7168]{1,0:T(8,128)(2,1)} %residual_ref.1) | copy-start | bytes 688132
  29.3 14.0 %collective-permute-start.11 = (bf16[4,16,3840]{2,1,0:T(8,128)(2,1)S(1)}, bf16[4,16,3840]{2,1,0:T(8,128)(2,1)S(1)}, u32[]{:S(2)}, u32[]{:S(2)}) collective-permute-start(bf16[4,16,3840]{2,1,0:T(8,128)(2,1)S(1)} %get-tuple-element.34), channel_id=1, source_target_pairs={{0,68},{1,69},{2,70},{3,71},{4,64},{5,65},{6,66},{7,67},{8,76},{9,... | collective-permute-start | bytes 1474568 | tf_op jit(solution)/shard_map/ppermute | solution.py:412
  33.0 15.1 %collective-permute-start.7 = (bf16[2,16,3328]{2,1,0:T(8,128)(2,1)S(1)}, bf16[2,16,3328]{2,1,0:T(8,128)(2,1)S(1)}, u32[]{:S(2)}, u32[]{:S(2)}) collective-permute-start(bf16[2,16,3328]{2,1,0:T(8,128)(2,1)S(1)} %get-tuple-element.30), channel_id=1, source_target_pairs={{0,1},{1,2},{2,3},{3,0},{4,5},{5,6},{6,7},{7,4},{8,9},{9,10},{10,1... | collective-permute-start | bytes 638984 | tf_op jit(solution)/shard_map/ppermute | solution.py:412
  33.9 15.8 %collective-permute-start.8 = (bf16[2,16,3328]{2,1,0:T(8,128)(2,1)S(1)}, bf16[2,16,3328]{2,1,0:T(8,128)(2,1)S(1)}, u32[]{:S(2)}, u32[]{:S(2)}) collective-permute-start(bf16[2,16,3328]{2,1,0:T(8,128)(2,1)S(1)} %get-tuple-element.31), channel_id=1, source_target_pairs={{0,2},{1,3},{2,0},{3,1},{4,6},{5,7},{6,4},{7,5},{8,10},{9,11},{10,... | collective-permute-start | bytes 638984 | tf_op jit(solution)/shard_map/ppermute | solution.py:412
  37.2 12.5 %collective-permute-start.9 = (bf16[2,16,3328]{2,1,0:T(8,128)(2,1)S(1)}, bf16[2,16,3328]{2,1,0:T(8,128)(2,1)S(1)}, u32[]{:S(2)}, u32[]{:S(2)}) collective-permute-start(bf16[2,16,3328]{2,1,0:T(8,128)(2,1)S(1)} %get-tuple-element.32), channel_id=1, source_target_pairs={{0,3},{1,0},{2,1},{3,2},{4,7},{5,4},{6,5},{7,6},{8,11},{9,8},{10,9... | collective-permute-start | bytes 638984 | tf_op jit(solution)/shard_map/ppermute | solution.py:412
  43.4 12.3 %collective-permute-start.12 = (bf16[16,3840]{1,0:T(8,128)(2,1)S(1)}, bf16[16,3840]{1,0:T(8,128)(2,1)S(1)}, u32[]{:S(2)}, u32[]{:S(2)}) collective-permute-start(bf16[16,3840]{1,0:T(8,128)(2,1)S(1)} %get-tuple-element.35), channel_id=1, source_target_pairs={{0,1},{1,2},{2,3},{3,0},{4,5},{5,6},{6,7},{7,4},{8,9},{9,10},{10,1... | collective-permute-start | bytes 368648 | tf_op jit(solution)/shard_map/ppermute | solution.py:412
  44.6 11.1 %collective-permute-start.13 = (bf16[16,3840]{1,0:T(8,128)(2,1)S(1)}, bf16[16,3840]{1,0:T(8,128)(2,1)S(1)}, u32[]{:S(2)}, u32[]{:S(2)}) collective-permute-start(bf16[16,3840]{1,0:T(8,128)(2,1)S(1)} %get-tuple-element.36), channel_id=1, source_target_pairs={{0,2},{1,3},{2,0},{3,1},{4,6},{5,7},{6,4},{7,5},{8,10},{9,11},{10,... | collective-permute-start | bytes 368648 | tf_op jit(solution)/shard_map/ppermute | solution.py:412
  48.0 7.7 %collective-permute-start.14 = (bf16[16,3840]{1,0:T(8,128)(2,1)S(1)}, bf16[16,3840]{1,0:T(8,128)(2,1)S(1)}, u32[]{:S(2)}, u32[]{:S(2)}) collective-permute-start(bf16[16,3840]{1,0:T(8,128)(2,1)S(1)} %get-tuple-element.37), channel_id=1, source_target_pairs={{0,3},{1,0},{2,1},{3,2},{4,7},{5,4},{6,5},{7,6},{8,11},{9,8},{10,9... | collective-permute-start | bytes 368648 | tf_op jit(solution)/shard_map/ppermute | solution.py:412
  49.7 6.0 %collective-permute-start.10 = (bf16[16,3328]{1,0:T(8,128)(2,1)S(1)}, bf16[16,3328]{1,0:T(8,128)(2,1)S(1)}, u32[]{:S(2)}, u32[]{:S(2)}) collective-permute-start(bf16[16,3328]{1,0:T(8,128)(2,1)S(1)} %add_near.1), channel_id=1, source_target_pairs={{0,68},{1,69},{2,70},{3,71},{4,64},{5,65},{6,66},{7,67},{8,76},{9,... | collective-permute-start | bytes 319496 | tf_op jit(solution)/shard_map/ppermute | solution.py:412

commit v2 on v1

--- a/solution.py
+++ b/solution.py
@@ -9,6 +9,7 @@
 GROUP_ROWS = 4
 PROJ_STEP = 1024
 LEFT_COLUMNS = 3328
+ORDER = (6, 5, 7, 4, 2, 1, 3)
 score_scale = 192.0 ** (-0.5)
 norm_eps = 1e-06
 MIB = 1024 * 1024
@@ -241,7 +242,7 @@
     z_size = owners // 2
 
     size = rows_here * owned
-    for place, latent_ref in enumerate(latent_refs):
+    for place, latent_ref in zip((0,) + ORDER, latent_refs):
         far, step = place // z_size, place % z_size
         back = (far * z_size + (z_size - step) % z_size) * size
         for c in range(lat // 128):
@@ -422,7 +423,7 @@
     latents = attend(queries, latent_cache, new_latent, lengths, owners)
     owned_latents = [latents[0]] + [
         send(latents[place], place // z_size, place % z_size, mesh_shape)
-        for place in range(1, owners)
+        for place in ORDER
     ]
     proj_near = bring(output_proj, latents[0])
     values, own, across = make_values(owned_latents, value_up, proj_near, owners, rows_here)

time: 57.7 us -> 56.5 us (0.979)
  the two profiles are of different devices: /device:TPU:0 before, /device:TPU:4 now
where the time goes in v2:
time: 56.5 us; the launch traced here: 56 us
  starting transfers between devices  25.6 us (45%)
  waiting for transfers between devices  15.7 us (28%)
  Pallas kernels  13.9 us (25%)
  between operations  0.74 us (1%)
    ppermute x15, starting transfers between devices, send(): return lax.ppermute(array, ('rep', 'dp'), pairs)  25.6 us
    ppermute x15, waiting for transfers between devices, send(): return lax.ppermute(array, ('rep', 'dp'), pairs)  15.7 us
    pallas_call x1, Pallas kernels, bring(): pl.pallas_call(bring_kernel, out_shape=pltpu.VMEM(output_proj.shape, jnp....  5.27 us
    pallas_call x1, Pallas kernels, attend(): pl.pallas_call(attend_kernel, out_shape=[jax.ShapeDtypeStruct((row_count...  4.56 us
    pallas_call x1, Pallas kernels, make_values(): pl.pallas_call(values_kernel, out_shape=(jax.ShapeDtypeStruct((rows, owne...  1.82 us
  transfers between devices with their start and end apart: 15, of which 5 were waited for; matrix products, arithmetic and copies ran while one was open for 0% of the time, Pallas kernels for 12%

profile of v2, /device:TPU:4, one launch (start us, length us, event | category | flops | bytes accessed | tf_op | source)
XLA Modules:
  0.0 56.0 jit_solution(7360255063939018438)
XLA Ops:
  0.6 4.6 %attend.1 = (bf16[128,512]{1,0:T(8,128)(2,1)S(1)}, bf16[128,512]{1,0:T(8,128)(2,1)S(1)}, bf16[128,512]{1,0:T(8,128)(2,1)S(1)}, bf16[128,512]{1,0:T(8,128)(2,1)S(...) custom-call(s32[128]{0:T(128)} %lengths_hbm.1, ...), custom_call_target="tpu_custom_call" | custom-call | flops 1207959552 | bytes 9437184 | tf_op jit(solution)/shard_map/attend/pallas_call | solution.py:187
  5.2 6.4 %collective-permute-start = (bf16[128,512]{1,0:T(8,128)(2,1)S(1)}, bf16[128,512]{1,0:T(8,128)(2,1)S(1)}, u32[]{:S(2)}, u32[]{:S(2)}) collective-permute-start(bf16[128,512]{1,0:T(8,128)(2,1)S(1)} %get-tuple-element.21), channel_id=1, source_target_pairs={{0,70},{1,71},{2,68},{3,69},{4,66},{5,67},{6,64},{7,65},{8,78},{9,... | collective-permute-start | bytes 393224 | tf_op jit(solution)/shard_map/ppermute | solution.py:413
  11.6 0.7 %collective-permute-start.1 = (bf16[128,512]{1,0:T(8,128)(2,1)S(1)}, bf16[128,512]{1,0:T(8,128)(2,1)S(1)}, u32[]{:S(2)}, u32[]{:S(2)}) collective-permute-start(bf16[128,512]{1,0:T(8,128)(2,1)S(1)} %get-tuple-element.22), channel_id=1, source_target_pairs={{0,69},{1,70},{2,71},{3,68},{4,65},{5,66},{6,67},{7,64},{8,77},{9,... | collective-permute-start | bytes 393224 | tf_op jit(solution)/shard_map/ppermute | solution.py:413
  12.3 4.7 %collective-permute-start.2 = (bf16[128,512]{1,0:T(8,128)(2,1)S(1)}, bf16[128,512]{1,0:T(8,128)(2,1)S(1)}, u32[]{:S(2)}, u32[]{:S(2)}) collective-permute-start(bf16[128,512]{1,0:T(8,128)(2,1)S(1)} %get-tuple-element.23), channel_id=1, source_target_pairs={{0,71},{1,68},{2,69},{3,70},{4,67},{5,64},{6,65},{7,66},{8,79},{9,... | collective-permute-start | bytes 393224 | tf_op jit(solution)/shard_map/ppermute | solution.py:413
  16.9 0.2 collective-permute-start.3
  17.2 0.2 collective-permute-start.4
  17.4 0.0 collective-permute-done.latent_refs_1_
  17.4 1.0 %collective-permute-start.5 = (bf16[128,512]{1,0:T(8,128)(2,1)S(1)}, bf16[128,512]{1,0:T(8,128)(2,1)S(1)}, u32[]{:S(2)}, u32[]{:S(2)}) collective-permute-start(bf16[128,512]{1,0:T(8,128)(2,1)S(1)} %get-tuple-element.26), channel_id=1, source_target_pairs={{0,1},{1,2},{2,3},{3,0},{4,5},{5,6},{6,7},{7,4},{8,9},{9,10},{10,1... | collective-permute-start | bytes 393224 | tf_op jit(solution)/shard_map/ppermute | solution.py:413
  18.4 2.6 %collective-permute-done.1.latent_refs_2_ = bf16[128,512]{1,0:T(8,128)(2,1)S(1)} collective-permute-done((bf16[128,512]{1,0:T(8,128)(2,1)S(1)}, bf16[128,512]{1,0:T(8,128)(2,1)S(1)}, u32[]{:S(2)}, u32[]{:S(2)}) %collective-permute-start.1) | collective-permute-done | bytes 131104 | tf_op jit(solution)/shard_map/ppermute | solution.py:413
  20.9 0.0 collective-permute-start.6
  20.9 0.0 copy-start
  20.9 5.3 %bring.1.proj_ref = bf16[1024,7168]{1,0:T(8,128)(2,1)S(1)} custom-call(bf16[128,512]{1,0:T(8,128)(2,1)S(1)} %get-tuple-element.20.after_hbm.latent_refs_0_, bf16[1024,7168]{1,0:T(8,128)(2,1)} %proj_hbm.1), custom_call_target="tpu_custom_call" | custom-call | bytes 14680064 | tf_op jit(solution)/shard_map/bring/pallas_call | solution.py:224
  26.2 0.0 copy-start.2
  26.2 0.0 copy-start.1
  26.3 0.0 collective-permute-done.2.latent_refs_3_
  26.3 0.0 collective-permute-done.3.latent_refs_4_
  26.3 0.0 collective-permute-done.4.latent_refs_5_
  26.3 0.5 collective-permute-done.5.latent_refs_6_
  26.8 1.3 %collective-permute-done.6.latent_refs_7_ = bf16[128,512]{1,0:T(8,128)(2,1)S(1)} collective-permute-done((bf16[128,512]{1,0:T(8,128)(2,1)S(1)}, bf16[128,512]{1,0:T(8,128)(2,1)S(1)}, u32[]{:S(2)}, u32[]{:S(2)}) %collective-permute-start.6) | collective-permute-done | bytes 131104 | tf_op jit(solution)/shard_map/ppermute | solution.py:413
  28.0 0.0 copy-done
  28.0 1.8 %values.1 = (bf16[128,1024]{1,0:T(8,128)(2,1)S(1)}, bf16[4,16,3840]{2,1,0:T(8,128)(2,1)S(1)}, bf16[4,16,3840]{2,1,0:T(8,128)(2,1)S(1)}) custom-call(bf16[128,512]{1,0:T(8,128)(2,1)S(1)} %get-tuple-element.20.after_hbm.latent_refs_0_, bf16[128,512]{1,0:T(8,128)(2,1)S(1)} %collective-permute-done.latent_refs_1_, ...), custom_call_target="tpu_custom_call" | custom-call | flops 1006632960 | bytes 7864320 | tf_op jit(solution)/shard_map/values/pallas_call | solution.py:279
  29.9 1.9 %collective-permute-start.11 = (bf16[4,16,3840]{2,1,0:T(8,128)(2,1)S(1)}, bf16[4,16,3840]{2,1,0:T(8,128)(2,1)S(1)}, u32[]{:S(2)}, u32[]{:S(2)}) collective-permute-start(bf16[4,16,3840]{2,1,0:T(8,128)(2,1)S(1)} %get-tuple-element.34), channel_id=1, source_target_pairs={{0,68},{1,69},{2,70},{3,71},{4,64},{5,65},{6,66},{7,67},{8,76},{9,... | collective-permute-start | bytes 1474568 | tf_op jit(solution)/shard_map/ppermute | solution.py:413
  31.8 1.1 %project.1 = (bf16[2,16,3328]{2,1,0:T(8,128)(2,1)S(1)}, bf16[2,16,3328]{2,1,0:T(8,128)(2,1)S(1)}, bf16[2,16,3328]{2,1,0:T(8,128)(2,1)S(1)}, bf16[2,16,3328]{2,1,0:T(8,128)(2,1)S(1)}) custom-call(bf16[128,1024]{1,0:T(8,128)(2,1)S(1)} %get-tuple-element.28.values_ref, bf16[1024,7168]{1,0:T(8,128)(2,1)S(1)} %bring.1.proj_ref), custom_call_target="tpu_custom_call" | custom-call | flops 872415232 | bytes 6815744 | tf_op jit(solution)/shard_map/project/pallas_call | solution.py:313
  32.8 1.2 %collective-permute-start.7 = (bf16[2,16,3328]{2,1,0:T(8,128)(2,1)S(1)}, bf16[2,16,3328]{2,1,0:T(8,128)(2,1)S(1)}, u32[]{:S(2)}, u32[]{:S(2)}) collective-permute-start(bf16[2,16,3328]{2,1,0:T(8,128)(2,1)S(1)} %get-tuple-element.30), channel_id=1, source_target_pairs={{0,1},{1,2},{2,3},{3,0},{4,5},{5,6},{6,7},{7,4},{8,9},{9,10},{10,1... | collective-permute-start | bytes 638984 | tf_op jit(solution)/shard_map/ppermute | solution.py:413
  34.0 2.5 %collective-permute-start.8 = (bf16[2,16,3328]{2,1,0:T(8,128)(2,1)S(1)}, bf16[2,16,3328]{2,1,0:T(8,128)(2,1)S(1)}, u32[]{:S(2)}, u32[]{:S(2)}) collective-permute-start(bf16[2,16,3328]{2,1,0:T(8,128)(2,1)S(1)} %get-tuple-element.31), channel_id=1, source_target_pairs={{0,2},{1,3},{2,0},{3,1},{4,6},{5,7},{6,4},{7,5},{8,10},{9,11},{10,... | collective-permute-start | bytes 638984 | tf_op jit(solution)/shard_map/ppermute | solution.py:413
  36.5 0.5 collective-permute-start.9
  37.0 7.4 %collective-permute-done.11.came_ref = bf16[4,16,3840]{2,1,0:T(8,128)(2,1)S(1)} collective-permute-done((bf16[4,16,3840]{2,1,0:T(8,128)(2,1)S(1)}, bf16[4,16,3840]{2,1,0:T(8,128)(2,1)S(1)}, u32[]{:S(2)}, u32[]{:S(2)}) %collective-permute-start.11) | collective-permute-done | bytes 491552 | tf_op jit(solution)/shard_map/ppermute | solution.py:413
  44.4 0.1 add_far.1
  44.5 0.9 %collective-permute-start.12 = (bf16[16,3840]{1,0:T(8,128)(2,1)S(1)}, bf16[16,3840]{1,0:T(8,128)(2,1)S(1)}, u32[]{:S(2)}, u32[]{:S(2)}) collective-permute-start(bf16[16,3840]{1,0:T(8,128)(2,1)S(1)} %get-tuple-element.35), channel_id=1, source_target_pairs={{0,1},{1,2},{2,3},{3,0},{4,5},{5,6},{6,7},{7,4},{8,9},{9,10},{10,1... | collective-permute-start | bytes 368648 | tf_op jit(solution)/shard_map/ppermute | solution.py:413
  45.4 3.3 %collective-permute-start.13 = (bf16[16,3840]{1,0:T(8,128)(2,1)S(1)}, bf16[16,3840]{1,0:T(8,128)(2,1)S(1)}, u32[]{:S(2)}, u32[]{:S(2)}) collective-permute-start(bf16[16,3840]{1,0:T(8,128)(2,1)S(1)} %get-tuple-element.36), channel_id=1, source_target_pairs={{0,2},{1,3},{2,0},{3,1},{4,6},{5,7},{6,4},{7,5},{8,10},{9,11},{10,... | collective-permute-start | bytes 368648 | tf_op jit(solution)/shard_map/ppermute | solution.py:413
  48.6 0.0 collective-permute-done.7.refs_1_.near_refs_1_
  48.6 0.3 collective-permute-start.14
  48.9 0.0 collective-permute-done.8.refs_2_.near_refs_2_
  48.9 0.0 collective-permute-done.9.refs_3_.near_refs_3_
  48.9 0.1 add_near.1
  49.0 2.0 %collective-permute-start.10 = (bf16[16,3328]{1,0:T(8,128)(2,1)S(1)}, bf16[16,3328]{1,0:T(8,128)(2,1)S(1)}, u32[]{:S(2)}, u32[]{:S(2)}) collective-permute-start(bf16[16,3328]{1,0:T(8,128)(2,1)S(1)} %add_near.1), channel_id=1, source_target_pairs={{0,68},{1,69},{2,70},{3,71},{4,64},{5,65},{6,66},{7,67},{8,76},{9,... | collective-permute-start | bytes 319496 | tf_op jit(solution)/shard_map/ppermute | solution.py:413
  51.0 0.0 copy-done.2
  51.0 4.0 %collective-permute-done.10.far_ref = bf16[16,3328]{1,0:T(8,128)(2,1)S(1)} collective-permute-done((bf16[16,3328]{1,0:T(8,128)(2,1)S(1)}, bf16[16,3328]{1,0:T(8,128)(2,1)S(1)}, u32[]{:S(2)}, u32[]{:S(2)}) %collective-permute-start.10) | collective-permute-done | bytes 106528 | tf_op jit(solution)/shard_map/ppermute | solution.py:413
  55.0 0.0 collective-permute-done.12.step_refs_0_
  55.0 0.0 collective-permute-done.13.step_refs_1_
  55.0 0.0 collective-permute-done.14.step_refs_2_
  55.0 0.0 copy-done.1
  55.0 1.0 %finish.1 = (bf16[16,7168]{1,0:T(8,128)(2,1)}, bf16[16,7168]{1,0:T(8,128)(2,1)}) custom-call(bf16[2,16,3328]{2,1,0:T(8,128)(2,1)S(1)} %get-tuple-element.29.refs_0_.near_refs_0_, bf16[2,16,3328]{2,1,0:T(8,128)(2,1)S(1)} %collective-permute-done.7.refs_1_.near_refs_1_, bf16[2,16,3328]{2,1,0:T(8,128)(2,1)S(1)} %collective-permute-done.8.refs_2_.near_refs_2_, ...), custom_call_target="tpu_custom_call" | custom-call | tf_op jit(solution)/shard_map/finish/pallas_call | solution.py:393
  (1 shorter events, 0.0 us)
Async XLA Ops:
  5.2 12.2 %collective-permute-start = (bf16[128,512]{1,0:T(8,128)(2,1)S(1)}, bf16[128,512]{1,0:T(8,128)(2,1)S(1)}, u32[]{:S(2)}, u32[]{:S(2)}) collective-permute-start(bf16[128,512]{1,0:T(8,128)(2,1)S(1)} %get-tuple-element.21), channel_id=1, source_target_pairs={{0,70},{1,71},{2,68},{3,69},{4,66},{5,67},{6,64},{7,65},{8,78},{9,... | collective-permute-start | bytes 393224 | tf_op jit(solution)/shard_map/ppermute | solution.py:413
  11.6 9.3 %collective-permute-start.1 = (bf16[128,512]{1,0:T(8,128)(2,1)S(1)}, bf16[128,512]{1,0:T(8,128)(2,1)S(1)}, u32[]{:S(2)}, u32[]{:S(2)}) collective-permute-start(bf16[128,512]{1,0:T(8,128)(2,1)S(1)} %get-tuple-element.22), channel_id=1, source_target_pairs={{0,69},{1,70},{2,71},{3,68},{4,65},{5,66},{6,67},{7,64},{8,77},{9,... | collective-permute-start | bytes 393224 | tf_op jit(solution)/shard_map/ppermute | solution.py:413
  12.3 14.0 %collective-permute-start.2 = (bf16[128,512]{1,0:T(8,128)(2,1)S(1)}, bf16[128,512]{1,0:T(8,128)(2,1)S(1)}, u32[]{:S(2)}, u32[]{:S(2)}) collective-permute-start(bf16[128,512]{1,0:T(8,128)(2,1)S(1)} %get-tuple-element.23), channel_id=1, source_target_pairs={{0,71},{1,68},{2,69},{3,70},{4,67},{5,64},{6,65},{7,66},{8,79},{9,... | collective-permute-start | bytes 393224 | tf_op jit(solution)/shard_map/ppermute | solution.py:413
  16.9 9.3 %collective-permute-start.3 = (bf16[128,512]{1,0:T(8,128)(2,1)S(1)}, bf16[128,512]{1,0:T(8,128)(2,1)S(1)}, u32[]{:S(2)}, u32[]{:S(2)}) collective-permute-start(bf16[128,512]{1,0:T(8,128)(2,1)S(1)} %get-tuple-element.24), channel_id=1, source_target_pairs={{0,68},{1,69},{2,70},{3,71},{4,64},{5,65},{6,66},{7,67},{8,76},{9,... | collective-permute-start | bytes 393224 | tf_op jit(solution)/shard_map/ppermute | solution.py:413
  17.2 9.1 %collective-permute-start.4 = (bf16[128,512]{1,0:T(8,128)(2,1)S(1)}, bf16[128,512]{1,0:T(8,128)(2,1)S(1)}, u32[]{:S(2)}, u32[]{:S(2)}) collective-permute-start(bf16[128,512]{1,0:T(8,128)(2,1)S(1)} %get-tuple-element.25), channel_id=1, source_target_pairs={{0,2},{1,3},{2,0},{3,1},{4,6},{5,7},{6,4},{7,5},{8,10},{9,11},{10,... | collective-permute-start | bytes 393224 | tf_op jit(solution)/shard_map/ppermute | solution.py:413
  17.4 9.4 %collective-permute-start.5 = (bf16[128,512]{1,0:T(8,128)(2,1)S(1)}, bf16[128,512]{1,0:T(8,128)(2,1)S(1)}, u32[]{:S(2)}, u32[]{:S(2)}) collective-permute-start(bf16[128,512]{1,0:T(8,128)(2,1)S(1)} %get-tuple-element.26), channel_id=1, source_target_pairs={{0,1},{1,2},{2,3},{3,0},{4,5},{5,6},{6,7},{7,4},{8,9},{9,10},{10,1... | collective-permute-start | bytes 393224 | tf_op jit(solution)/shard_map/ppermute | solution.py:413
  20.9 7.1 %collective-permute-start.6 = (bf16[128,512]{1,0:T(8,128)(2,1)S(1)}, bf16[128,512]{1,0:T(8,128)(2,1)S(1)}, u32[]{:S(2)}, u32[]{:S(2)}) collective-permute-start(bf16[128,512]{1,0:T(8,128)(2,1)S(1)} %get-tuple-element.27), channel_id=1, source_target_pairs={{0,3},{1,0},{2,1},{3,2},{4,7},{5,4},{6,5},{7,6},{8,11},{9,8},{10,9... | collective-permute-start | bytes 393224 | tf_op jit(solution)/shard_map/ppermute | solution.py:413
  20.9 7.1 %copy-start = (bf16[8,512,128]{2,1,0:T(8,128)(2,1)S(1)}, bf16[8,512,128]{2,1,0:T(8,128)(2,1)}, u32[]{:S(2)}) copy-start(bf16[8,512,128]{2,1,0:T(8,128)(2,1)} %value_up_ref.1) | copy-start | bytes 3145732
  26.2 24.7 %copy-start.2 = (bf16[7168]{0:T(1024)(128)(2,1)S(1)}, bf16[7168]{0:T(1024)(128)(2,1)}, u32[]{:S(2)}) copy-start(bf16[7168]{0:T(1024)(128)(2,1)} %param.15) | copy-start | bytes 43012
  26.2 28.7 %copy-start.1 = (bf16[16,7168]{1,0:T(8,128)(2,1)S(1)}, bf16[16,7168]{1,0:T(8,128)(2,1)}, u32[]{:S(2)}) copy-start(bf16[16,7168]{1,0:T(8,128)(2,1)} %residual_ref.1) | copy-start | bytes 688132
  29.9 14.5 %collective-permute-start.11 = (bf16[4,16,3840]{2,1,0:T(8,128)(2,1)S(1)}, bf16[4,16,3840]{2,1,0:T(8,128)(2,1)S(1)}, u32[]{:S(2)}, u32[]{:S(2)}) collective-permute-start(bf16[4,16,3840]{2,1,0:T(8,128)(2,1)S(1)} %get-tuple-element.34), channel_id=1, source_target_pairs={{0,68},{1,69},{2,70},{3,71},{4,64},{5,65},{6,66},{7,67},{8,76},{9,... | collective-permute-start | bytes 1474568 | tf_op jit(solution)/shard_map/ppermute | solution.py:413
  32.8 15.8 %collective-permute-start.7 = (bf16[2,16,3328]{2,1,0:T(8,128)(2,1)S(1)}, bf16[2,16,3328]{2,1,0:T(8,128)(2,1)S(1)}, u32[]{:S(2)}, u32[]{:S(2)}) collective-permute-start(bf16[2,16,3328]{2,1,0:T(8,128)(2,1)S(1)} %get-tuple-element.30), channel_id=1, source_target_pairs={{0,1},{1,2},{2,3},{3,0},{4,5},{5,6},{6,7},{7,4},{8,9},{9,10},{10,1... | collective-permute-start | bytes 638984 | tf_op jit(solution)/shard_map/ppermute | solution.py:413
  34.0 14.9 %collective-permute-start.8 = (bf16[2,16,3328]{2,1,0:T(8,128)(2,1)S(1)}, bf16[2,16,3328]{2,1,0:T(8,128)(2,1)S(1)}, u32[]{:S(2)}, u32[]{:S(2)}) collective-permute-start(bf16[2,16,3328]{2,1,0:T(8,128)(2,1)S(1)} %get-tuple-element.31), channel_id=1, source_target_pairs={{0,2},{1,3},{2,0},{3,1},{4,6},{5,7},{6,4},{7,5},{8,10},{9,11},{10,... | collective-permute-start | bytes 638984 | tf_op jit(solution)/shard_map/ppermute | solution.py:413
  36.5 12.4 %collective-permute-start.9 = (bf16[2,16,3328]{2,1,0:T(8,128)(2,1)S(1)}, bf16[2,16,3328]{2,1,0:T(8,128)(2,1)S(1)}, u32[]{:S(2)}, u32[]{:S(2)}) collective-permute-start(bf16[2,16,3328]{2,1,0:T(8,128)(2,1)S(1)} %get-tuple-element.32), channel_id=1, source_target_pairs={{0,3},{1,0},{2,1},{3,2},{4,7},{5,4},{6,5},{7,6},{8,11},{9,8},{10,9... | collective-permute-start | bytes 638984 | tf_op jit(solution)/shard_map/ppermute | solution.py:413
  44.5 10.5 %collective-permute-start.12 = (bf16[16,3840]{1,0:T(8,128)(2,1)S(1)}, bf16[16,3840]{1,0:T(8,128)(2,1)S(1)}, u32[]{:S(2)}, u32[]{:S(2)}) collective-permute-start(bf16[16,3840]{1,0:T(8,128)(2,1)S(1)} %get-tuple-element.35), channel_id=1, source_target_pairs={{0,1},{1,2},{2,3},{3,0},{4,5},{5,6},{6,7},{7,4},{8,9},{9,10},{10,1... | collective-permute-start | bytes 368648 | tf_op jit(solution)/shard_map/ppermute | solution.py:413
  45.4 9.6 %collective-permute-start.13 = (bf16[16,3840]{1,0:T(8,128)(2,1)S(1)}, bf16[16,3840]{1,0:T(8,128)(2,1)S(1)}, u32[]{:S(2)}, u32[]{:S(2)}) collective-permute-start(bf16[16,3840]{1,0:T(8,128)(2,1)S(1)} %get-tuple-element.36), channel_id=1, source_target_pairs={{0,2},{1,3},{2,0},{3,1},{4,6},{5,7},{6,4},{7,5},{8,10},{9,11},{10,... | collective-permute-start | bytes 368648 | tf_op jit(solution)/shard_map/ppermute | solution.py:413
  48.6 6.3 %collective-permute-start.14 = (bf16[16,3840]{1,0:T(8,128)(2,1)S(1)}, bf16[16,3840]{1,0:T(8,128)(2,1)S(1)}, u32[]{:S(2)}, u32[]{:S(2)}) collective-permute-start(bf16[16,3840]{1,0:T(8,128)(2,1)S(1)} %get-tuple-element.37), channel_id=1, source_target_pairs={{0,3},{1,0},{2,1},{3,2},{4,7},{5,4},{6,5},{7,6},{8,11},{9,8},{10,9... | collective-permute-start | bytes 368648 | tf_op jit(solution)/shard_map/ppermute | solution.py:413
  49.0 6.0 %collective-permute-start.10 = (bf16[16,3328]{1,0:T(8,128)(2,1)S(1)}, bf16[16,3328]{1,0:T(8,128)(2,1)S(1)}, u32[]{:S(2)}, u32[]{:S(2)}) collective-permute-start(bf16[16,3328]{1,0:T(8,128)(2,1)S(1)} %add_near.1), channel_id=1, source_target_pairs={{0,68},{1,69},{2,70},{3,71},{4,64},{5,65},{6,66},{7,67},{8,76},{9,... | collective-permute-start | bytes 319496 | tf_op jit(solution)/shard_map/ppermute | solution.py:413

commit v3 on v2

--- a/solution.py
+++ b/solution.py
@@ -8,9 +8,9 @@
 LAT = 512
 GROUP_ROWS = 4
 PROJ_STEP = 1024
-LEFT_COLUMNS = 3328
+LEFT_COLUMNS = 3456
 ORDER = (6, 5, 7, 4, 2, 1, 3)
-score_scale = 192.0 ** (-0.5)
+exponent_scale = 192.0 ** (-0.5) * 1.4426950408889634
 norm_eps = 1e-06
 MIB = 1024 * 1024
 
@@ -18,158 +18,147 @@
 def attend_kernel(
     lengths_hbm, queries_hbm, latent_hbm, cache_hbm, *refs
 ):
-    *owner_refs, out_ref = refs[:-11]
+    *owner_refs, out_ref = refs[:-9]
     (
-        held, queries_ref, latent_ref, latent_wide, gathered_ref, softmax_ref,
-        lengths_ref, order, arrived_small, arrived_first, arrived_second,
-    ) = refs[-11:]
+        held, queries_ref, latent_ref, latent_wide,
+        lengths_ref, order, arrived_small, arrived_queries, arrived_keys,
+    ) = refs[-9:]
     row_count, width, span = held.shape
     owners, _, _ = out_ref.shape
     heads = queries_ref.shape[1]
     owned = heads // owners
     first_row = lax.axis_index("dp") * row_count
     pair_count = row_count // 2
-    group_count = row_count // GROUP_ROWS
     group_pairs = GROUP_ROWS // 2
+    group_count = pair_count // group_pairs
     short = span // 2
 
     lengths_copy = pltpu.make_async_copy(lengths_hbm, lengths_ref, arrived_small.at[0])
     latent_copy = pltpu.make_async_copy(latent_hbm, latent_ref, arrived_small.at[1])
 
-    def fetch_first(group):
-        rows, keys = pl.ds(group * GROUP_ROWS, GROUP_ROWS), pl.ds(0, short)
-        return (
-            pltpu.make_async_copy(
-                queries_hbm.at[rows], queries_ref.at[rows], arrived_first.at[0, group]
-            ),
-            pltpu.make_async_copy(
-                cache_hbm.at[rows, :, keys], held.at[rows, :, keys], arrived_first.at[1, group]
-            ),
+    def fetch_queries(pair):
+        rows = pl.ds(2 * pair, 2)
+        return pltpu.make_async_copy(
+            queries_hbm.at[rows], queries_ref.at[rows], arrived_queries.at[pair]
         )
 
-    def fetch_second(slot):
-        rows, keys = pl.ds(2 * order[slot], 2), pl.ds(short, short)
+    def fetch_keys(pair, keys):
+        rows = pl.ds(2 * pair, 2)
         return pltpu.make_async_copy(
-            cache_hbm.at[rows, :, keys], held.at[rows, :, keys], arrived_second.at[slot]
+            cache_hbm.at[rows, :, pl.ds(0, keys)],
+            held.at[rows, :, pl.ds(0, keys)],
+            arrived_keys.at[pair],
         )
 
-    def start_first(group):
-        for copy in fetch_first(group):
-            copy.start()
-
-    start_first(0)
+    for pair in range(group_pairs):
+        order[pair] = pair
+        fetch_queries(pair).start()
+        fetch_keys(pair, span).start()
     lengths_copy.start()
     latent_copy.start()
-    start_first(1)
-
     lengths_copy.wait()
     longest = [
         jnp.maximum(lengths_ref[first_row + 2 * pair], lengths_ref[first_row + 2 * pair + 1])
         for pair in range(pair_count)
     ]
     is_long = [(length > short).astype(jnp.int32) for length in longest]
-    long_slot, short_slot = 0, sum(is_long)
-    long_groups = (short_slot + group_pairs - 1) // group_pairs
-    for pair in range(pair_count):
+
+    short_slot = group_pairs
+    long_slot = pair_count - sum(is_long[group_pairs:])
+    first_is_long = sum(is_long[:group_pairs]) > 0
+    short_groups = long_slot // group_pairs
+    for pair in range(group_pairs, pair_count):
         order[jnp.where(is_long[pair] == 1, long_slot, short_slot)] = pair
         long_slot = long_slot + is_long[pair]
         short_slot = short_slot + 1 - is_long[pair]
+
+    def start(group):
+        for pair in [order[group * group_pairs + i] for i in range(group_pairs)]:
+            fetch_queries(pair).start()
+
+            @pl.when(group < short_groups)
+            def _():
+                fetch_keys(pair, short).start()
+
+            @pl.when(group >= short_groups)
+            def _():
+                fetch_keys(pair, span).start()
+
+    start(1)
     latent_copy.wait()
     latent_wide[...] = latent_ref[...].astype(jnp.float32)
 
-    def score(row, start):
+    def score(row, keys):
         scores = jnp.dot(
-            queries_ref[row],
-            held[row, :, start : start + short],
-            preferred_element_type=jnp.float32,
+            queries_ref[row], held[row, :, :keys], preferred_element_type=jnp.float32
         )
-        position = start + lax.broadcasted_iota(jnp.int32, scores.shape, 1)
-        return jnp.where(
-            position < lengths_ref[first_row + row], scores * score_scale, -jnp.inf
+        position = lax.broadcasted_iota(jnp.int32, scores.shape, 1)
+        return jnp.where(position < lengths_ref[first_row + row], scores, -jnp.inf)
+
+    def weigh(row, scores):
+        fresh = latent_wide[pl.ds(row, 1), :]
+        self_score = jnp.sum(
+            queries_ref[row].astype(jnp.float32) * fresh, axis=1, keepdims=True
         )
-
-    def gather(row, start, raised):
-        return lax.dot_general(
-            raised.astype(jnp.bfloat16),
-            held[row, :LAT, start : start + short],
+        row_max = jnp.maximum(jnp.max(scores, axis=1, keepdims=True), self_score)
+        raised = jnp.exp2((scores - row_max) * exponent_scale)
+        self_raised = jnp.exp2((self_score - row_max) * exponent_scale)
+        row_total = jnp.sum(raised, axis=1, keepdims=True) + self_raised
+        self_weight = self_raised.astype(jnp.bfloat16).astype(jnp.float32)
+        return raised.astype(jnp.bfloat16), self_weight, row_total
+
+    def gather(row, keys, weights, self_weight, row_total):
+        gathered = lax.dot_general(
+            weights,
+            held[row, :LAT, :keys],
             (((1,), (1,)), ((), ())),
             preferred_element_type=jnp.float32,
         )
-
-    def weigh_first(row, scores):
-        fresh = latent_wide[pl.ds(row, 1), :]
-        self_score = (
-            jnp.sum(queries_ref[row].astype(jnp.float32) * fresh, axis=1, keepdims=True)
-            * score_scale
-        )
-        row_max = jnp.maximum(jnp.max(scores, axis=1, keepdims=True), self_score)
-        raised = jnp.exp(scores - row_max)
-        self_raised = jnp.exp(self_score - row_max)
-        row_total = jnp.sum(raised, axis=1, keepdims=True) + self_raised
-        self_weight = self_raised.astype(jnp.bfloat16).astype(jnp.float32)
-        softmax_ref[row, :, 0:1] = row_max
-        softmax_ref[row, :, 1:2] = row_total
-        return raised, self_weight * fresh[:, :LAT], row_total
-
-    def weigh_second(row, scores):
-        old_max = softmax_ref[row, :, 0:1]
-        row_max = jnp.maximum(jnp.max(scores, axis=1, keepdims=True), old_max)
-        raised = jnp.exp(scores - row_max)
-        kept = jnp.exp(old_max - row_max)
-        row_total = softmax_ref[row, :, 1:2] * kept + jnp.sum(raised, axis=1, keepdims=True)
-        return raised, kept, row_total
-
-    def first_half(group, carry):
-        for copy in fetch_first(group):
-            copy.wait()
-
-        @pl.when(group + 2 < group_count)
-        def _():
-            start_first(group + 2)
-
-        @pl.when(group == group_count - 2)
-        def _():
-            def start(slot, carry):
-                fetch_second(slot).start()
-                return carry
-
-            lax.fori_loop(0, long_groups * group_pairs, start, 0)
-
-        rows = [group * GROUP_ROWS + i for i in range(GROUP_ROWS)]
-        scores = [score(row, 0) for row in rows]
-        weighed = [weigh_first(row, some) for row, some in zip(rows, scores)]
-        done = []
-        for row, (raised, fresh_part, row_total) in zip(rows, weighed):
-            gathered = gather(row, 0, raised) + fresh_part
-            gathered_ref[row] = gathered
-            done.append((gathered / row_total).reshape(owners, owned, LAT))
-        size = GROUP_ROWS * owned
-        out_ref[:, pl.ds(pl.multiple_of(group * size, size), size), :] = jnp.concatenate(
-            done, axis=1
-        ).astype(jnp.bfloat16)
-        return carry
-
-    def second_half(group, carry):
-        slots = [group * group_pairs + i for i in range(group_pairs)]
-        for slot in slots:
-            fetch_second(slot).wait()
-        pairs = [order[slot] for slot in slots]
+        gathered = gathered + self_weight * latent_wide[pl.ds(row, 1), :LAT]
+        return (gathered * (1.0 / row_total)).reshape(owners, owned, LAT)
+
+    def attend_rows(pairs, keys):
         rows = [2 * pair + i for pair in pairs for i in range(2)]
-        scores = [score(row, short) for row in rows]
-        weighed = [weigh_second(row, some) for row, some in zip(rows, scores)]
-        done = []
-        for row, (raised, kept, row_total) in zip(rows, weighed):
-            gathered = gather(row, short, raised) + gathered_ref[row] * kept
-            done.append((gathered / row_total).reshape(owners, owned, LAT))
+        scored = [score(row, keys) for row in rows]
+        weighed = [weigh(row, scores) for row, scores in zip(rows, scored)]
+        done = [gather(row, keys, *parts) for row, parts in zip(rows, weighed)]
         size = 2 * owned
         for i, pair in enumerate(pairs):
             out_ref[:, pl.ds(pl.multiple_of(pair * size, size), size), :] = jnp.concatenate(
                 done[2 * i : 2 * i + 2], axis=1
             ).astype(jnp.bfloat16)
+
+    def attend_group(group, carry):
+        pairs = [order[group * group_pairs + i] for i in range(group_pairs)]
+        whole = jnp.logical_or(group == 0, group >= short_groups)
+        is_long = jnp.where(group == 0, first_is_long, group >= short_groups)
+        for pair in pairs:
+            fetch_queries(pair).wait()
+
+            @pl.when(whole)
+            def _():
+                fetch_keys(pair, span).wait()
+
+            @pl.when(jnp.logical_not(whole))
+            def _():
+                fetch_keys(pair, short).wait()
+
+        @pl.when(group == 0)
+        def _():
+            for later in range(2, group_count):
+                start(later)
+
+        @pl.when(is_long)
+        def _():
+            attend_rows(pairs, span)
+
+        @pl.when(jnp.logical_not(is_long))
+        def _():
+            attend_rows(pairs, short)
+
         return carry
 
-    lax.fori_loop(0, group_count, first_half, 0)
-    lax.fori_loop(0, long_groups, second_half, 0)
+    lax.fori_loop(0, group_count, attend_group, 0)
     here = lax.axis_index("dp")
     z_size = owners // 2
     for place, owner_ref in enumerate(owner_refs):
@@ -195,12 +184,10 @@
             pltpu.VMEM(queries.shape, jnp.bfloat16),
             pltpu.VMEM(new_latent.shape, jnp.bfloat16),
             pltpu.VMEM(new_latent.shape, jnp.float32),
-            pltpu.VMEM((row_count, heads, LAT), jnp.float32),
-            pltpu.VMEM((row_count, heads, 128), jnp.float32),
             pltpu.SMEM(lengths.shape, jnp.int32),
             pltpu.SMEM((row_count // 2,), jnp.int32),
             pltpu.SemaphoreType.DMA((2,)),
-            pltpu.SemaphoreType.DMA((2, row_count // GROUP_ROWS)),
+            pltpu.SemaphoreType.DMA((row_count // 2,)),
             pltpu.SemaphoreType.DMA((row_count // 2,)),
         ],
         cost_estimate=pl.CostEstimate(

time: 56.5 us -> 56 us (level)
  the two profiles are of different devices: /device:TPU:4 before, /device:TPU:0 now
where the time goes in v3:
time: 56 us; the launch traced here: 55.9 us
  starting transfers between devices  26.1 us (47%)
  Pallas kernels  15.8 us (28%)
  waiting for transfers between devices  13.2 us (24%)
  between operations  0.75 us (1%)
    ppermute x15, starting transfers between devices, send(): return lax.ppermute(array, ('rep', 'dp'), pairs)  26.1 us
    ppermute x15, waiting for transfers between devices, send(): return lax.ppermute(array, ('rep', 'dp'), pairs)  13.2 us
    pallas_call x1, Pallas kernels, attend(): pl.pallas_call(attend_kernel, out_shape=[jax.ShapeDtypeStruct((row_count...  6.44 us
    pallas_call x1, Pallas kernels, bring(): pl.pallas_call(bring_kernel, out_shape=pltpu.VMEM(output_proj.shape, jnp....  5.27 us
    pallas_call x1, Pallas kernels, make_values(): pl.pallas_call(values_kernel, out_shape=(jax.ShapeDtypeStruct((rows, owne...  1.81 us
    pallas_call x1, Pallas kernels, project(): pl.pallas_call(project_kernel, out_shape=[part] * z_size, in_specs=[vmem,...  1.13 us
  transfers between devices with their start and end apart: 15, of which 4 were waited for; matrix products, arithmetic and copies ran while one was open for 0% of the time, Pallas kernels for 12%

profile of v3, /device:TPU:0, one launch (start us, length us, event | category | flops | bytes accessed | tf_op | source)
XLA Modules:
  0.0 55.9 jit_solution(3384776897931623067)
XLA Ops:
  0.6 6.4 %attend.1 = (bf16[128,512]{1,0:T(8,128)(2,1)S(1)}, bf16[128,512]{1,0:T(8,128)(2,1)S(1)}, bf16[128,512]{1,0:T(8,128)(2,1)S(1)}, bf16[128,512]{1,0:T(8,128)(2,1)S(...) custom-call(s32[128]{0:T(128)} %lengths_hbm.1, ...), custom_call_target="tpu_custom_call" | custom-call | flops 1207959552 | bytes 9437184 | tf_op jit(solution)/shard_map/attend/pallas_call | solution.py:176
  7.1 5.1 %collective-permute-start = (bf16[128,512]{1,0:T(8,128)(2,1)S(1)}, bf16[128,512]{1,0:T(8,128)(2,1)S(1)}, u32[]{:S(2)}, u32[]{:S(2)}) collective-permute-start(bf16[128,512]{1,0:T(8,128)(2,1)S(1)} %get-tuple-element.21), channel_id=1, source_target_pairs={{0,70},{1,71},{2,68},{3,69},{4,66},{5,67},{6,64},{7,65},{8,78},{9,... | collective-permute-start | bytes 393224 | tf_op jit(solution)/shard_map/ppermute | solution.py:400
  12.2 0.7 %collective-permute-start.1 = (bf16[128,512]{1,0:T(8,128)(2,1)S(1)}, bf16[128,512]{1,0:T(8,128)(2,1)S(1)}, u32[]{:S(2)}, u32[]{:S(2)}) collective-permute-start(bf16[128,512]{1,0:T(8,128)(2,1)S(1)} %get-tuple-element.22), channel_id=1, source_target_pairs={{0,69},{1,70},{2,71},{3,68},{4,65},{5,66},{6,67},{7,64},{8,77},{9,... | collective-permute-start | bytes 393224 | tf_op jit(solution)/shard_map/ppermute | solution.py:400
  12.9 4.7 %collective-permute-start.2 = (bf16[128,512]{1,0:T(8,128)(2,1)S(1)}, bf16[128,512]{1,0:T(8,128)(2,1)S(1)}, u32[]{:S(2)}, u32[]{:S(2)}) collective-permute-start(bf16[128,512]{1,0:T(8,128)(2,1)S(1)} %get-tuple-element.23), channel_id=1, source_target_pairs={{0,71},{1,68},{2,69},{3,70},{4,67},{5,64},{6,65},{7,66},{8,79},{9,... | collective-permute-start | bytes 393224 | tf_op jit(solution)/shard_map/ppermute | solution.py:400
  17.6 0.2 collective-permute-start.3
  17.8 0.2 collective-permute-start.4
  18.0 0.0 collective-permute-done.latent_refs_1_
  18.0 1.0 %collective-permute-start.5 = (bf16[128,512]{1,0:T(8,128)(2,1)S(1)}, bf16[128,512]{1,0:T(8,128)(2,1)S(1)}, u32[]{:S(2)}, u32[]{:S(2)}) collective-permute-start(bf16[128,512]{1,0:T(8,128)(2,1)S(1)} %get-tuple-element.26), channel_id=1, source_target_pairs={{0,1},{1,2},{2,3},{3,0},{4,5},{5,6},{6,7},{7,4},{8,9},{9,10},{10,1... | collective-permute-start | bytes 393224 | tf_op jit(solution)/shard_map/ppermute | solution.py:400
  19.0 3.5 %collective-permute-done.1.latent_refs_2_ = bf16[128,512]{1,0:T(8,128)(2,1)S(1)} collective-permute-done((bf16[128,512]{1,0:T(8,128)(2,1)S(1)}, bf16[128,512]{1,0:T(8,128)(2,1)S(1)}, u32[]{:S(2)}, u32[]{:S(2)}) %collective-permute-start.1) | collective-permute-done | bytes 131104 | tf_op jit(solution)/shard_map/ppermute | solution.py:400
  22.5 0.0 collective-permute-start.6
  22.5 0.0 copy-start
  22.5 5.3 %bring.1.proj_ref = bf16[1024,7168]{1,0:T(8,128)(2,1)S(1)} custom-call(bf16[128,512]{1,0:T(8,128)(2,1)S(1)} %get-tuple-element.20.after_hbm.latent_refs_0_, bf16[1024,7168]{1,0:T(8,128)(2,1)} %proj_hbm.1), custom_call_target="tpu_custom_call" | custom-call | bytes 14680064 | tf_op jit(solution)/shard_map/bring/pallas_call | solution.py:211
  27.8 0.0 copy-start.2
  27.8 0.0 copy-start.1
  27.8 0.0 collective-permute-done.2.latent_refs_3_
  27.8 0.0 collective-permute-done.3.latent_refs_4_
  27.9 0.0 collective-permute-done.4.latent_refs_5_
  27.9 0.0 collective-permute-done.5.latent_refs_6_
  27.9 0.1 collective-permute-done.6.latent_refs_7_
  28.0 0.0 copy-done
  28.0 1.8 %values.1 = (bf16[128,1024]{1,0:T(8,128)(2,1)S(1)}, bf16[4,16,3712]{2,1,0:T(8,128)(2,1)S(1)}, bf16[4,16,3712]{2,1,0:T(8,128)(2,1)S(1)}) custom-call(bf16[128,512]{1,0:T(8,128)(2,1)S(1)} %get-tuple-element.20.after_hbm.latent_refs_0_, bf16[128,512]{1,0:T(8,128)(2,1)S(1)} %collective-permute-done.latent_refs_1_, ...), custom_call_target="tpu_custom_call" | custom-call | flops 973078528 | bytes 7602176 | tf_op jit(solution)/shard_map/values/pallas_call | solution.py:266
  29.8 2.5 %collective-permute-start.11 = (bf16[4,16,3712]{2,1,0:T(8,128)(2,1)S(1)}, bf16[4,16,3712]{2,1,0:T(8,128)(2,1)S(1)}, u32[]{:S(2)}, u32[]{:S(2)}) collective-permute-start(bf16[4,16,3712]{2,1,0:T(8,128)(2,1)S(1)} %get-tuple-element.34), channel_id=1, source_target_pairs={{0,68},{1,69},{2,70},{3,71},{4,64},{5,65},{6,66},{7,67},{8,76},{9,... | collective-permute-start | bytes 1425416 | tf_op jit(solution)/shard_map/ppermute | solution.py:400
  32.3 1.1 %project.1 = (bf16[2,16,3456]{2,1,0:T(8,128)(2,1)S(1)}, bf16[2,16,3456]{2,1,0:T(8,128)(2,1)S(1)}, bf16[2,16,3456]{2,1,0:T(8,128)(2,1)S(1)}, bf16[2,16,3456]{2,1,0:T(8,128)(2,1)S(1)}) custom-call(bf16[128,1024]{1,0:T(8,128)(2,1)S(1)} %get-tuple-element.28.values_ref, bf16[1024,7168]{1,0:T(8,128)(2,1)S(1)} %bring.1.proj_ref), custom_call_target="tpu_custom_call" | custom-call | flops 905969664 | bytes 7077888 | tf_op jit(solution)/shard_map/project/pallas_call | solution.py:300
  33.5 1.0 %collective-permute-start.7 = (bf16[2,16,3456]{2,1,0:T(8,128)(2,1)S(1)}, bf16[2,16,3456]{2,1,0:T(8,128)(2,1)S(1)}, u32[]{:S(2)}, u32[]{:S(2)}) collective-permute-start(bf16[2,16,3456]{2,1,0:T(8,128)(2,1)S(1)} %get-tuple-element.30), channel_id=1, source_target_pairs={{0,1},{1,2},{2,3},{3,0},{4,5},{5,6},{6,7},{7,4},{8,9},{9,10},{10,1... | collective-permute-start | bytes 663560 | tf_op jit(solution)/shard_map/ppermute | solution.py:400
  34.5 2.6 %collective-permute-start.8 = (bf16[2,16,3456]{2,1,0:T(8,128)(2,1)S(1)}, bf16[2,16,3456]{2,1,0:T(8,128)(2,1)S(1)}, u32[]{:S(2)}, u32[]{:S(2)}) collective-permute-start(bf16[2,16,3456]{2,1,0:T(8,128)(2,1)S(1)} %get-tuple-element.31), channel_id=1, source_target_pairs={{0,2},{1,3},{2,0},{3,1},{4,6},{5,7},{6,4},{7,5},{8,10},{9,11},{10,... | collective-permute-start | bytes 663560 | tf_op jit(solution)/shard_map/ppermute | solution.py:400
  37.0 0.7 %collective-permute-start.9 = (bf16[2,16,3456]{2,1,0:T(8,128)(2,1)S(1)}, bf16[2,16,3456]{2,1,0:T(8,128)(2,1)S(1)}, u32[]{:S(2)}, u32[]{:S(2)}) collective-permute-start(bf16[2,16,3456]{2,1,0:T(8,128)(2,1)S(1)} %get-tuple-element.32), channel_id=1, source_target_pairs={{0,3},{1,0},{2,1},{3,2},{4,7},{5,4},{6,5},{7,6},{8,11},{9,8},{10,9... | collective-permute-start | bytes 663560 | tf_op jit(solution)/shard_map/ppermute | solution.py:400
  37.7 5.4 %collective-permute-done.11.came_ref = bf16[4,16,3712]{2,1,0:T(8,128)(2,1)S(1)} collective-permute-done((bf16[4,16,3712]{2,1,0:T(8,128)(2,1)S(1)}, bf16[4,16,3712]{2,1,0:T(8,128)(2,1)S(1)}, u32[]{:S(2)}, u32[]{:S(2)}) %collective-permute-start.11) | collective-permute-done | bytes 475168 | tf_op jit(solution)/shard_map/ppermute | solution.py:400
  43.1 0.1 add_far.1
  43.2 1.9 %collective-permute-start.12 = (bf16[16,3712]{1,0:T(8,128)(2,1)S(1)}, bf16[16,3712]{1,0:T(8,128)(2,1)S(1)}, u32[]{:S(2)}, u32[]{:S(2)}) collective-permute-start(bf16[16,3712]{1,0:T(8,128)(2,1)S(1)} %get-tuple-element.35), channel_id=1, source_target_pairs={{0,1},{1,2},{2,3},{3,0},{4,5},{5,6},{6,7},{7,4},{8,9},{9,10},{10,1... | collective-permute-start | bytes 356360 | tf_op jit(solution)/shard_map/ppermute | solution.py:400
  45.2 3.3 %collective-permute-start.13 = (bf16[16,3712]{1,0:T(8,128)(2,1)S(1)}, bf16[16,3712]{1,0:T(8,128)(2,1)S(1)}, u32[]{:S(2)}, u32[]{:S(2)}) collective-permute-start(bf16[16,3712]{1,0:T(8,128)(2,1)S(1)} %get-tuple-element.36), channel_id=1, source_target_pairs={{0,2},{1,3},{2,0},{3,1},{4,6},{5,7},{6,4},{7,5},{8,10},{9,11},{10,... | collective-permute-start | bytes 356360 | tf_op jit(solution)/shard_map/ppermute | solution.py:400
  48.5 0.0 collective-permute-done.7.refs_1_.near_refs_1_
  48.5 0.3 collective-permute-start.14
  48.7 0.0 collective-permute-done.8.refs_2_.near_refs_2_
  48.7 0.0 collective-permute-done.9.refs_3_.near_refs_3_
  48.7 0.1 add_near.1
  48.8 1.9 %collective-permute-start.10 = (bf16[16,3456]{1,0:T(8,128)(2,1)S(1)}, bf16[16,3456]{1,0:T(8,128)(2,1)S(1)}, u32[]{:S(2)}, u32[]{:S(2)}) collective-permute-start(bf16[16,3456]{1,0:T(8,128)(2,1)S(1)} %add_near.1), channel_id=1, source_target_pairs={{0,68},{1,69},{2,70},{3,71},{4,64},{5,65},{6,66},{7,67},{8,76},{9,... | collective-permute-start | bytes 331784 | tf_op jit(solution)/shard_map/ppermute | solution.py:400
  50.7 0.0 copy-done.2
  50.7 4.1 %collective-permute-done.10.far_ref = bf16[16,3456]{1,0:T(8,128)(2,1)S(1)} collective-permute-done((bf16[16,3456]{1,0:T(8,128)(2,1)S(1)}, bf16[16,3456]{1,0:T(8,128)(2,1)S(1)}, u32[]{:S(2)}, u32[]{:S(2)}) %collective-permute-start.10) | collective-permute-done | bytes 110624 | tf_op jit(solution)/shard_map/ppermute | solution.py:400
  54.8 0.0 collective-permute-done.12.step_refs_0_
  54.9 0.0 collective-permute-done.13.step_refs_1_
  54.9 0.0 collective-permute-done.14.step_refs_2_
  54.9 0.0 copy-done.1
  54.9 1.0 %finish.1 = (bf16[16,7168]{1,0:T(8,128)(2,1)}, bf16[16,7168]{1,0:T(8,128)(2,1)}) custom-call(bf16[2,16,3456]{2,1,0:T(8,128)(2,1)S(1)} %get-tuple-element.29.refs_0_.near_refs_0_, bf16[2,16,3456]{2,1,0:T(8,128)(2,1)S(1)} %collective-permute-done.7.refs_1_.near_refs_1_, bf16[2,16,3456]{2,1,0:T(8,128)(2,1)S(1)} %collective-permute-done.8.refs_2_.near_refs_2_, ...), custom_call_target="tpu_custom_call" | custom-call | tf_op jit(solution)/shard_map/finish/pallas_call | solution.py:380
  (1 shorter events, 0.0 us)
Async XLA Ops:
  7.1 10.9 %collective-permute-start = (bf16[128,512]{1,0:T(8,128)(2,1)S(1)}, bf16[128,512]{1,0:T(8,128)(2,1)S(1)}, u32[]{:S(2)}, u32[]{:S(2)}) collective-permute-start(bf16[128,512]{1,0:T(8,128)(2,1)S(1)} %get-tuple-element.21), channel_id=1, source_target_pairs={{0,70},{1,71},{2,68},{3,69},{4,66},{5,67},{6,64},{7,65},{8,78},{9,... | collective-permute-start | bytes 393224 | tf_op jit(solution)/shard_map/ppermute | solution.py:400
  12.2 10.3 %collective-permute-start.1 = (bf16[128,512]{1,0:T(8,128)(2,1)S(1)}, bf16[128,512]{1,0:T(8,128)(2,1)S(1)}, u32[]{:S(2)}, u32[]{:S(2)}) collective-permute-start(bf16[128,512]{1,0:T(8,128)(2,1)S(1)} %get-tuple-element.22), channel_id=1, source_target_pairs={{0,69},{1,70},{2,71},{3,68},{4,65},{5,66},{6,67},{7,64},{8,77},{9,... | collective-permute-start | bytes 393224 | tf_op jit(solution)/shard_map/ppermute | solution.py:400
  12.9 14.9 %collective-permute-start.2 = (bf16[128,512]{1,0:T(8,128)(2,1)S(1)}, bf16[128,512]{1,0:T(8,128)(2,1)S(1)}, u32[]{:S(2)}, u32[]{:S(2)}) collective-permute-start(bf16[128,512]{1,0:T(8,128)(2,1)S(1)} %get-tuple-element.23), channel_id=1, source_target_pairs={{0,71},{1,68},{2,69},{3,70},{4,67},{5,64},{6,65},{7,66},{8,79},{9,... | collective-permute-start | bytes 393224 | tf_op jit(solution)/shard_map/ppermute | solution.py:400
  17.6 10.3 %collective-permute-start.3 = (bf16[128,512]{1,0:T(8,128)(2,1)S(1)}, bf16[128,512]{1,0:T(8,128)(2,1)S(1)}, u32[]{:S(2)}, u32[]{:S(2)}) collective-permute-start(bf16[128,512]{1,0:T(8,128)(2,1)S(1)} %get-tuple-element.24), channel_id=1, source_target_pairs={{0,68},{1,69},{2,70},{3,71},{4,64},{5,65},{6,66},{7,67},{8,76},{9,... | collective-permute-start | bytes 393224 | tf_op jit(solution)/shard_map/ppermute | solution.py:400
  17.8 10.1 %collective-permute-start.4 = (bf16[128,512]{1,0:T(8,128)(2,1)S(1)}, bf16[128,512]{1,0:T(8,128)(2,1)S(1)}, u32[]{:S(2)}, u32[]{:S(2)}) collective-permute-start(bf16[128,512]{1,0:T(8,128)(2,1)S(1)} %get-tuple-element.25), channel_id=1, source_target_pairs={{0,2},{1,3},{2,0},{3,1},{4,6},{5,7},{6,4},{7,5},{8,10},{9,11},{10,... | collective-permute-start | bytes 393224 | tf_op jit(solution)/shard_map/ppermute | solution.py:400
  18.0 9.9 %collective-permute-start.5 = (bf16[128,512]{1,0:T(8,128)(2,1)S(1)}, bf16[128,512]{1,0:T(8,128)(2,1)S(1)}, u32[]{:S(2)}, u32[]{:S(2)}) collective-permute-start(bf16[128,512]{1,0:T(8,128)(2,1)S(1)} %get-tuple-element.26), channel_id=1, source_target_pairs={{0,1},{1,2},{2,3},{3,0},{4,5},{5,6},{6,7},{7,4},{8,9},{9,10},{10,1... | collective-permute-start | bytes 393224 | tf_op jit(solution)/shard_map/ppermute | solution.py:400
  22.5 5.5 %collective-permute-start.6 = (bf16[128,512]{1,0:T(8,128)(2,1)S(1)}, bf16[128,512]{1,0:T(8,128)(2,1)S(1)}, u32[]{:S(2)}, u32[]{:S(2)}) collective-permute-start(bf16[128,512]{1,0:T(8,128)(2,1)S(1)} %get-tuple-element.27), channel_id=1, source_target_pairs={{0,3},{1,0},{2,1},{3,2},{4,7},{5,4},{6,5},{7,6},{8,11},{9,8},{10,9... | collective-permute-start | bytes 393224 | tf_op jit(solution)/shard_map/ppermute | solution.py:400
  22.5 5.5 %copy-start = (bf16[8,512,128]{2,1,0:T(8,128)(2,1)S(1)}, bf16[8,512,128]{2,1,0:T(8,128)(2,1)}, u32[]{:S(2)}) copy-start(bf16[8,512,128]{2,1,0:T(8,128)(2,1)} %value_up_ref.1) | copy-start | bytes 3145732
  27.8 22.9 %copy-start.2 = (bf16[7168]{0:T(1024)(128)(2,1)S(1)}, bf16[7168]{0:T(1024)(128)(2,1)}, u32[]{:S(2)}) copy-start(bf16[7168]{0:T(1024)(128)(2,1)} %param.15) | copy-start | bytes 43012
  27.8 27.0 %copy-start.1 = (bf16[16,7168]{1,0:T(8,128)(2,1)S(1)}, bf16[16,7168]{1,0:T(8,128)(2,1)}, u32[]{:S(2)}) copy-start(bf16[16,7168]{1,0:T(8,128)(2,1)} %residual_ref.1) | copy-start | bytes 688132
  29.8 13.3 %collective-permute-start.11 = (bf16[4,16,3712]{2,1,0:T(8,128)(2,1)S(1)}, bf16[4,16,3712]{2,1,0:T(8,128)(2,1)S(1)}, u32[]{:S(2)}, u32[]{:S(2)}) collective-permute-start(bf16[4,16,3712]{2,1,0:T(8,128)(2,1)S(1)} %get-tuple-element.34), channel_id=1, source_target_pairs={{0,68},{1,69},{2,70},{3,71},{4,64},{5,65},{6,66},{7,67},{8,76},{9,... | collective-permute-start | bytes 1425416 | tf_op jit(solution)/shard_map/ppermute | solution.py:400
  33.5 15.0 %collective-permute-start.7 = (bf16[2,16,3456]{2,1,0:T(8,128)(2,1)S(1)}, bf16[2,16,3456]{2,1,0:T(8,128)(2,1)S(1)}, u32[]{:S(2)}, u32[]{:S(2)}) collective-permute-start(bf16[2,16,3456]{2,1,0:T(8,128)(2,1)S(1)} %get-tuple-element.30), channel_id=1, source_target_pairs={{0,1},{1,2},{2,3},{3,0},{4,5},{5,6},{6,7},{7,4},{8,9},{9,10},{10,1... | collective-permute-start | bytes 663560 | tf_op jit(solution)/shard_map/ppermute | solution.py:400
  34.5 14.3 %collective-permute-start.8 = (bf16[2,16,3456]{2,1,0:T(8,128)(2,1)S(1)}, bf16[2,16,3456]{2,1,0:T(8,128)(2,1)S(1)}, u32[]{:S(2)}, u32[]{:S(2)}) collective-permute-start(bf16[2,16,3456]{2,1,0:T(8,128)(2,1)S(1)} %get-tuple-element.31), channel_id=1, source_target_pairs={{0,2},{1,3},{2,0},{3,1},{4,6},{5,7},{6,4},{7,5},{8,10},{9,11},{10,... | collective-permute-start | bytes 663560 | tf_op jit(solution)/shard_map/ppermute | solution.py:400
  37.0 11.7 %collective-permute-start.9 = (bf16[2,16,3456]{2,1,0:T(8,128)(2,1)S(1)}, bf16[2,16,3456]{2,1,0:T(8,128)(2,1)S(1)}, u32[]{:S(2)}, u32[]{:S(2)}) collective-permute-start(bf16[2,16,3456]{2,1,0:T(8,128)(2,1)S(1)} %get-tuple-element.32), channel_id=1, source_target_pairs={{0,3},{1,0},{2,1},{3,2},{4,7},{5,4},{6,5},{7,6},{8,11},{9,8},{10,9... | collective-permute-start | bytes 663560 | tf_op jit(solution)/shard_map/ppermute | solution.py:400
  43.2 11.6 %collective-permute-start.12 = (bf16[16,3712]{1,0:T(8,128)(2,1)S(1)}, bf16[16,3712]{1,0:T(8,128)(2,1)S(1)}, u32[]{:S(2)}, u32[]{:S(2)}) collective-permute-start(bf16[16,3712]{1,0:T(8,128)(2,1)S(1)} %get-tuple-element.35), channel_id=1, source_target_pairs={{0,1},{1,2},{2,3},{3,0},{4,5},{5,6},{6,7},{7,4},{8,9},{9,10},{10,1... | collective-permute-start | bytes 356360 | tf_op jit(solution)/shard_map/ppermute | solution.py:400
  45.2 9.7 %collective-permute-start.13 = (bf16[16,3712]{1,0:T(8,128)(2,1)S(1)}, bf16[16,3712]{1,0:T(8,128)(2,1)S(1)}, u32[]{:S(2)}, u32[]{:S(2)}) collective-permute-start(bf16[16,3712]{1,0:T(8,128)(2,1)S(1)} %get-tuple-element.36), channel_id=1, source_target_pairs={{0,2},{1,3},{2,0},{3,1},{4,6},{5,7},{6,4},{7,5},{8,10},{9,11},{10,... | collective-permute-start | bytes 356360 | tf_op jit(solution)/shard_map/ppermute | solution.py:400
  48.5 6.4 %collective-permute-start.14 = (bf16[16,3712]{1,0:T(8,128)(2,1)S(1)}, bf16[16,3712]{1,0:T(8,128)(2,1)S(1)}, u32[]{:S(2)}, u32[]{:S(2)}) collective-permute-start(bf16[16,3712]{1,0:T(8,128)(2,1)S(1)} %get-tuple-element.37), channel_id=1, source_target_pairs={{0,3},{1,0},{2,1},{3,2},{4,7},{5,4},{6,5},{7,6},{8,11},{9,8},{10,9... | collective-permute-start | bytes 356360 | tf_op jit(solution)/shard_map/ppermute | solution.py:400
  48.8 6.0 %collective-permute-start.10 = (bf16[16,3456]{1,0:T(8,128)(2,1)S(1)}, bf16[16,3456]{1,0:T(8,128)(2,1)S(1)}, u32[]{:S(2)}, u32[]{:S(2)}) collective-permute-start(bf16[16,3456]{1,0:T(8,128)(2,1)S(1)} %add_near.1), channel_id=1, source_target_pairs={{0,68},{1,69},{2,70},{3,71},{4,64},{5,65},{6,66},{7,67},{8,76},{9,... | collective-permute-start | bytes 331784 | tf_op jit(solution)/shard_map/ppermute | solution.py:400

commit v4 on v3

--- a/solution.py
+++ b/solution.py
@@ -9,7 +9,7 @@
 GROUP_ROWS = 4
 PROJ_STEP = 1024
 LEFT_COLUMNS = 3456
-ORDER = (6, 5, 7, 4, 2, 1, 3)
+ORDERS = ((6, 5, 7, 4, 2, 1, 3), (6, 5, 7, 4, 2, 1, 3))
 exponent_scale = 192.0 ** (-0.5) * 1.4426950408889634
 norm_eps = 1e-06
 MIB = 1024 * 1024
@@ -160,10 +160,13 @@
 
     lax.fori_loop(0, group_count, attend_group, 0)
     here = lax.axis_index("dp")
+    core = lax.axis_index("rep") % 2
     z_size = owners // 2
-    for place, owner_ref in enumerate(owner_refs):
+    for owner_ref, places in zip(owner_refs, ((0, 0),) + tuple(zip(*ORDERS))):
+        place = jnp.where(core == 0, *places)
         far = (here // z_size + place // z_size) % 2
-        owner_ref[...] = out_ref[far * z_size + (here + place) % z_size]
+        step = jnp.where(core == 0, place, z_size - place % z_size)
+        owner_ref[...] = out_ref[far * z_size + (here + step) % z_size]
 
 
 def attend(queries, latent_cache, new_latent, lengths, owners):
@@ -229,11 +232,13 @@
     z_size = owners // 2
 
     size = rows_here * owned
-    for place, latent_ref in zip((0,) + ORDER, latent_refs):
-        far, step = place // z_size, place % z_size
-        back = (far * z_size + (z_size - step) % z_size) * size
+    core = lax.axis_index("rep") % 2
+    for latent_ref, places in zip(latent_refs, ((0, 0),) + tuple(zip(*ORDERS))):
+        place = jnp.where(core == 0, *places)
+        step = (z_size - place % z_size) % z_size
+        back = pl.multiple_of((place // z_size * z_size + step) * size, size)
         for c in range(lat // 128):
-            wide[c, back : back + size] = latent_ref[:, c * 128 : (c + 1) * 128].astype(
+            wide[c, pl.ds(back, size)] = latent_ref[:, c * 128 : (c + 1) * 128].astype(
                 jnp.float32
             )
     for h in range(owned):
@@ -387,11 +392,13 @@
     )(nears, far, own, came, steps, residual, norm_gain.reshape(1, -1))
 
 
-def send(array, far, step, mesh_shape):
+def send(array, places, mesh_shape):
     replicas, owners = mesh_shape
     z_size = owners // 2
     pairs = []
     for replica in range(replicas):
+        far, step = divmod(places[replica % 2], z_size)
+        step = -step if replica % 2 else step
         for owner in range(owners):
             to_replica = (replica + far * (replicas // 2)) % replicas
             to_half = (owner // z_size + far) % 2
@@ -409,17 +416,16 @@
     z_size = owners // 2
     latents = attend(queries, latent_cache, new_latent, lengths, owners)
     owned_latents = [latents[0]] + [
-        send(latents[place], place // z_size, place % z_size, mesh_shape)
-        for place in ORDER
+        send(latent, places, mesh_shape) for latent, places in zip(latents[1:], zip(*ORDERS))
     ]
     proj_near = bring(output_proj, latents[0])
     values, own, across = make_values(owned_latents, value_up, proj_near, owners, rows_here)
-    came = send(across, 1, 0, mesh_shape)
+    came = send(across, (z_size, z_size), mesh_shape)
     parts = project(values, proj_near, owners, rows_here)
-    nears = [parts[0]] + [send(parts[k], 0, k, mesh_shape) for k in range(1, z_size)]
+    nears = [parts[0]] + [send(parts[k], (k, k), mesh_shape) for k in range(1, z_size)]
     pairs = add_far(own, came)
-    steps = [send(pair, 0, k, mesh_shape) for k, pair in enumerate(pairs, 1)]
-    far = send(add_near(nears), 1, 0, mesh_shape)
+    steps = [send(pair, (k, k), mesh_shape) for k, pair in enumerate(pairs, 1)]
+    far = send(add_near(nears), (z_size, z_size), mesh_shape)
     return finish(nears, far, own, came, steps, residual, norm_gain)
 
 

time: 56 us -> 55.9 us (level); the launches traced: 55.9 us -> 55 us
  Pallas kernels: 15.8 us -> 14.5 us
    pallas_call x1, Pallas kernels: 6.44 us -> 5.1 us  [attend(): pl.pallas_call(attend_kernel, out_shape=[jax.ShapeDtypeStruct((row_count...]
  transfers between devices with their start and end apart: 15 -> 15, of which waited for: 4 -> 3; matrix products, arithmetic and copies ran while one was open for 0% -> 0% of each run, Pallas kernels for 12% -> 12%
where the time goes in v4:
time: 55.9 us; the launch traced here: 55 us
  starting transfers between devices  26.5 us (47%)
  Pallas kernels  14.5 us (26%)
  waiting for transfers between devices  13.1 us (23%)
  between operations  0.75 us (1%)
    ppermute x15, starting transfers between devices, send(): return lax.ppermute(array, ('rep', 'dp'), pairs)  26.5 us
    ppermute x15, waiting for transfers between devices, send(): return lax.ppermute(array, ('rep', 'dp'), pairs)  13.1 us
    pallas_call x1, Pallas kernels, bring(): pl.pallas_call(bring_kernel, out_shape=pltpu.VMEM(output_proj.shape, jnp....  5.27 us
    pallas_call x1, Pallas kernels, attend(): pl.pallas_call(attend_kernel, out_shape=[jax.ShapeDtypeStruct((row_count...  5.1 us
    pallas_call x1, Pallas kernels, make_values(): pl.pallas_call(values_kernel, out_shape=(jax.ShapeDtypeStruct((rows, owne...  1.81 us
    pallas_call x1, Pallas kernels, project(): pl.pallas_call(project_kernel, out_shape=[part] * z_size, in_specs=[vmem,...  1.13 us
  transfers between devices with their start and end apart: 15, of which 3 were waited for; matrix products, arithmetic and copies ran while one was open for 0% of the time, Pallas kernels for 12%

profile of v4, /device:TPU:0, one launch (start us, length us, event | category | flops | bytes accessed | tf_op | source)
XLA Modules:
  0.0 55.0 jit_solution(4067758343454986989)
XLA Ops:
  0.6 5.1 %attend.1 = (bf16[128,512]{1,0:T(8,128)(2,1)S(1)}, bf16[128,512]{1,0:T(8,128)(2,1)S(1)}, bf16[128,512]{1,0:T(8,128)(2,1)S(1)}, bf16[128,512]{1,0:T(8,128)(2,1)S(...) custom-call(s32[128]{0:T(128)} %lengths_hbm.1, ...), custom_call_target="tpu_custom_call" | custom-call | flops 1207959552 | bytes 9437184 | tf_op jit(solution)/shard_map/attend/pallas_call | solution.py:179
  5.7 6.5 %collective-permute-start = (bf16[128,512]{1,0:T(8,128)(2,1)S(1)}, bf16[128,512]{1,0:T(8,128)(2,1)S(1)}, u32[]{:S(2)}, u32[]{:S(2)}) collective-permute-start(bf16[128,512]{1,0:T(8,128)(2,1)S(1)} %get-tuple-element.21), channel_id=1, source_target_pairs={{0,70},{1,71},{2,68},{3,69},{4,66},{5,67},{6,64},{7,65},{8,78},{9,... | collective-permute-start | bytes 393224 | tf_op jit(solution)/shard_map/ppermute | solution.py:407
  12.2 2.0 %collective-permute-start.1 = (bf16[128,512]{1,0:T(8,128)(2,1)S(1)}, bf16[128,512]{1,0:T(8,128)(2,1)S(1)}, u32[]{:S(2)}, u32[]{:S(2)}) collective-permute-start(bf16[128,512]{1,0:T(8,128)(2,1)S(1)} %get-tuple-element.22), channel_id=1, source_target_pairs={{0,69},{1,70},{2,71},{3,68},{4,65},{5,66},{6,67},{7,64},{8,79},{9,... | collective-permute-start | bytes 393224 | tf_op jit(solution)/shard_map/ppermute | solution.py:407
  14.3 3.3 %collective-permute-start.2 = (bf16[128,512]{1,0:T(8,128)(2,1)S(1)}, bf16[128,512]{1,0:T(8,128)(2,1)S(1)}, u32[]{:S(2)}, u32[]{:S(2)}) collective-permute-start(bf16[128,512]{1,0:T(8,128)(2,1)S(1)} %get-tuple-element.23), channel_id=1, source_target_pairs={{0,71},{1,68},{2,69},{3,70},{4,67},{5,64},{6,65},{7,66},{8,77},{9,... | collective-permute-start | bytes 393224 | tf_op jit(solution)/shard_map/ppermute | solution.py:407
  17.6 0.2 collective-permute-start.3
  17.8 0.2 collective-permute-start.4
  18.0 0.0 collective-permute-done.latent_refs_1_
  18.0 1.0 %collective-permute-start.5 = (bf16[128,512]{1,0:T(8,128)(2,1)S(1)}, bf16[128,512]{1,0:T(8,128)(2,1)S(1)}, u32[]{:S(2)}, u32[]{:S(2)}) collective-permute-start(bf16[128,512]{1,0:T(8,128)(2,1)S(1)} %get-tuple-element.26), channel_id=1, source_target_pairs={{0,1},{1,2},{2,3},{3,0},{4,5},{5,6},{6,7},{7,4},{8,11},{9,8},{10,9... | collective-permute-start | bytes 393224 | tf_op jit(solution)/shard_map/ppermute | solution.py:407
  19.0 3.4 %collective-permute-done.1.latent_refs_2_ = bf16[128,512]{1,0:T(8,128)(2,1)S(1)} collective-permute-done((bf16[128,512]{1,0:T(8,128)(2,1)S(1)}, bf16[128,512]{1,0:T(8,128)(2,1)S(1)}, u32[]{:S(2)}, u32[]{:S(2)}) %collective-permute-start.1) | collective-permute-done | bytes 131104 | tf_op jit(solution)/shard_map/ppermute | solution.py:407
  22.4 0.0 collective-permute-start.6
  22.4 0.0 copy-start
  22.4 5.3 %bring.1.proj_ref = bf16[1024,7168]{1,0:T(8,128)(2,1)S(1)} custom-call(bf16[128,512]{1,0:T(8,128)(2,1)S(1)} %get-tuple-element.20.after_hbm.latent_refs_0_, bf16[1024,7168]{1,0:T(8,128)(2,1)} %proj_hbm.1), custom_call_target="tpu_custom_call" | custom-call | bytes 14680064 | tf_op jit(solution)/shard_map/bring/pallas_call | solution.py:214
  27.7 0.0 copy-start.2
  27.7 0.0 copy-start.1
  27.7 0.0 collective-permute-done.2.latent_refs_3_
  27.7 0.0 collective-permute-done.3.latent_refs_4_
  27.7 0.0 collective-permute-done.4.latent_refs_5_
  27.7 0.0 collective-permute-done.5.latent_refs_6_
  27.8 0.0 collective-permute-done.6.latent_refs_7_
  27.8 0.0 copy-done
  27.8 1.8 %values.1 = (bf16[128,1024]{1,0:T(8,128)(2,1)S(1)}, bf16[4,16,3712]{2,1,0:T(8,128)(2,1)S(1)}, bf16[4,16,3712]{2,1,0:T(8,128)(2,1)S(1)}) custom-call(bf16[128,512]{1,0:T(8,128)(2,1)S(1)} %get-tuple-element.20.after_hbm.latent_refs_0_, bf16[128,512]{1,0:T(8,128)(2,1)S(1)} %collective-permute-done.latent_refs_1_, ...), custom_call_target="tpu_custom_call" | custom-call | flops 973078528 | bytes 7602176 | tf_op jit(solution)/shard_map/values/pallas_call | solution.py:271
  29.6 1.8 %collective-permute-start.11 = (bf16[4,16,3712]{2,1,0:T(8,128)(2,1)S(1)}, bf16[4,16,3712]{2,1,0:T(8,128)(2,1)S(1)}, u32[]{:S(2)}, u32[]{:S(2)}) collective-permute-start(bf16[4,16,3712]{2,1,0:T(8,128)(2,1)S(1)} %get-tuple-element.34), channel_id=1, source_target_pairs={{0,68},{1,69},{2,70},{3,71},{4,64},{5,65},{6,66},{7,67},{8,76},{9,... | collective-permute-start | bytes 1425416 | tf_op jit(solution)/shard_map/ppermute | solution.py:407
  31.4 1.1 %project.1 = (bf16[2,16,3456]{2,1,0:T(8,128)(2,1)S(1)}, bf16[2,16,3456]{2,1,0:T(8,128)(2,1)S(1)}, bf16[2,16,3456]{2,1,0:T(8,128)(2,1)S(1)}, bf16[2,16,3456]{2,1,0:T(8,128)(2,1)S(1)}) custom-call(bf16[128,1024]{1,0:T(8,128)(2,1)S(1)} %get-tuple-element.28.values_ref, bf16[1024,7168]{1,0:T(8,128)(2,1)S(1)} %bring.1.proj_ref), custom_call_target="tpu_custom_call" | custom-call | flops 905969664 | bytes 7077888 | tf_op jit(solution)/shard_map/project/pallas_call | solution.py:305
  32.5 0.7 %collective-permute-start.7 = (bf16[2,16,3456]{2,1,0:T(8,128)(2,1)S(1)}, bf16[2,16,3456]{2,1,0:T(8,128)(2,1)S(1)}, u32[]{:S(2)}, u32[]{:S(2)}) collective-permute-start(bf16[2,16,3456]{2,1,0:T(8,128)(2,1)S(1)} %get-tuple-element.30), channel_id=1, source_target_pairs={{0,1},{1,2},{2,3},{3,0},{4,5},{5,6},{6,7},{7,4},{8,11},{9,8},{10,9... | collective-permute-start | bytes 663560 | tf_op jit(solution)/shard_map/ppermute | solution.py:407
  33.2 3.2 %collective-permute-start.8 = (bf16[2,16,3456]{2,1,0:T(8,128)(2,1)S(1)}, bf16[2,16,3456]{2,1,0:T(8,128)(2,1)S(1)}, u32[]{:S(2)}, u32[]{:S(2)}) collective-permute-start(bf16[2,16,3456]{2,1,0:T(8,128)(2,1)S(1)} %get-tuple-element.31), channel_id=1, source_target_pairs={{0,2},{1,3},{2,0},{3,1},{4,6},{5,7},{6,4},{7,5},{8,10},{9,11},{10,... | collective-permute-start | bytes 663560 | tf_op jit(solution)/shard_map/ppermute | solution.py:407
  36.4 1.1 %collective-permute-start.9 = (bf16[2,16,3456]{2,1,0:T(8,128)(2,1)S(1)}, bf16[2,16,3456]{2,1,0:T(8,128)(2,1)S(1)}, u32[]{:S(2)}, u32[]{:S(2)}) collective-permute-start(bf16[2,16,3456]{2,1,0:T(8,128)(2,1)S(1)} %get-tuple-element.32), channel_id=1, source_target_pairs={{0,3},{1,0},{2,1},{3,2},{4,7},{5,4},{6,5},{7,6},{8,9},{9,10},{10,1... | collective-permute-start | bytes 663560 | tf_op jit(solution)/shard_map/ppermute | solution.py:407
  37.5 5.9 %collective-permute-done.11.came_ref = bf16[4,16,3712]{2,1,0:T(8,128)(2,1)S(1)} collective-permute-done((bf16[4,16,3712]{2,1,0:T(8,128)(2,1)S(1)}, bf16[4,16,3712]{2,1,0:T(8,128)(2,1)S(1)}, u32[]{:S(2)}, u32[]{:S(2)}) %collective-permute-start.11) | collective-permute-done | bytes 475168 | tf_op jit(solution)/shard_map/ppermute | solution.py:407
  43.4 0.1 add_far.1
  43.5 0.7 %collective-permute-start.12 = (bf16[16,3712]{1,0:T(8,128)(2,1)S(1)}, bf16[16,3712]{1,0:T(8,128)(2,1)S(1)}, u32[]{:S(2)}, u32[]{:S(2)}) collective-permute-start(bf16[16,3712]{1,0:T(8,128)(2,1)S(1)} %get-tuple-element.35), channel_id=1, source_target_pairs={{0,1},{1,2},{2,3},{3,0},{4,5},{5,6},{6,7},{7,4},{8,11},{9,8},{10,9... | collective-permute-start | bytes 356360 | tf_op jit(solution)/shard_map/ppermute | solution.py:407
  44.2 2.0 %collective-permute-start.13 = (bf16[16,3712]{1,0:T(8,128)(2,1)S(1)}, bf16[16,3712]{1,0:T(8,128)(2,1)S(1)}, u32[]{:S(2)}, u32[]{:S(2)}) collective-permute-start(bf16[16,3712]{1,0:T(8,128)(2,1)S(1)} %get-tuple-element.36), channel_id=1, source_target_pairs={{0,2},{1,3},{2,0},{3,1},{4,6},{5,7},{6,4},{7,5},{8,10},{9,11},{10,... | collective-permute-start | bytes 356360 | tf_op jit(solution)/shard_map/ppermute | solution.py:407
  46.2 0.0 collective-permute-done.7.refs_1_.near_refs_1_
  46.2 1.6 %collective-permute-start.14 = (bf16[16,3712]{1,0:T(8,128)(2,1)S(1)}, bf16[16,3712]{1,0:T(8,128)(2,1)S(1)}, u32[]{:S(2)}, u32[]{:S(2)}) collective-permute-start(bf16[16,3712]{1,0:T(8,128)(2,1)S(1)} %get-tuple-element.37), channel_id=1, source_target_pairs={{0,3},{1,0},{2,1},{3,2},{4,7},{5,4},{6,5},{7,6},{8,9},{9,10},{10,1... | collective-permute-start | bytes 356360 | tf_op jit(solution)/shard_map/ppermute | solution.py:407
  47.8 0.0 collective-permute-done.8.refs_2_.near_refs_2_
  47.8 0.0 collective-permute-done.9.refs_3_.near_refs_3_
  47.8 0.1 add_near.1
  47.9 2.2 %collective-permute-start.10 = (bf16[16,3456]{1,0:T(8,128)(2,1)S(1)}, bf16[16,3456]{1,0:T(8,128)(2,1)S(1)}, u32[]{:S(2)}, u32[]{:S(2)}) collective-permute-start(bf16[16,3456]{1,0:T(8,128)(2,1)S(1)} %add_near.1), channel_id=1, source_target_pairs={{0,68},{1,69},{2,70},{3,71},{4,64},{5,65},{6,66},{7,67},{8,76},{9,... | collective-permute-start | bytes 331784 | tf_op jit(solution)/shard_map/ppermute | solution.py:407
  50.0 0.0 copy-done.2
  50.1 3.9 %collective-permute-done.10.far_ref = bf16[16,3456]{1,0:T(8,128)(2,1)S(1)} collective-permute-done((bf16[16,3456]{1,0:T(8,128)(2,1)S(1)}, bf16[16,3456]{1,0:T(8,128)(2,1)S(1)}, u32[]{:S(2)}, u32[]{:S(2)}) %collective-permute-start.10) | collective-permute-done | bytes 110624 | tf_op jit(solution)/shard_map/ppermute | solution.py:407
  53.9 0.0 collective-permute-done.12.step_refs_0_
  53.9 0.0 collective-permute-done.13.step_refs_1_
  53.9 0.0 collective-permute-done.14.step_refs_2_
  53.9 0.0 copy-done.1
  53.9 1.0 %finish.1 = (bf16[16,7168]{1,0:T(8,128)(2,1)}, bf16[16,7168]{1,0:T(8,128)(2,1)}) custom-call(bf16[2,16,3456]{2,1,0:T(8,128)(2,1)S(1)} %get-tuple-element.29.refs_0_.near_refs_0_, bf16[2,16,3456]{2,1,0:T(8,128)(2,1)S(1)} %collective-permute-done.7.refs_1_.near_refs_1_, bf16[2,16,3456]{2,1,0:T(8,128)(2,1)S(1)} %collective-permute-done.8.refs_2_.near_refs_2_, ...), custom_call_target="tpu_custom_call" | custom-call | tf_op jit(solution)/shard_map/finish/pallas_call | solution.py:385
  (1 shorter events, 0.0 us)
Async XLA Ops:
  5.7 12.3 %collective-permute-start = (bf16[128,512]{1,0:T(8,128)(2,1)S(1)}, bf16[128,512]{1,0:T(8,128)(2,1)S(1)}, u32[]{:S(2)}, u32[]{:S(2)}) collective-permute-start(bf16[128,512]{1,0:T(8,128)(2,1)S(1)} %get-tuple-element.21), channel_id=1, source_target_pairs={{0,70},{1,71},{2,68},{3,69},{4,66},{5,67},{6,64},{7,65},{8,78},{9,... | collective-permute-start | bytes 393224 | tf_op jit(solution)/shard_map/ppermute | solution.py:407
  12.2 10.2 %collective-permute-start.1 = (bf16[128,512]{1,0:T(8,128)(2,1)S(1)}, bf16[128,512]{1,0:T(8,128)(2,1)S(1)}, u32[]{:S(2)}, u32[]{:S(2)}) collective-permute-start(bf16[128,512]{1,0:T(8,128)(2,1)S(1)} %get-tuple-element.22), channel_id=1, source_target_pairs={{0,69},{1,70},{2,71},{3,68},{4,65},{5,66},{6,67},{7,64},{8,79},{9,... | collective-permute-start | bytes 393224 | tf_op jit(solution)/shard_map/ppermute | solution.py:407
  14.3 13.4 %collective-permute-start.2 = (bf16[128,512]{1,0:T(8,128)(2,1)S(1)}, bf16[128,512]{1,0:T(8,128)(2,1)S(1)}, u32[]{:S(2)}, u32[]{:S(2)}) collective-permute-start(bf16[128,512]{1,0:T(8,128)(2,1)S(1)} %get-tuple-element.23), channel_id=1, source_target_pairs={{0,71},{1,68},{2,69},{3,70},{4,67},{5,64},{6,65},{7,66},{8,77},{9,... | collective-permute-start | bytes 393224 | tf_op jit(solution)/shard_map/ppermute | solution.py:407
  17.6 10.1 %collective-permute-start.3 = (bf16[128,512]{1,0:T(8,128)(2,1)S(1)}, bf16[128,512]{1,0:T(8,128)(2,1)S(1)}, u32[]{:S(2)}, u32[]{:S(2)}) collective-permute-start(bf16[128,512]{1,0:T(8,128)(2,1)S(1)} %get-tuple-element.24), channel_id=1, source_target_pairs={{0,68},{1,69},{2,70},{3,71},{4,64},{5,65},{6,66},{7,67},{8,76},{9,... | collective-permute-start | bytes 393224 | tf_op jit(solution)/shard_map/ppermute | solution.py:407
  17.8 9.9 %collective-permute-start.4 = (bf16[128,512]{1,0:T(8,128)(2,1)S(1)}, bf16[128,512]{1,0:T(8,128)(2,1)S(1)}, u32[]{:S(2)}, u32[]{:S(2)}) collective-permute-start(bf16[128,512]{1,0:T(8,128)(2,1)S(1)} %get-tuple-element.25), channel_id=1, source_target_pairs={{0,2},{1,3},{2,0},{3,1},{4,6},{5,7},{6,4},{7,5},{8,10},{9,11},{10,... | collective-permute-start | bytes 393224 | tf_op jit(solution)/shard_map/ppermute | solution.py:407
  18.0 9.8 %collective-permute-start.5 = (bf16[128,512]{1,0:T(8,128)(2,1)S(1)}, bf16[128,512]{1,0:T(8,128)(2,1)S(1)}, u32[]{:S(2)}, u32[]{:S(2)}) collective-permute-start(bf16[128,512]{1,0:T(8,128)(2,1)S(1)} %get-tuple-element.26), channel_id=1, source_target_pairs={{0,1},{1,2},{2,3},{3,0},{4,5},{5,6},{6,7},{7,4},{8,11},{9,8},{10,9... | collective-permute-start | bytes 393224 | tf_op jit(solution)/shard_map/ppermute | solution.py:407
  22.4 5.4 %collective-permute-start.6 = (bf16[128,512]{1,0:T(8,128)(2,1)S(1)}, bf16[128,512]{1,0:T(8,128)(2,1)S(1)}, u32[]{:S(2)}, u32[]{:S(2)}) collective-permute-start(bf16[128,512]{1,0:T(8,128)(2,1)S(1)} %get-tuple-element.27), channel_id=1, source_target_pairs={{0,3},{1,0},{2,1},{3,2},{4,7},{5,4},{6,5},{7,6},{8,9},{9,10},{10,1... | collective-permute-start | bytes 393224 | tf_op jit(solution)/shard_map/ppermute | solution.py:407
  22.4 5.4 %copy-start = (bf16[8,512,128]{2,1,0:T(8,128)(2,1)S(1)}, bf16[8,512,128]{2,1,0:T(8,128)(2,1)}, u32[]{:S(2)}) copy-start(bf16[8,512,128]{2,1,0:T(8,128)(2,1)} %value_up_ref.1) | copy-start | bytes 3145732
  27.7 22.4 %copy-start.2 = (bf16[7168]{0:T(1024)(128)(2,1)S(1)}, bf16[7168]{0:T(1024)(128)(2,1)}, u32[]{:S(2)}) copy-start(bf16[7168]{0:T(1024)(128)(2,1)} %param.15) | copy-start | bytes 43012
  27.7 26.2 %copy-start.1 = (bf16[16,7168]{1,0:T(8,128)(2,1)S(1)}, bf16[16,7168]{1,0:T(8,128)(2,1)}, u32[]{:S(2)}) copy-start(bf16[16,7168]{1,0:T(8,128)(2,1)} %residual_ref.1) | copy-start | bytes 688132
  29.6 13.7 %collective-permute-start.11 = (bf16[4,16,3712]{2,1,0:T(8,128)(2,1)S(1)}, bf16[4,16,3712]{2,1,0:T(8,128)(2,1)S(1)}, u32[]{:S(2)}, u32[]{:S(2)}) collective-permute-start(bf16[4,16,3712]{2,1,0:T(8,128)(2,1)S(1)} %get-tuple-element.34), channel_id=1, source_target_pairs={{0,68},{1,69},{2,70},{3,71},{4,64},{5,65},{6,66},{7,67},{8,76},{9,... | collective-permute-start | bytes 1425416 | tf_op jit(solution)/shard_map/ppermute | solution.py:407
  32.5 13.7 %collective-permute-start.7 = (bf16[2,16,3456]{2,1,0:T(8,128)(2,1)S(1)}, bf16[2,16,3456]{2,1,0:T(8,128)(2,1)S(1)}, u32[]{:S(2)}, u32[]{:S(2)}) collective-permute-start(bf16[2,16,3456]{2,1,0:T(8,128)(2,1)S(1)} %get-tuple-element.30), channel_id=1, source_target_pairs={{0,1},{1,2},{2,3},{3,0},{4,5},{5,6},{6,7},{7,4},{8,11},{9,8},{10,9... | collective-permute-start | bytes 663560 | tf_op jit(solution)/shard_map/ppermute | solution.py:407
  33.2 14.6 %collective-permute-start.8 = (bf16[2,16,3456]{2,1,0:T(8,128)(2,1)S(1)}, bf16[2,16,3456]{2,1,0:T(8,128)(2,1)S(1)}, u32[]{:S(2)}, u32[]{:S(2)}) collective-permute-start(bf16[2,16,3456]{2,1,0:T(8,128)(2,1)S(1)} %get-tuple-element.31), channel_id=1, source_target_pairs={{0,2},{1,3},{2,0},{3,1},{4,6},{5,7},{6,4},{7,5},{8,10},{9,11},{10,... | collective-permute-start | bytes 663560 | tf_op jit(solution)/shard_map/ppermute | solution.py:407
  36.4 11.4 %collective-permute-start.9 = (bf16[2,16,3456]{2,1,0:T(8,128)(2,1)S(1)}, bf16[2,16,3456]{2,1,0:T(8,128)(2,1)S(1)}, u32[]{:S(2)}, u32[]{:S(2)}) collective-permute-start(bf16[2,16,3456]{2,1,0:T(8,128)(2,1)S(1)} %get-tuple-element.32), channel_id=1, source_target_pairs={{0,3},{1,0},{2,1},{3,2},{4,7},{5,4},{6,5},{7,6},{8,9},{9,10},{10,1... | collective-permute-start | bytes 663560 | tf_op jit(solution)/shard_map/ppermute | solution.py:407
  43.5 10.5 %collective-permute-start.12 = (bf16[16,3712]{1,0:T(8,128)(2,1)S(1)}, bf16[16,3712]{1,0:T(8,128)(2,1)S(1)}, u32[]{:S(2)}, u32[]{:S(2)}) collective-permute-start(bf16[16,3712]{1,0:T(8,128)(2,1)S(1)} %get-tuple-element.35), channel_id=1, source_target_pairs={{0,1},{1,2},{2,3},{3,0},{4,5},{5,6},{6,7},{7,4},{8,11},{9,8},{10,9... | collective-permute-start | bytes 356360 | tf_op jit(solution)/shard_map/ppermute | solution.py:407
  44.2 9.7 %collective-permute-start.13 = (bf16[16,3712]{1,0:T(8,128)(2,1)S(1)}, bf16[16,3712]{1,0:T(8,128)(2,1)S(1)}, u32[]{:S(2)}, u32[]{:S(2)}) collective-permute-start(bf16[16,3712]{1,0:T(8,128)(2,1)S(1)} %get-tuple-element.36), channel_id=1, source_target_pairs={{0,2},{1,3},{2,0},{3,1},{4,6},{5,7},{6,4},{7,5},{8,10},{9,11},{10,... | collective-permute-start | bytes 356360 | tf_op jit(solution)/shard_map/ppermute | solution.py:407
  46.2 7.7 %collective-permute-start.14 = (bf16[16,3712]{1,0:T(8,128)(2,1)S(1)}, bf16[16,3712]{1,0:T(8,128)(2,1)S(1)}, u32[]{:S(2)}, u32[]{:S(2)}) collective-permute-start(bf16[16,3712]{1,0:T(8,128)(2,1)S(1)} %get-tuple-element.37), channel_id=1, source_target_pairs={{0,3},{1,0},{2,1},{3,2},{4,7},{5,4},{6,5},{7,6},{8,9},{9,10},{10,1... | collective-permute-start | bytes 356360 | tf_op jit(solution)/shard_map/ppermute | solution.py:407
  47.9 6.0 %collective-permute-start.10 = (bf16[16,3456]{1,0:T(8,128)(2,1)S(1)}, bf16[16,3456]{1,0:T(8,128)(2,1)S(1)}, u32[]{:S(2)}, u32[]{:S(2)}) collective-permute-start(bf16[16,3456]{1,0:T(8,128)(2,1)S(1)} %add_near.1), channel_id=1, source_target_pairs={{0,68},{1,69},{2,70},{3,71},{4,64},{5,65},{6,66},{7,67},{8,76},{9,... | collective-permute-start | bytes 331784 | tf_op jit(solution)/shard_map/ppermute | solution.py:407

commit v5 on v4

--- a/solution.py
+++ b/solution.py
@@ -9,6 +9,7 @@
 GROUP_ROWS = 4
 PROJ_STEP = 1024
 LEFT_COLUMNS = 3456
+Z_ORDER = (1, 3, 2)
 ORDERS = ((6, 5, 7, 4, 2, 1, 3), (6, 5, 7, 4, 2, 1, 3))
 exponent_scale = 192.0 ** (-0.5) * 1.4426950408889634
 norm_eps = 1e-06
@@ -422,9 +423,9 @@
     values, own, across = make_values(owned_latents, value_up, proj_near, owners, rows_here)
     came = send(across, (z_size, z_size), mesh_shape)
     parts = project(values, proj_near, owners, rows_here)
-    nears = [parts[0]] + [send(parts[k], (k, k), mesh_shape) for k in range(1, z_size)]
+    nears = [parts[0]] + [send(parts[k], (k, k), mesh_shape) for k in Z_ORDER]
     pairs = add_far(own, came)
-    steps = [send(pair, (k, k), mesh_shape) for k, pair in enumerate(pairs, 1)]
+    steps = [send(pairs[k - 1], (k, k), mesh_shape) for k in Z_ORDER]
     far = send(add_near(nears), (z_size, z_size), mesh_shape)
     return finish(nears, far, own, came, steps, residual, norm_gain)
 

time: 55.9 us -> 55 us (0.984)
  transfers between devices with their start and end apart: 15 -> 15, of which waited for: 3 -> 5; matrix products, arithmetic and copies ran while one was open for 0% -> 0% of each run, Pallas kernels for 12% -> 12%
where the time goes in v5:
time: 55 us; the launch traced here: 54.2 us
  starting transfers between devices  26.3 us (48%)
  Pallas kernels  14.5 us (26%)
  waiting for transfers between devices  12.6 us (23%)
  between operations  0.74 us (1%)
    ppermute x15, starting transfers between devices, send(): return lax.ppermute(array, ('rep', 'dp'), pairs)  26.3 us
    ppermute x15, waiting for transfers between devices, send(): return lax.ppermute(array, ('rep', 'dp'), pairs)  12.6 us
    pallas_call x1, Pallas kernels, bring(): pl.pallas_call(bring_kernel, out_shape=pltpu.VMEM(output_proj.shape, jnp....  5.27 us
    pallas_call x1, Pallas kernels, attend(): pl.pallas_call(attend_kernel, out_shape=[jax.ShapeDtypeStruct((row_count...  5.1 us
    pallas_call x1, Pallas kernels, make_values(): pl.pallas_call(values_kernel, out_shape=(jax.ShapeDtypeStruct((rows, owne...  1.81 us
    pallas_call x1, Pallas kernels, project(): pl.pallas_call(project_kernel, out_shape=[part] * z_size, in_specs=[vmem,...  1.13 us
  transfers between devices with their start and end apart: 15, of which 5 were waited for; matrix products, arithmetic and copies ran while one was open for 0% of the time, Pallas kernels for 12%

profile of v5, /device:TPU:0, one launch (start us, length us, event | category | flops | bytes accessed | tf_op | source)
XLA Modules:
  0.0 54.2 jit_solution(9196768056728589791)
XLA Ops:
  0.6 5.1 %attend.1 = (bf16[128,512]{1,0:T(8,128)(2,1)S(1)}, bf16[128,512]{1,0:T(8,128)(2,1)S(1)}, bf16[128,512]{1,0:T(8,128)(2,1)S(1)}, bf16[128,512]{1,0:T(8,128)(2,1)S(...) custom-call(s32[128]{0:T(128)} %lengths_hbm.1, ...), custom_call_target="tpu_custom_call" | custom-call | flops 1207959552 | bytes 9437184 | tf_op jit(solution)/shard_map/attend/pallas_call | solution.py:180
  5.7 6.5 %collective-permute-start = (bf16[128,512]{1,0:T(8,128)(2,1)S(1)}, bf16[128,512]{1,0:T(8,128)(2,1)S(1)}, u32[]{:S(2)}, u32[]{:S(2)}) collective-permute-start(bf16[128,512]{1,0:T(8,128)(2,1)S(1)} %get-tuple-element.21), channel_id=1, source_target_pairs={{0,70},{1,71},{2,68},{3,69},{4,66},{5,67},{6,64},{7,65},{8,78},{9,... | collective-permute-start | bytes 393224 | tf_op jit(solution)/shard_map/ppermute | solution.py:408
  12.2 0.7 %collective-permute-start.1 = (bf16[128,512]{1,0:T(8,128)(2,1)S(1)}, bf16[128,512]{1,0:T(8,128)(2,1)S(1)}, u32[]{:S(2)}, u32[]{:S(2)}) collective-permute-start(bf16[128,512]{1,0:T(8,128)(2,1)S(1)} %get-tuple-element.22), channel_id=1, source_target_pairs={{0,69},{1,70},{2,71},{3,68},{4,65},{5,66},{6,67},{7,64},{8,79},{9,... | collective-permute-start | bytes 393224 | tf_op jit(solution)/shard_map/ppermute | solution.py:408
  12.9 4.7 %collective-permute-start.2 = (bf16[128,512]{1,0:T(8,128)(2,1)S(1)}, bf16[128,512]{1,0:T(8,128)(2,1)S(1)}, u32[]{:S(2)}, u32[]{:S(2)}) collective-permute-start(bf16[128,512]{1,0:T(8,128)(2,1)S(1)} %get-tuple-element.23), channel_id=1, source_target_pairs={{0,71},{1,68},{2,69},{3,70},{4,67},{5,64},{6,65},{7,66},{8,77},{9,... | collective-permute-start | bytes 393224 | tf_op jit(solution)/shard_map/ppermute | solution.py:408
  17.6 0.2 collective-permute-start.3
  17.8 0.2 collective-permute-start.4
  18.0 0.0 collective-permute-done.latent_refs_1_
  18.0 1.0 %collective-permute-start.5 = (bf16[128,512]{1,0:T(8,128)(2,1)S(1)}, bf16[128,512]{1,0:T(8,128)(2,1)S(1)}, u32[]{:S(2)}, u32[]{:S(2)}) collective-permute-start(bf16[128,512]{1,0:T(8,128)(2,1)S(1)} %get-tuple-element.26), channel_id=1, source_target_pairs={{0,1},{1,2},{2,3},{3,0},{4,5},{5,6},{6,7},{7,4},{8,11},{9,8},{10,9... | collective-permute-start | bytes 393224 | tf_op jit(solution)/shard_map/ppermute | solution.py:408
  19.0 2.1 %collective-permute-done.1.latent_refs_2_ = bf16[128,512]{1,0:T(8,128)(2,1)S(1)} collective-permute-done((bf16[128,512]{1,0:T(8,128)(2,1)S(1)}, bf16[128,512]{1,0:T(8,128)(2,1)S(1)}, u32[]{:S(2)}, u32[]{:S(2)}) %collective-permute-start.1) | collective-permute-done | bytes 131104 | tf_op jit(solution)/shard_map/ppermute | solution.py:408
  21.1 0.4 collective-permute-start.6
  21.5 0.0 copy-start
  21.5 5.3 %bring.1.proj_ref = bf16[1024,7168]{1,0:T(8,128)(2,1)S(1)} custom-call(bf16[128,512]{1,0:T(8,128)(2,1)S(1)} %get-tuple-element.20.after_hbm.latent_refs_0_, bf16[1024,7168]{1,0:T(8,128)(2,1)} %proj_hbm.1), custom_call_target="tpu_custom_call" | custom-call | bytes 14680064 | tf_op jit(solution)/shard_map/bring/pallas_call | solution.py:215
  26.7 0.0 copy-start.2
  26.7 0.0 copy-start.1
  26.8 0.0 collective-permute-done.2.latent_refs_3_
  26.8 0.0 collective-permute-done.3.latent_refs_4_
  26.8 0.0 collective-permute-done.4.latent_refs_5_
  26.8 0.3 collective-permute-done.5.latent_refs_6_
  27.0 0.0 collective-permute-done.6.latent_refs_7_
  27.0 0.0 copy-done
  27.0 1.8 %values.1 = (bf16[128,1024]{1,0:T(8,128)(2,1)S(1)}, bf16[4,16,3712]{2,1,0:T(8,128)(2,1)S(1)}, bf16[4,16,3712]{2,1,0:T(8,128)(2,1)S(1)}) custom-call(bf16[128,512]{1,0:T(8,128)(2,1)S(1)} %get-tuple-element.20.after_hbm.latent_refs_0_, bf16[128,512]{1,0:T(8,128)(2,1)S(1)} %collective-permute-done.latent_refs_1_, ...), custom_call_target="tpu_custom_call" | custom-call | flops 973078528 | bytes 7602176 | tf_op jit(solution)/shard_map/values/pallas_call | solution.py:272
  28.9 2.5 %collective-permute-start.11 = (bf16[4,16,3712]{2,1,0:T(8,128)(2,1)S(1)}, bf16[4,16,3712]{2,1,0:T(8,128)(2,1)S(1)}, u32[]{:S(2)}, u32[]{:S(2)}) collective-permute-start(bf16[4,16,3712]{2,1,0:T(8,128)(2,1)S(1)} %get-tuple-element.34), channel_id=1, source_target_pairs={{0,68},{1,69},{2,70},{3,71},{4,64},{5,65},{6,66},{7,67},{8,76},{9,... | collective-permute-start | bytes 1425416 | tf_op jit(solution)/shard_map/ppermute | solution.py:408
  31.4 1.1 %project.1 = (bf16[2,16,3456]{2,1,0:T(8,128)(2,1)S(1)}, bf16[2,16,3456]{2,1,0:T(8,128)(2,1)S(1)}, bf16[2,16,3456]{2,1,0:T(8,128)(2,1)S(1)}, bf16[2,16,3456]{2,1,0:T(8,128)(2,1)S(1)}) custom-call(bf16[128,1024]{1,0:T(8,128)(2,1)S(1)} %get-tuple-element.28.values_ref, bf16[1024,7168]{1,0:T(8,128)(2,1)S(1)} %bring.1.proj_ref), custom_call_target="tpu_custom_call" | custom-call | flops 905969664 | bytes 7077888 | tf_op jit(solution)/shard_map/project/pallas_call | solution.py:306
  32.5 0.4 collective-permute-start.7
  32.9 2.9 %collective-permute-start.8 = (bf16[2,16,3456]{2,1,0:T(8,128)(2,1)S(1)}, bf16[2,16,3456]{2,1,0:T(8,128)(2,1)S(1)}, u32[]{:S(2)}, u32[]{:S(2)}) collective-permute-start(bf16[2,16,3456]{2,1,0:T(8,128)(2,1)S(1)} %get-tuple-element.31), channel_id=1, source_target_pairs={{0,3},{1,0},{2,1},{3,2},{4,7},{5,4},{6,5},{7,6},{8,9},{9,10},{10,1... | collective-permute-start | bytes 663560 | tf_op jit(solution)/shard_map/ppermute | solution.py:408
  35.8 1.1 %collective-permute-start.9 = (bf16[2,16,3456]{2,1,0:T(8,128)(2,1)S(1)}, bf16[2,16,3456]{2,1,0:T(8,128)(2,1)S(1)}, u32[]{:S(2)}, u32[]{:S(2)}) collective-permute-start(bf16[2,16,3456]{2,1,0:T(8,128)(2,1)S(1)} %get-tuple-element.32), channel_id=1, source_target_pairs={{0,2},{1,3},{2,0},{3,1},{4,6},{5,7},{6,4},{7,5},{8,10},{9,11},{10,... | collective-permute-start | bytes 663560 | tf_op jit(solution)/shard_map/ppermute | solution.py:408
  36.9 6.1 %collective-permute-done.11.came_ref = bf16[4,16,3712]{2,1,0:T(8,128)(2,1)S(1)} collective-permute-done((bf16[4,16,3712]{2,1,0:T(8,128)(2,1)S(1)}, bf16[4,16,3712]{2,1,0:T(8,128)(2,1)S(1)}, u32[]{:S(2)}, u32[]{:S(2)}) %collective-permute-start.11) | collective-permute-done | bytes 475168 | tf_op jit(solution)/shard_map/ppermute | solution.py:408
  43.0 0.1 add_far.1
  43.1 0.2 collective-permute-start.12
  43.4 3.1 %collective-permute-start.13 = (bf16[16,3712]{1,0:T(8,128)(2,1)S(1)}, bf16[16,3712]{1,0:T(8,128)(2,1)S(1)}, u32[]{:S(2)}, u32[]{:S(2)}) collective-permute-start(bf16[16,3712]{1,0:T(8,128)(2,1)S(1)} %get-tuple-element.36), channel_id=1, source_target_pairs={{0,3},{1,0},{2,1},{3,2},{4,7},{5,4},{6,5},{7,6},{8,9},{9,10},{10,1... | collective-permute-start | bytes 356360 | tf_op jit(solution)/shard_map/ppermute | solution.py:408
  46.4 0.1 collective-permute-done.7.refs_1_.near_refs_1_
  46.6 0.4 collective-permute-start.14
  47.0 0.0 collective-permute-done.8.refs_2_.near_refs_2_
  47.0 0.0 collective-permute-done.9.refs_3_.near_refs_3_
  47.0 0.1 add_near.1
  47.1 2.0 %collective-permute-start.10 = (bf16[16,3456]{1,0:T(8,128)(2,1)S(1)}, bf16[16,3456]{1,0:T(8,128)(2,1)S(1)}, u32[]{:S(2)}, u32[]{:S(2)}) collective-permute-start(bf16[16,3456]{1,0:T(8,128)(2,1)S(1)} %add_near.1), channel_id=1, source_target_pairs={{0,68},{1,69},{2,70},{3,71},{4,64},{5,65},{6,66},{7,67},{8,76},{9,... | collective-permute-start | bytes 331784 | tf_op jit(solution)/shard_map/ppermute | solution.py:408
  49.1 0.0 copy-done.2
  49.1 4.0 %collective-permute-done.10.far_ref = bf16[16,3456]{1,0:T(8,128)(2,1)S(1)} collective-permute-done((bf16[16,3456]{1,0:T(8,128)(2,1)S(1)}, bf16[16,3456]{1,0:T(8,128)(2,1)S(1)}, u32[]{:S(2)}, u32[]{:S(2)}) %collective-permute-start.10) | collective-permute-done | bytes 110624 | tf_op jit(solution)/shard_map/ppermute | solution.py:408
  53.1 0.0 collective-permute-done.12.step_refs_0_
  53.1 0.0 collective-permute-done.13.step_refs_1_
  53.1 0.0 collective-permute-done.14.step_refs_2_
  53.1 0.0 copy-done.1
  53.1 1.0 %finish.1 = (bf16[16,7168]{1,0:T(8,128)(2,1)}, bf16[16,7168]{1,0:T(8,128)(2,1)}) custom-call(bf16[2,16,3456]{2,1,0:T(8,128)(2,1)S(1)} %get-tuple-element.29.refs_0_.near_refs_0_, bf16[2,16,3456]{2,1,0:T(8,128)(2,1)S(1)} %collective-permute-done.7.refs_1_.near_refs_1_, bf16[2,16,3456]{2,1,0:T(8,128)(2,1)S(1)} %collective-permute-done.8.refs_2_.near_refs_2_, ...), custom_call_target="tpu_custom_call" | custom-call | tf_op jit(solution)/shard_map/finish/pallas_call | solution.py:386
  (1 shorter events, 0.0 us)
Async XLA Ops:
  5.7 12.3 %collective-permute-start = (bf16[128,512]{1,0:T(8,128)(2,1)S(1)}, bf16[128,512]{1,0:T(8,128)(2,1)S(1)}, u32[]{:S(2)}, u32[]{:S(2)}) collective-permute-start(bf16[128,512]{1,0:T(8,128)(2,1)S(1)} %get-tuple-element.21), channel_id=1, source_target_pairs={{0,70},{1,71},{2,68},{3,69},{4,66},{5,67},{6,64},{7,65},{8,78},{9,... | collective-permute-start | bytes 393224 | tf_op jit(solution)/shard_map/ppermute | solution.py:408
  12.2 8.9 %collective-permute-start.1 = (bf16[128,512]{1,0:T(8,128)(2,1)S(1)}, bf16[128,512]{1,0:T(8,128)(2,1)S(1)}, u32[]{:S(2)}, u32[]{:S(2)}) collective-permute-start(bf16[128,512]{1,0:T(8,128)(2,1)S(1)} %get-tuple-element.22), channel_id=1, source_target_pairs={{0,69},{1,70},{2,71},{3,68},{4,65},{5,66},{6,67},{7,64},{8,79},{9,... | collective-permute-start | bytes 393224 | tf_op jit(solution)/shard_map/ppermute | solution.py:408
  12.9 13.9 %collective-permute-start.2 = (bf16[128,512]{1,0:T(8,128)(2,1)S(1)}, bf16[128,512]{1,0:T(8,128)(2,1)S(1)}, u32[]{:S(2)}, u32[]{:S(2)}) collective-permute-start(bf16[128,512]{1,0:T(8,128)(2,1)S(1)} %get-tuple-element.23), channel_id=1, source_target_pairs={{0,71},{1,68},{2,69},{3,70},{4,67},{5,64},{6,65},{7,66},{8,77},{9,... | collective-permute-start | bytes 393224 | tf_op jit(solution)/shard_map/ppermute | solution.py:408
  17.6 9.2 %collective-permute-start.3 = (bf16[128,512]{1,0:T(8,128)(2,1)S(1)}, bf16[128,512]{1,0:T(8,128)(2,1)S(1)}, u32[]{:S(2)}, u32[]{:S(2)}) collective-permute-start(bf16[128,512]{1,0:T(8,128)(2,1)S(1)} %get-tuple-element.24), channel_id=1, source_target_pairs={{0,68},{1,69},{2,70},{3,71},{4,64},{5,65},{6,66},{7,67},{8,76},{9,... | collective-permute-start | bytes 393224 | tf_op jit(solution)/shard_map/ppermute | solution.py:408
  17.8 9.0 %collective-permute-start.4 = (bf16[128,512]{1,0:T(8,128)(2,1)S(1)}, bf16[128,512]{1,0:T(8,128)(2,1)S(1)}, u32[]{:S(2)}, u32[]{:S(2)}) collective-permute-start(bf16[128,512]{1,0:T(8,128)(2,1)S(1)} %get-tuple-element.25), channel_id=1, source_target_pairs={{0,2},{1,3},{2,0},{3,1},{4,6},{5,7},{6,4},{7,5},{8,10},{9,11},{10,... | collective-permute-start | bytes 393224 | tf_op jit(solution)/shard_map/ppermute | solution.py:408
  18.0 9.0 %collective-permute-start.5 = (bf16[128,512]{1,0:T(8,128)(2,1)S(1)}, bf16[128,512]{1,0:T(8,128)(2,1)S(1)}, u32[]{:S(2)}, u32[]{:S(2)}) collective-permute-start(bf16[128,512]{1,0:T(8,128)(2,1)S(1)} %get-tuple-element.26), channel_id=1, source_target_pairs={{0,1},{1,2},{2,3},{3,0},{4,5},{5,6},{6,7},{7,4},{8,11},{9,8},{10,9... | collective-permute-start | bytes 393224 | tf_op jit(solution)/shard_map/ppermute | solution.py:408
  21.1 6.0 %collective-permute-start.6 = (bf16[128,512]{1,0:T(8,128)(2,1)S(1)}, bf16[128,512]{1,0:T(8,128)(2,1)S(1)}, u32[]{:S(2)}, u32[]{:S(2)}) collective-permute-start(bf16[128,512]{1,0:T(8,128)(2,1)S(1)} %get-tuple-element.27), channel_id=1, source_target_pairs={{0,3},{1,0},{2,1},{3,2},{4,7},{5,4},{6,5},{7,6},{8,9},{9,10},{10,1... | collective-permute-start | bytes 393224 | tf_op jit(solution)/shard_map/ppermute | solution.py:408
  21.5 5.6 %copy-start = (bf16[8,512,128]{2,1,0:T(8,128)(2,1)S(1)}, bf16[8,512,128]{2,1,0:T(8,128)(2,1)}, u32[]{:S(2)}) copy-start(bf16[8,512,128]{2,1,0:T(8,128)(2,1)} %value_up_ref.1) | copy-start | bytes 3145732
  26.7 22.4 %copy-start.2 = (bf16[7168]{0:T(1024)(128)(2,1)S(1)}, bf16[7168]{0:T(1024)(128)(2,1)}, u32[]{:S(2)}) copy-start(bf16[7168]{0:T(1024)(128)(2,1)} %param.15) | copy-start | bytes 43012
  26.7 26.4 %copy-start.1 = (bf16[16,7168]{1,0:T(8,128)(2,1)S(1)}, bf16[16,7168]{1,0:T(8,128)(2,1)}, u32[]{:S(2)}) copy-start(bf16[16,7168]{1,0:T(8,128)(2,1)} %residual_ref.1) | copy-start | bytes 688132
  28.9 14.2 %collective-permute-start.11 = (bf16[4,16,3712]{2,1,0:T(8,128)(2,1)S(1)}, bf16[4,16,3712]{2,1,0:T(8,128)(2,1)S(1)}, u32[]{:S(2)}, u32[]{:S(2)}) collective-permute-start(bf16[4,16,3712]{2,1,0:T(8,128)(2,1)S(1)} %get-tuple-element.34), channel_id=1, source_target_pairs={{0,68},{1,69},{2,70},{3,71},{4,64},{5,65},{6,66},{7,67},{8,76},{9,... | collective-permute-start | bytes 1425416 | tf_op jit(solution)/shard_map/ppermute | solution.py:408
  32.5 14.0 %collective-permute-start.7 = (bf16[2,16,3456]{2,1,0:T(8,128)(2,1)S(1)}, bf16[2,16,3456]{2,1,0:T(8,128)(2,1)S(1)}, u32[]{:S(2)}, u32[]{:S(2)}) collective-permute-start(bf16[2,16,3456]{2,1,0:T(8,128)(2,1)S(1)} %get-tuple-element.30), channel_id=1, source_target_pairs={{0,1},{1,2},{2,3},{3,0},{4,5},{5,6},{6,7},{7,4},{8,11},{9,8},{10,9... | collective-permute-start | bytes 663560 | tf_op jit(solution)/shard_map/ppermute | solution.py:408
  32.9 14.1 %collective-permute-start.8 = (bf16[2,16,3456]{2,1,0:T(8,128)(2,1)S(1)}, bf16[2,16,3456]{2,1,0:T(8,128)(2,1)S(1)}, u32[]{:S(2)}, u32[]{:S(2)}) collective-permute-start(bf16[2,16,3456]{2,1,0:T(8,128)(2,1)S(1)} %get-tuple-element.31), channel_id=1, source_target_pairs={{0,3},{1,0},{2,1},{3,2},{4,7},{5,4},{6,5},{7,6},{8,9},{9,10},{10,1... | collective-permute-start | bytes 663560 | tf_op jit(solution)/shard_map/ppermute | solution.py:408
  35.8 11.2 %collective-permute-start.9 = (bf16[2,16,3456]{2,1,0:T(8,128)(2,1)S(1)}, bf16[2,16,3456]{2,1,0:T(8,128)(2,1)S(1)}, u32[]{:S(2)}, u32[]{:S(2)}) collective-permute-start(bf16[2,16,3456]{2,1,0:T(8,128)(2,1)S(1)} %get-tuple-element.32), channel_id=1, source_target_pairs={{0,2},{1,3},{2,0},{3,1},{4,6},{5,7},{6,4},{7,5},{8,10},{9,11},{10,... | collective-permute-start | bytes 663560 | tf_op jit(solution)/shard_map/ppermute | solution.py:408
  43.1 10.0 %collective-permute-start.12 = (bf16[16,3712]{1,0:T(8,128)(2,1)S(1)}, bf16[16,3712]{1,0:T(8,128)(2,1)S(1)}, u32[]{:S(2)}, u32[]{:S(2)}) collective-permute-start(bf16[16,3712]{1,0:T(8,128)(2,1)S(1)} %get-tuple-element.35), channel_id=1, source_target_pairs={{0,1},{1,2},{2,3},{3,0},{4,5},{5,6},{6,7},{7,4},{8,11},{9,8},{10,9... | collective-permute-start | bytes 356360 | tf_op jit(solution)/shard_map/ppermute | solution.py:408
  43.4 9.8 %collective-permute-start.13 = (bf16[16,3712]{1,0:T(8,128)(2,1)S(1)}, bf16[16,3712]{1,0:T(8,128)(2,1)S(1)}, u32[]{:S(2)}, u32[]{:S(2)}) collective-permute-start(bf16[16,3712]{1,0:T(8,128)(2,1)S(1)} %get-tuple-element.36), channel_id=1, source_target_pairs={{0,3},{1,0},{2,1},{3,2},{4,7},{5,4},{6,5},{7,6},{8,9},{9,10},{10,1... | collective-permute-start | bytes 356360 | tf_op jit(solution)/shard_map/ppermute | solution.py:408
  46.6 6.6 %collective-permute-start.14 = (bf16[16,3712]{1,0:T(8,128)(2,1)S(1)}, bf16[16,3712]{1,0:T(8,128)(2,1)S(1)}, u32[]{:S(2)}, u32[]{:S(2)}) collective-permute-start(bf16[16,3712]{1,0:T(8,128)(2,1)S(1)} %get-tuple-element.37), channel_id=1, source_target_pairs={{0,2},{1,3},{2,0},{3,1},{4,6},{5,7},{6,4},{7,5},{8,10},{9,11},{10,... | collective-permute-start | bytes 356360 | tf_op jit(solution)/shard_map/ppermute | solution.py:408
  47.1 6.0 %collective-permute-start.10 = (bf16[16,3456]{1,0:T(8,128)(2,1)S(1)}, bf16[16,3456]{1,0:T(8,128)(2,1)S(1)}, u32[]{:S(2)}, u32[]{:S(2)}) collective-permute-start(bf16[16,3456]{1,0:T(8,128)(2,1)S(1)} %add_near.1), channel_id=1, source_target_pairs={{0,68},{1,69},{2,70},{3,71},{4,64},{5,65},{6,66},{7,67},{8,76},{9,... | collective-permute-start | bytes 331784 | tf_op jit(solution)/shard_map/ppermute | solution.py:408

commit v6 on v4

--- a/solution.py
+++ b/solution.py
@@ -85,6 +85,7 @@
                 fetch_keys(pair, span).start()
 
     start(1)
+    start(2)
     latent_copy.wait()
     latent_wide[...] = latent_ref[...].astype(jnp.float32)
 
@@ -145,7 +146,7 @@
 
         @pl.when(group == 0)
         def _():
-            for later in range(2, group_count):
+            for later in range(3, group_count):
                 start(later)
 
         @pl.when(is_long)

time: 55.9 us -> 55.8 us (level); the launches traced: 55 us -> 55.8 us
  starting transfers between devices: 26.5 us -> 28.5 us
  waiting for transfers between devices: 13.1 us -> 12.2 us
    ppermute x15, starting transfers between devices: 26.5 us -> 28.5 us  [send(): return lax.ppermute(array, ('rep', 'dp'), pairs)]
    ppermute x15, waiting for transfers between devices: 13.1 us -> 12.2 us  [send(): return lax.ppermute(array, ('rep', 'dp'), pairs)]
  transfers between devices with their start and end apart: 15 -> 15, of which waited for: 3 -> 4; matrix products, arithmetic and copies ran while one was open for 0% -> 0% of each run, Pallas kernels for 12% -> 12%
where the time goes in v6:
time: 55.8 us
  starting transfers between devices  28.5 us (51%)
  Pallas kernels  14.4 us (26%)
  waiting for transfers between devices  12.2 us (22%)
  between operations  0.74 us (1%)
    ppermute x15, starting transfers between devices, send(): return lax.ppermute(array, ('rep', 'dp'), pairs)  28.5 us
    ppermute x15, waiting for transfers between devices, send(): return lax.ppermute(array, ('rep', 'dp'), pairs)  12.2 us
    pallas_call x1, Pallas kernels, bring(): pl.pallas_call(bring_kernel, out_shape=pltpu.VMEM(output_proj.shape, jnp....  5.27 us
    pallas_call x1, Pallas kernels, attend(): pl.pallas_call(attend_kernel, out_shape=[jax.ShapeDtypeStruct((row_count...  4.99 us
    pallas_call x1, Pallas kernels, make_values(): pl.pallas_call(values_kernel, out_shape=(jax.ShapeDtypeStruct((rows, owne...  1.81 us
    pallas_call x1, Pallas kernels, project(): pl.pallas_call(project_kernel, out_shape=[part] * z_size, in_specs=[vmem,...  1.13 us
  transfers between devices with their start and end apart: 15, of which 4 were waited for; matrix products, arithmetic and copies ran while one was open for 0% of the time, Pallas kernels for 12%

profile of v6, /device:TPU:0, one launch (start us, length us, event | category | flops | bytes accessed | tf_op | source)
XLA Modules:
  0.0 55.8 jit_solution(7179114584130270160)
XLA Ops:
  0.6 5.0 %attend.1 = (bf16[128,512]{1,0:T(8,128)(2,1)S(1)}, bf16[128,512]{1,0:T(8,128)(2,1)S(1)}, bf16[128,512]{1,0:T(8,128)(2,1)S(1)}, bf16[128,512]{1,0:T(8,128)(2,1)S(...) custom-call(s32[128]{0:T(128)} %lengths_hbm.1, ...), custom_call_target="tpu_custom_call" | custom-call | flops 1207959552 | bytes 9437184 | tf_op jit(solution)/shard_map/attend/pallas_call | solution.py:180
  5.6 6.5 %collective-permute-start = (bf16[128,512]{1,0:T(8,128)(2,1)S(1)}, bf16[128,512]{1,0:T(8,128)(2,1)S(1)}, u32[]{:S(2)}, u32[]{:S(2)}) collective-permute-start(bf16[128,512]{1,0:T(8,128)(2,1)S(1)} %get-tuple-element.21), channel_id=1, source_target_pairs={{0,70},{1,71},{2,68},{3,69},{4,66},{5,67},{6,64},{7,65},{8,78},{9,... | collective-permute-start | bytes 393224 | tf_op jit(solution)/shard_map/ppermute | solution.py:408
  12.1 0.7 %collective-permute-start.1 = (bf16[128,512]{1,0:T(8,128)(2,1)S(1)}, bf16[128,512]{1,0:T(8,128)(2,1)S(1)}, u32[]{:S(2)}, u32[]{:S(2)}) collective-permute-start(bf16[128,512]{1,0:T(8,128)(2,1)S(1)} %get-tuple-element.22), channel_id=1, source_target_pairs={{0,69},{1,70},{2,71},{3,68},{4,65},{5,66},{6,67},{7,64},{8,79},{9,... | collective-permute-start | bytes 393224 | tf_op jit(solution)/shard_map/ppermute | solution.py:408
  12.8 4.7 %collective-permute-start.2 = (bf16[128,512]{1,0:T(8,128)(2,1)S(1)}, bf16[128,512]{1,0:T(8,128)(2,1)S(1)}, u32[]{:S(2)}, u32[]{:S(2)}) collective-permute-start(bf16[128,512]{1,0:T(8,128)(2,1)S(1)} %get-tuple-element.23), channel_id=1, source_target_pairs={{0,71},{1,68},{2,69},{3,70},{4,67},{5,64},{6,65},{7,66},{8,77},{9,... | collective-permute-start | bytes 393224 | tf_op jit(solution)/shard_map/ppermute | solution.py:408
  17.5 0.2 collective-permute-start.3
  17.7 0.2 collective-permute-start.4
  17.9 0.0 collective-permute-done.latent_refs_1_
  17.9 1.0 %collective-permute-start.5 = (bf16[128,512]{1,0:T(8,128)(2,1)S(1)}, bf16[128,512]{1,0:T(8,128)(2,1)S(1)}, u32[]{:S(2)}, u32[]{:S(2)}) collective-permute-start(bf16[128,512]{1,0:T(8,128)(2,1)S(1)} %get-tuple-element.26), channel_id=1, source_target_pairs={{0,1},{1,2},{2,3},{3,0},{4,5},{5,6},{6,7},{7,4},{8,11},{9,8},{10,9... | collective-permute-start | bytes 393224 | tf_op jit(solution)/shard_map/ppermute | solution.py:408
  18.9 2.6 %collective-permute-done.1.latent_refs_2_ = bf16[128,512]{1,0:T(8,128)(2,1)S(1)} collective-permute-done((bf16[128,512]{1,0:T(8,128)(2,1)S(1)}, bf16[128,512]{1,0:T(8,128)(2,1)S(1)}, u32[]{:S(2)}, u32[]{:S(2)}) %collective-permute-start.1) | collective-permute-done | bytes 131104 | tf_op jit(solution)/shard_map/ppermute | solution.py:408
  21.5 0.0 collective-permute-start.6
  21.5 0.0 copy-start
  21.5 5.3 %bring.1.proj_ref = bf16[1024,7168]{1,0:T(8,128)(2,1)S(1)} custom-call(bf16[128,512]{1,0:T(8,128)(2,1)S(1)} %get-tuple-element.20.after_hbm.latent_refs_0_, bf16[1024,7168]{1,0:T(8,128)(2,1)} %proj_hbm.1), custom_call_target="tpu_custom_call" | custom-call | bytes 14680064 | tf_op jit(solution)/shard_map/bring/pallas_call | solution.py:215
  26.7 0.0 copy-start.2
  26.8 0.0 copy-start.1
  26.8 0.0 collective-permute-done.2.latent_refs_3_
  26.8 0.0 collective-permute-done.3.latent_refs_4_
  26.8 0.0 collective-permute-done.4.latent_refs_5_
  26.8 0.2 collective-permute-done.5.latent_refs_6_
  27.0 0.0 collective-permute-done.6.latent_refs_7_
  27.0 0.0 copy-done
  27.0 1.8 %values.1 = (bf16[128,1024]{1,0:T(8,128)(2,1)S(1)}, bf16[4,16,3712]{2,1,0:T(8,128)(2,1)S(1)}, bf16[4,16,3712]{2,1,0:T(8,128)(2,1)S(1)}) custom-call(bf16[128,512]{1,0:T(8,128)(2,1)S(1)} %get-tuple-element.20.after_hbm.latent_refs_0_, bf16[128,512]{1,0:T(8,128)(2,1)S(1)} %collective-permute-done.latent_refs_1_, ...), custom_call_target="tpu_custom_call" | custom-call | flops 973078528 | bytes 7602176 | tf_op jit(solution)/shard_map/values/pallas_call | solution.py:272
  28.8 2.7 %collective-permute-start.11 = (bf16[4,16,3712]{2,1,0:T(8,128)(2,1)S(1)}, bf16[4,16,3712]{2,1,0:T(8,128)(2,1)S(1)}, u32[]{:S(2)}, u32[]{:S(2)}) collective-permute-start(bf16[4,16,3712]{2,1,0:T(8,128)(2,1)S(1)} %get-tuple-element.34), channel_id=1, source_target_pairs={{0,68},{1,69},{2,70},{3,71},{4,64},{5,65},{6,66},{7,67},{8,76},{9,... | collective-permute-start | bytes 1425416 | tf_op jit(solution)/shard_map/ppermute | solution.py:408
  31.5 1.1 %project.1 = (bf16[2,16,3456]{2,1,0:T(8,128)(2,1)S(1)}, bf16[2,16,3456]{2,1,0:T(8,128)(2,1)S(1)}, bf16[2,16,3456]{2,1,0:T(8,128)(2,1)S(1)}, bf16[2,16,3456]{2,1,0:T(8,128)(2,1)S(1)}) custom-call(bf16[128,1024]{1,0:T(8,128)(2,1)S(1)} %get-tuple-element.28.values_ref, bf16[1024,7168]{1,0:T(8,128)(2,1)S(1)} %bring.1.proj_ref), custom_call_target="tpu_custom_call" | custom-call | flops 905969664 | bytes 7077888 | tf_op jit(solution)/shard_map/project/pallas_call | solution.py:306
  32.6 0.8 %collective-permute-start.7 = (bf16[2,16,3456]{2,1,0:T(8,128)(2,1)S(1)}, bf16[2,16,3456]{2,1,0:T(8,128)(2,1)S(1)}, u32[]{:S(2)}, u32[]{:S(2)}) collective-permute-start(bf16[2,16,3456]{2,1,0:T(8,128)(2,1)S(1)} %get-tuple-element.30), channel_id=1, source_target_pairs={{0,1},{1,2},{2,3},{3,0},{4,5},{5,6},{6,7},{7,4},{8,11},{9,8},{10,9... | collective-permute-start | bytes 663560 | tf_op jit(solution)/shard_map/ppermute | solution.py:408
  33.4 3.2 %collective-permute-start.8 = (bf16[2,16,3456]{2,1,0:T(8,128)(2,1)S(1)}, bf16[2,16,3456]{2,1,0:T(8,128)(2,1)S(1)}, u32[]{:S(2)}, u32[]{:S(2)}) collective-permute-start(bf16[2,16,3456]{2,1,0:T(8,128)(2,1)S(1)} %get-tuple-element.31), channel_id=1, source_target_pairs={{0,2},{1,3},{2,0},{3,1},{4,6},{5,7},{6,4},{7,5},{8,10},{9,11},{10,... | collective-permute-start | bytes 663560 | tf_op jit(solution)/shard_map/ppermute | solution.py:408
  36.7 0.7 %collective-permute-start.9 = (bf16[2,16,3456]{2,1,0:T(8,128)(2,1)S(1)}, bf16[2,16,3456]{2,1,0:T(8,128)(2,1)S(1)}, u32[]{:S(2)}, u32[]{:S(2)}) collective-permute-start(bf16[2,16,3456]{2,1,0:T(8,128)(2,1)S(1)} %get-tuple-element.32), channel_id=1, source_target_pairs={{0,3},{1,0},{2,1},{3,2},{4,7},{5,4},{6,5},{7,6},{8,9},{9,10},{10,1... | collective-permute-start | bytes 663560 | tf_op jit(solution)/shard_map/ppermute | solution.py:408
  37.4 5.9 %collective-permute-done.11.came_ref = bf16[4,16,3712]{2,1,0:T(8,128)(2,1)S(1)} collective-permute-done((bf16[4,16,3712]{2,1,0:T(8,128)(2,1)S(1)}, bf16[4,16,3712]{2,1,0:T(8,128)(2,1)S(1)}, u32[]{:S(2)}, u32[]{:S(2)}) %collective-permute-start.11) | collective-permute-done | bytes 475168 | tf_op jit(solution)/shard_map/ppermute | solution.py:408
  43.3 0.1 add_far.1
  43.3 0.7 %collective-permute-start.12 = (bf16[16,3712]{1,0:T(8,128)(2,1)S(1)}, bf16[16,3712]{1,0:T(8,128)(2,1)S(1)}, u32[]{:S(2)}, u32[]{:S(2)}) collective-permute-start(bf16[16,3712]{1,0:T(8,128)(2,1)S(1)} %get-tuple-element.35), channel_id=1, source_target_pairs={{0,1},{1,2},{2,3},{3,0},{4,5},{5,6},{6,7},{7,4},{8,11},{9,8},{10,9... | collective-permute-start | bytes 356360 | tf_op jit(solution)/shard_map/ppermute | solution.py:408
  44.1 3.0 %collective-permute-start.13 = (bf16[16,3712]{1,0:T(8,128)(2,1)S(1)}, bf16[16,3712]{1,0:T(8,128)(2,1)S(1)}, u32[]{:S(2)}, u32[]{:S(2)}) collective-permute-start(bf16[16,3712]{1,0:T(8,128)(2,1)S(1)} %get-tuple-element.36), channel_id=1, source_target_pairs={{0,2},{1,3},{2,0},{3,1},{4,6},{5,7},{6,4},{7,5},{8,10},{9,11},{10,... | collective-permute-start | bytes 356360 | tf_op jit(solution)/shard_map/ppermute | solution.py:408
  47.1 0.0 collective-permute-done.7.refs_1_.near_refs_1_
  47.1 1.6 %collective-permute-start.14 = (bf16[16,3712]{1,0:T(8,128)(2,1)S(1)}, bf16[16,3712]{1,0:T(8,128)(2,1)S(1)}, u32[]{:S(2)}, u32[]{:S(2)}) collective-permute-start(bf16[16,3712]{1,0:T(8,128)(2,1)S(1)} %get-tuple-element.37), channel_id=1, source_target_pairs={{0,3},{1,0},{2,1},{3,2},{4,7},{5,4},{6,5},{7,6},{8,9},{9,10},{10,1... | collective-permute-start | bytes 356360 | tf_op jit(solution)/shard_map/ppermute | solution.py:408
  48.6 0.0 collective-permute-done.8.refs_2_.near_refs_2_
  48.6 0.0 collective-permute-done.9.refs_3_.near_refs_3_
  48.6 0.1 add_near.1
  48.7 2.5 %collective-permute-start.10 = (bf16[16,3456]{1,0:T(8,128)(2,1)S(1)}, bf16[16,3456]{1,0:T(8,128)(2,1)S(1)}, u32[]{:S(2)}, u32[]{:S(2)}) collective-permute-start(bf16[16,3456]{1,0:T(8,128)(2,1)S(1)} %add_near.1), channel_id=1, source_target_pairs={{0,68},{1,69},{2,70},{3,71},{4,64},{5,65},{6,66},{7,67},{8,76},{9,... | collective-permute-start | bytes 331784 | tf_op jit(solution)/shard_map/ppermute | solution.py:408
  51.2 0.0 copy-done.2
  51.2 3.5 %collective-permute-done.10.far_ref = bf16[16,3456]{1,0:T(8,128)(2,1)S(1)} collective-permute-done((bf16[16,3456]{1,0:T(8,128)(2,1)S(1)}, bf16[16,3456]{1,0:T(8,128)(2,1)S(1)}, u32[]{:S(2)}, u32[]{:S(2)}) %collective-permute-start.10) | collective-permute-done | bytes 110624 | tf_op jit(solution)/shard_map/ppermute | solution.py:408
  54.7 0.0 collective-permute-done.12.step_refs_0_
  54.7 0.0 collective-permute-done.13.step_refs_1_
  54.7 0.0 collective-permute-done.14.step_refs_2_
  54.8 0.0 copy-done.1
  54.8 1.0 %finish.1 = (bf16[16,7168]{1,0:T(8,128)(2,1)}, bf16[16,7168]{1,0:T(8,128)(2,1)}) custom-call(bf16[2,16,3456]{2,1,0:T(8,128)(2,1)S(1)} %get-tuple-element.29.refs_0_.near_refs_0_, bf16[2,16,3456]{2,1,0:T(8,128)(2,1)S(1)} %collective-permute-done.7.refs_1_.near_refs_1_, bf16[2,16,3456]{2,1,0:T(8,128)(2,1)S(1)} %collective-permute-done.8.refs_2_.near_refs_2_, ...), custom_call_target="tpu_custom_call" | custom-call | tf_op jit(solution)/shard_map/finish/pallas_call | solution.py:386
  (1 shorter events, 0.0 us)
Async XLA Ops:
  5.6 12.3 %collective-permute-start = (bf16[128,512]{1,0:T(8,128)(2,1)S(1)}, bf16[128,512]{1,0:T(8,128)(2,1)S(1)}, u32[]{:S(2)}, u32[]{:S(2)}) collective-permute-start(bf16[128,512]{1,0:T(8,128)(2,1)S(1)} %get-tuple-element.21), channel_id=1, source_target_pairs={{0,70},{1,71},{2,68},{3,69},{4,66},{5,67},{6,64},{7,65},{8,78},{9,... | collective-permute-start | bytes 393224 | tf_op jit(solution)/shard_map/ppermute | solution.py:408
  12.1 9.3 %collective-permute-start.1 = (bf16[128,512]{1,0:T(8,128)(2,1)S(1)}, bf16[128,512]{1,0:T(8,128)(2,1)S(1)}, u32[]{:S(2)}, u32[]{:S(2)}) collective-permute-start(bf16[128,512]{1,0:T(8,128)(2,1)S(1)} %get-tuple-element.22), channel_id=1, source_target_pairs={{0,69},{1,70},{2,71},{3,68},{4,65},{5,66},{6,67},{7,64},{8,79},{9,... | collective-permute-start | bytes 393224 | tf_op jit(solution)/shard_map/ppermute | solution.py:408
  12.8 14.0 %collective-permute-start.2 = (bf16[128,512]{1,0:T(8,128)(2,1)S(1)}, bf16[128,512]{1,0:T(8,128)(2,1)S(1)}, u32[]{:S(2)}, u32[]{:S(2)}) collective-permute-start(bf16[128,512]{1,0:T(8,128)(2,1)S(1)} %get-tuple-element.23), channel_id=1, source_target_pairs={{0,71},{1,68},{2,69},{3,70},{4,67},{5,64},{6,65},{7,66},{8,77},{9,... | collective-permute-start | bytes 393224 | tf_op jit(solution)/shard_map/ppermute | solution.py:408
  17.5 9.3 %collective-permute-start.3 = (bf16[128,512]{1,0:T(8,128)(2,1)S(1)}, bf16[128,512]{1,0:T(8,128)(2,1)S(1)}, u32[]{:S(2)}, u32[]{:S(2)}) collective-permute-start(bf16[128,512]{1,0:T(8,128)(2,1)S(1)} %get-tuple-element.24), channel_id=1, source_target_pairs={{0,68},{1,69},{2,70},{3,71},{4,64},{5,65},{6,66},{7,67},{8,76},{9,... | collective-permute-start | bytes 393224 | tf_op jit(solution)/shard_map/ppermute | solution.py:408
  17.7 9.1 %collective-permute-start.4 = (bf16[128,512]{1,0:T(8,128)(2,1)S(1)}, bf16[128,512]{1,0:T(8,128)(2,1)S(1)}, u32[]{:S(2)}, u32[]{:S(2)}) collective-permute-start(bf16[128,512]{1,0:T(8,128)(2,1)S(1)} %get-tuple-element.25), channel_id=1, source_target_pairs={{0,2},{1,3},{2,0},{3,1},{4,6},{5,7},{6,4},{7,5},{8,10},{9,11},{10,... | collective-permute-start | bytes 393224 | tf_op jit(solution)/shard_map/ppermute | solution.py:408
  17.9 9.1 %collective-permute-start.5 = (bf16[128,512]{1,0:T(8,128)(2,1)S(1)}, bf16[128,512]{1,0:T(8,128)(2,1)S(1)}, u32[]{:S(2)}, u32[]{:S(2)}) collective-permute-start(bf16[128,512]{1,0:T(8,128)(2,1)S(1)} %get-tuple-element.26), channel_id=1, source_target_pairs={{0,1},{1,2},{2,3},{3,0},{4,5},{5,6},{6,7},{7,4},{8,11},{9,8},{10,9... | collective-permute-start | bytes 393224 | tf_op jit(solution)/shard_map/ppermute | solution.py:408
  21.5 5.6 %collective-permute-start.6 = (bf16[128,512]{1,0:T(8,128)(2,1)S(1)}, bf16[128,512]{1,0:T(8,128)(2,1)S(1)}, u32[]{:S(2)}, u32[]{:S(2)}) collective-permute-start(bf16[128,512]{1,0:T(8,128)(2,1)S(1)} %get-tuple-element.27), channel_id=1, source_target_pairs={{0,3},{1,0},{2,1},{3,2},{4,7},{5,4},{6,5},{7,6},{8,9},{9,10},{10,1... | collective-permute-start | bytes 393224 | tf_op jit(solution)/shard_map/ppermute | solution.py:408
  21.5 5.6 %copy-start = (bf16[8,512,128]{2,1,0:T(8,128)(2,1)S(1)}, bf16[8,512,128]{2,1,0:T(8,128)(2,1)}, u32[]{:S(2)}) copy-start(bf16[8,512,128]{2,1,0:T(8,128)(2,1)} %value_up_ref.1) | copy-start | bytes 3145732
  26.7 24.5 %copy-start.2 = (bf16[7168]{0:T(1024)(128)(2,1)S(1)}, bf16[7168]{0:T(1024)(128)(2,1)}, u32[]{:S(2)}) copy-start(bf16[7168]{0:T(1024)(128)(2,1)} %param.15) | copy-start | bytes 43012
  26.8 28.0 %copy-start.1 = (bf16[16,7168]{1,0:T(8,128)(2,1)S(1)}, bf16[16,7168]{1,0:T(8,128)(2,1)}, u32[]{:S(2)}) copy-start(bf16[16,7168]{1,0:T(8,128)(2,1)} %residual_ref.1) | copy-start | bytes 688132
  28.8 14.4 %collective-permute-start.11 = (bf16[4,16,3712]{2,1,0:T(8,128)(2,1)S(1)}, bf16[4,16,3712]{2,1,0:T(8,128)(2,1)S(1)}, u32[]{:S(2)}, u32[]{:S(2)}) collective-permute-start(bf16[4,16,3712]{2,1,0:T(8,128)(2,1)S(1)} %get-tuple-element.34), channel_id=1, source_target_pairs={{0,68},{1,69},{2,70},{3,71},{4,64},{5,65},{6,66},{7,67},{8,76},{9,... | collective-permute-start | bytes 1425416 | tf_op jit(solution)/shard_map/ppermute | solution.py:408
  32.6 14.4 %collective-permute-start.7 = (bf16[2,16,3456]{2,1,0:T(8,128)(2,1)S(1)}, bf16[2,16,3456]{2,1,0:T(8,128)(2,1)S(1)}, u32[]{:S(2)}, u32[]{:S(2)}) collective-permute-start(bf16[2,16,3456]{2,1,0:T(8,128)(2,1)S(1)} %get-tuple-element.30), channel_id=1, source_target_pairs={{0,1},{1,2},{2,3},{3,0},{4,5},{5,6},{6,7},{7,4},{8,11},{9,8},{10,9... | collective-permute-start | bytes 663560 | tf_op jit(solution)/shard_map/ppermute | solution.py:408
  33.4 15.2 %collective-permute-start.8 = (bf16[2,16,3456]{2,1,0:T(8,128)(2,1)S(1)}, bf16[2,16,3456]{2,1,0:T(8,128)(2,1)S(1)}, u32[]{:S(2)}, u32[]{:S(2)}) collective-permute-start(bf16[2,16,3456]{2,1,0:T(8,128)(2,1)S(1)} %get-tuple-element.31), channel_id=1, source_target_pairs={{0,2},{1,3},{2,0},{3,1},{4,6},{5,7},{6,4},{7,5},{8,10},{9,11},{10,... | collective-permute-start | bytes 663560 | tf_op jit(solution)/shard_map/ppermute | solution.py:408
  36.7 12.0 %collective-permute-start.9 = (bf16[2,16,3456]{2,1,0:T(8,128)(2,1)S(1)}, bf16[2,16,3456]{2,1,0:T(8,128)(2,1)S(1)}, u32[]{:S(2)}, u32[]{:S(2)}) collective-permute-start(bf16[2,16,3456]{2,1,0:T(8,128)(2,1)S(1)} %get-tuple-element.32), channel_id=1, source_target_pairs={{0,3},{1,0},{2,1},{3,2},{4,7},{5,4},{6,5},{7,6},{8,9},{9,10},{10,1... | collective-permute-start | bytes 663560 | tf_op jit(solution)/shard_map/ppermute | solution.py:408
  43.3 11.4 %collective-permute-start.12 = (bf16[16,3712]{1,0:T(8,128)(2,1)S(1)}, bf16[16,3712]{1,0:T(8,128)(2,1)S(1)}, u32[]{:S(2)}, u32[]{:S(2)}) collective-permute-start(bf16[16,3712]{1,0:T(8,128)(2,1)S(1)} %get-tuple-element.35), channel_id=1, source_target_pairs={{0,1},{1,2},{2,3},{3,0},{4,5},{5,6},{6,7},{7,4},{8,11},{9,8},{10,9... | collective-permute-start | bytes 356360 | tf_op jit(solution)/shard_map/ppermute | solution.py:408
  44.1 10.7 %collective-permute-start.13 = (bf16[16,3712]{1,0:T(8,128)(2,1)S(1)}, bf16[16,3712]{1,0:T(8,128)(2,1)S(1)}, u32[]{:S(2)}, u32[]{:S(2)}) collective-permute-start(bf16[16,3712]{1,0:T(8,128)(2,1)S(1)} %get-tuple-element.36), channel_id=1, source_target_pairs={{0,2},{1,3},{2,0},{3,1},{4,6},{5,7},{6,4},{7,5},{8,10},{9,11},{10,... | collective-permute-start | bytes 356360 | tf_op jit(solution)/shard_map/ppermute | solution.py:408
  47.1 7.7 %collective-permute-start.14 = (bf16[16,3712]{1,0:T(8,128)(2,1)S(1)}, bf16[16,3712]{1,0:T(8,128)(2,1)S(1)}, u32[]{:S(2)}, u32[]{:S(2)}) collective-permute-start(bf16[16,3712]{1,0:T(8,128)(2,1)S(1)} %get-tuple-element.37), channel_id=1, source_target_pairs={{0,3},{1,0},{2,1},{3,2},{4,7},{5,4},{6,5},{7,6},{8,9},{9,10},{10,1... | collective-permute-start | bytes 356360 | tf_op jit(solution)/shard_map/ppermute | solution.py:408
  48.7 6.0 %collective-permute-start.10 = (bf16[16,3456]{1,0:T(8,128)(2,1)S(1)}, bf16[16,3456]{1,0:T(8,128)(2,1)S(1)}, u32[]{:S(2)}, u32[]{:S(2)}) collective-permute-start(bf16[16,3456]{1,0:T(8,128)(2,1)S(1)} %add_near.1), channel_id=1, source_target_pairs={{0,68},{1,69},{2,70},{3,71},{4,64},{5,65},{6,66},{7,67},{8,76},{9,... | collective-permute-start | bytes 331784 | tf_op jit(solution)/shard_map/ppermute | solution.py:408
